TPU v7x, 256 devices: a whole 4x4x8 slice. The times are simulated.
256 devices in a mesh: width: 8 (over x, core), latent: 32 (over z, y).
Axes of the slice: x: 4, y: 4, z: 8, core: 2. Of those that a mesh axis runs over, the one named last changes fastest.
Arguments:
- activations: bfloat16 [256, 4608], P(None, 'width'), may hold values from -6 to 6
- encoder: bfloat16 [4608, 65536], P('width', 'latent'), may hold values from -0.09375 to 0.09375
- latent_bias: float32 [65536], P('latent'), may hold values from -0.6 to 0.2
- decoder: bfloat16 [65536, 4608], P('latent', 'width')
- output_bias: float32 [4608], P('width'), may hold values from -3 to 3
Outputs:
- loss_value: float32 [], replicated
- encoder_grad: bfloat16 [4608, 65536], P('width', 'latent')
- latent_grad: float32 [65536], P('latent')
- decoder_grad: bfloat16 [65536, 4608], P('latent', 'width')
- output_grad: float32 [4608], P('width')
All inputs are finite; a program needn't handle non-finite values.
Results may differ from a plain program's by a relative error of at most 0.018.
Values may be sent and summed in bfloat16 or wider, within the bound.
No kernel may reach another device: no remote copies, remote signals or barrier semaphores. Data moves between devices by JAX's collectives and lax.ppermute only.
A program may use at most 64 MiB of HBM per device.

v0:
```python
import jax
import jax.numpy as jnp
from jax import lax
from jax.sharding import PartitionSpec as P

D = 2304
LAYERS = 2


SPARSITY = 0.5
EPSILON = 1e-06
FIRST_FIRST = (((0,), (0,)), ((), ()))
FIRST_SECOND = (((0,), (1,)), ((), ()))
SECOND_SECOND = (((1,), (1,)), ((), ()))


def shards(activations, encoder, latent_bias, decoder, output_bias):
    token_count, column_count = activations.shape
    width_count = lax.axis_size("width")
    latent_devices = lax.axis_size("latent")
    width_index = lax.axis_index("width")
    layer_index = width_index * column_count // D
    layer_mask = (jnp.arange(LAYERS) == layer_index).astype(jnp.float32)
    square_part = jnp.einsum("jc,jc->j", decoder, decoder, preferred_element_type=jnp.float32)
    square_rows = layer_mask[:, None] * square_part[None, :]
    square_sums = lax.psum(square_rows, "width")
    norms = jnp.sqrt(square_sums + EPSILON)
    weights = jnp.sum(norms, axis=0)
    partial_pre = lax.dot_general(
        encoder, activations, FIRST_SECOND, preferred_element_type=jnp.float32
    )
    preact = lax.psum(partial_pre, "width") + latent_bias[:, None]
    features = jnp.maximum(preact, 0.0).astype(jnp.bfloat16)
    act_float = activations.astype(jnp.float32)
    partial_rebuild = lax.dot_general(
        features, decoder, FIRST_FIRST, preferred_element_type=jnp.float32
    )
    errors = lax.psum(partial_rebuild, "latent") + output_bias - act_float
    squared = 0.5 * jnp.sum(errors * errors) / latent_devices
    error_half = errors.astype(jnp.bfloat16)
    output_grad = jnp.sum(error_half.astype(jnp.float32), axis=0)
    back_part = lax.dot_general(
        decoder, error_half, SECOND_SECOND, preferred_element_type=jnp.float32
    )
    back_sums = lax.psum(back_part, "width")
    grad_pre = jnp.where(features > 0, back_sums + SPARSITY * weights[:, None], 0.0).astype(
        jnp.bfloat16
    )
    encoder_grad = lax.dot_general(
        activations, grad_pre, FIRST_SECOND, preferred_element_type=jnp.float32
    ).astype(jnp.bfloat16)
    latent_grad = jnp.sum(grad_pre.astype(jnp.float32), axis=1)
    feature_totals = jnp.sum(features.astype(jnp.float32), axis=1)
    own_norms = jnp.sum(layer_mask[:, None] * norms, axis=0)
    direct = jnp.dot(features, error_half, preferred_element_type=jnp.float32)
    shrink = SPARSITY * feature_totals[:, None] * decoder.astype(jnp.float32) / own_norms[:, None]
    decoder_grad = (direct + shrink).astype(jnp.bfloat16)
    local_loss = squared + SPARSITY * jnp.sum(feature_totals * weights) / width_count
    loss_value = lax.psum(local_loss, ("width", "latent")) / (token_count * LAYERS * D)
    return (loss_value, encoder_grad, latent_grad, decoder_grad, output_grad)


def solution(mesh):
    placed = (P(None, "width"), P("width", "latent"), P("latent"), P("latent", "width"), P("width"))
    return jax.shard_map(
        shards,
        mesh=mesh,
        in_specs=placed,
        out_specs=(P(), P("width", "latent"), P("latent"), P("latent", "width"), P("width")),
        check_vma=False,
    )
```

profile of v0, /device:TPU:1, one launch (start us, length us, event | category | flops | bytes accessed | tf_op | source)
XLA Modules:
  0.0 339.2 jit_solution(15833977377919186432)
XLA Ops:
  7.2 0.0 copy-start
  7.2 0.0 copy-start.4
  7.2 0.0 all-reduce.4.cloned.1.call-start
  7.2 1.6 copy-done
  8.8 3.3 fusion.8
  12.1 0.0 all-reduce.4.cloned.1.call-update
  12.2 0.0 all-reduce.6.cloned.1.call-start
  12.2 72.8 %all-reduce.4.cloned.1.call-done = f32[2048,256]{1,0:T(8,128)} async-done(((f32[2048,256]{1,0:T(8,128)}), f32[2048,256]{1,0:T(8,128)}) %all-reduce.4.cloned.1.call-update) | async-done | bytes 2097168 | tf_op jit(solution)/shard_map/psum | solution.py:32
  85.0 0.0 copy-done.4
  85.0 0.0 copy-start.1
  85.0 2.4 convert_reduce_fusion.1
  87.4 0.0 copy-done.1
  87.4 1.6 fusion.9
  89.0 0.0 copy-start.5
  89.0 0.0 all-reduce.6.cloned.1.call-update
  89.0 0.0 all-reduce.8.cloned.1.call-start
  89.1 2.2 fusion
  91.3 0.1 broadcast_multiply_fusion
  91.3 23.9 %psum.37 = f32[2,2048]{1,0:T(2,128)S(1)} all-reduce(f32[2,2048]{1,0:T(2,128)S(1)} %broadcast_multiply_fusion), channel_id=1, replica_groups=mesh['width'=8,'latent'=32] {'width'}, use_global_device_ids=true, to_apply=%region_4.5 | all-reduce | flops 4096 | bytes 32768 | tf_op jit(solution)/shard_map/psum | solution.py:26
  115.2 118.4 %all-reduce.6.cloned.1.call-done = f32[256,576]{0,1:T(8,128)} async-done(((f32[256,576]{0,1:T(8,128)}), f32[256,576]{0,1:T(8,128)}) %all-reduce.6.cloned.1.call-update) | async-done | bytes 589840 | tf_op jit(solution)/shard_map/psum | solution.py:38
  233.6 0.0 copy-done.5
  233.6 2.0 convert_reduce_fusion.2
  235.7 0.0 copy-start.3
  235.7 0.7 copy-done.3
  236.4 4.2 %convolution_bitcast_fusion = f32[2048,256]{1,0:T(8,128)} fusion(bf16[256,576]{0,1:T(8,128)(2,1)S(1)} %get-tuple-element.8, bf16[2048,576]{0,1:T(8,128)(2,1)} %param.8), kind=kOutput, calls=%fused_computation.8 | convolution fusion | flops 603979776 | bytes 4751360 | tf_op jit(solution)/shard_map/dot_general | solution.py:42
  240.6 0.0 all-reduce.8.cloned.1.call-update
  240.6 0.1 multiply_reduce_fusion.1
  240.7 0.6 broadcast_multiply_fusion.1
  242.6 79.1 %psum.38 = f32[]{:T(128)} all-reduce(f32[]{:T(128)S(6)} %add.53), channel_id=1, replica_groups=mesh['width'=8,'latent'=32] {'width','latent'}, use_global_device_ids=true, to_apply=%region_7.8 | all-reduce | flops 1 | bytes 8 | tf_op jit(solution)/shard_map/psum | solution.py:59
  322.3 4.0 %fusion.3 = bf16[2048,576]{0,1:T(8,128)(2,1)} fusion(bf16[2048,576]{0,1:T(8,128)(2,1)} %param.8, bf16[2048,256]{1,0:T(8,128)(2,1)S(1)} %get-tuple-element.12, bf16[256,576]{0,1:T(8,128)(2,1)} %copy-done.3, f32[2048]{0:T(1024)S(1)} %get-tuple-element.5, f32[2048]{0:T(1024)S(1)} %get-tuple-element.14), kind=kOutput, calls=%fused_computation.5 | convolution fusion | flops 609878016 | bytes 6078464 | tf_op jit(solution)/shard_map/dot_general | solution.py:55
  326.4 0.0 all-reduce.8.cloned.1.call-done
  326.4 0.0 copy-start.2
  326.4 2.9 convert_reduce_fusion
  329.3 0.0 copy-done.2
  329.3 2.2 fusion.4
  (1 shorter events, 0.0 us)
Async XLA Ops:
  7.2 1.7 copy-start
  7.2 77.8 %copy-start.4 = (f32[2048]{0:T(1024)S(1)}, f32[2048]{0:T(1024)}, u32[]{:S(2)}) copy-start(f32[2048]{0:T(1024)} %param.7) | copy-start | bytes 24580
  7.2 77.8 %all-reduce.4.cloned.1.call-start = ((), (), s32[]{:S(2)}) async-start(), calls=%async_computation | async-start | bytes 4194304 | tf_op jit(solution)/shard_map/psum | solution.py:32
  12.2 221.4 %all-reduce.6.cloned.1.call-start = ((), (), s32[]{:S(2)}) async-start(), calls=%async_computation.1 | async-start | bytes 1179648 | tf_op jit(solution)/shard_map/psum | solution.py:38
  85.0 2.4 copy-start.1
  89.0 144.6 %copy-start.5 = (f32[576]{0:T(1024)S(1)}, f32[576]{0:T(1024)}, u32[]{:S(2)}) copy-start(f32[576]{0:T(1024)} %param.9) | copy-start | bytes 6916
  89.0 237.4 %all-reduce.8.cloned.1.call-start = ((), (), s32[]{:S(2)}) async-start(), calls=%async_computation.2 | async-start | bytes 4194304 | tf_op jit(solution)/shard_map/psum | solution.py:45
  235.7 0.7 copy-start.3
  326.4 2.9 copy-start.2
Sparse Core Ops, SparseCore 0:
  12.3 72.6 all-reduce.3
  89.1 144.4 all-reduce.5
  240.7 71.0 all-reduce.7
where the time goes:
time: 340 us; the launch traced here: 339 us
  waiting for transfers between devices  191 us (56%)
  blocking collectives  103 us (30%)
  between operations  16.9 us (5%)
  matrix products  15.4 us (5%)
  other arithmetic  10.3 us (3%)
    psum x1, waiting for transfers between devices, shards(): errors = lax.psum(partial_rebuild, 'latent') + output_bias - act_float  118 us
    psum x1, blocking collectives, shards(): lax.psum(local_loss, ('width', 'latent')) / (token_count * LAYERS * D)  79.1 us
    psum x1, waiting for transfers between devices, shards(): preact = lax.psum(partial_pre, 'width') + latent_bias[:, None]  72.8 us
    psum x1, blocking collectives, shards(): square_sums = lax.psum(square_rows, 'width')  23.9 us
  transfers between devices with their start and end apart: 3, of which 2 were waited for; matrix products, arithmetic and copies ran while one was open for 2% of the time, Pallas kernels for 0%

commit v1 on v0

v1 whole, which is shorter than its diff:
```python
import jax
import jax.numpy as jnp
from jax import lax
from jax.experimental import pallas as pl
from jax.experimental.pallas import tpu as pltpu
from jax.sharding import PartitionSpec as P

D = 2304
LAYERS = 2
SPARSITY = 0.5
EPSILON = 1e-06
F32 = jnp.float32
BF16 = jnp.bfloat16
TOK = 256
COL = 576
CHUNK = 256
WIDE = 640
LAT = 2048
VMEM_BYTES = 20 * 1024 * 1024

CORE_SWAP = [(i, i ^ 1) for i in range(8)]
X_PAIR_NEAR = [(i, ((i // 2) ^ 1) * 2 + i % 2) for i in range(8)]
X_PAIR_FAR = [(i, (3 - i // 2) * 2 + i % 2) for i in range(8)]


def x_shift(d):
    return [(i, (i + 2 * d) % 8) for i in range(8)]


def on_width(value, pairs):
    return lax.ppermute(value, "width", pairs)


def dot(a, b, dims):
    return lax.dot_general(a, b, (dims, ((), ())), preferred_element_type=F32)


def params():
    return pltpu.CompilerParams(vmem_limit_bytes=VMEM_BYTES)


def whole(shape):
    return pl.BlockSpec(shape, lambda *_: (0,) * len(shape))


def four_chunks(left, matrix, order, contract, kind, name):
    rows = matrix.shape[0]

    def body(order_ref, left_ref, matrix_ref, *outs):
        step = pl.program_id(0)
        if contract == 0:
            value = dot(left_ref[...], matrix_ref[...], ((0,), (0,)))
        else:
            value = dot(left_ref[:, :COL], matrix_ref[...], ((1,), (0,)))
        for k in range(4):
            @pl.when(step == k)
            def _():
                outs[k][...] = value.astype(kind)

    return pl.pallas_call(
        body,
        grid_spec=pltpu.PrefetchScalarGridSpec(
            num_scalar_prefetch=1,
            grid=(4,),
            in_specs=[whole(left.shape), pl.BlockSpec((rows, CHUNK), lambda i, order: (0, order[i]))],
            out_specs=[whole((TOK, CHUNK))] * 4,
        ),
        out_shape=[jax.ShapeDtypeStruct((TOK, CHUNK), kind)] * 4,
        compiler_params=params(),
        name=name,
        cost_estimate=pl.CostEstimate(
            flops=2 * TOK * COL * CHUNK * 4, bytes_accessed=COL * CHUNK * 8 + TOK * CHUNK * 16, transcendentals=0
        ),
    )(order, left, matrix)


def rebuild(chunks, order, dec_t, own_weights):
    def body(order_ref, *refs):
        feats, (dec_ref, weight_ref, out_ref, acc, extra) = refs[:8], refs[8:]
        step = pl.program_id(0)
        for k in range(8):
            @pl.when(step == k)
            def _():
                value = dot(feats[k][...], dec_ref[...], ((1,), (1,)))
                if k == 0:
                    acc[...] = value
                    extra[...] = jnp.sum(feats[0][...].astype(F32) * weight_ref[...], axis=1, keepdims=True)
                else:
                    acc[...] += value

        @pl.when(step == 7)
        def _():
            out_ref[:, :COL] = acc[...].astype(BF16)
            out_ref[:, COL:] = jnp.broadcast_to(extra[...], (TOK, WIDE - COL)).astype(BF16)

    return pl.pallas_call(
        body,
        grid_spec=pltpu.PrefetchScalarGridSpec(
            num_scalar_prefetch=1,
            grid=(8,),
            in_specs=[whole((TOK, CHUNK))] * 8
            + [pl.BlockSpec((COL, CHUNK), lambda i, order: (0, order[i])), whole((1, CHUNK))],
            out_specs=whole((TOK, WIDE)),
            scratch_shapes=[pltpu.VMEM((TOK, COL), F32), pltpu.VMEM((TOK, 1), F32)],
        ),
        out_shape=jax.ShapeDtypeStruct((TOK, WIDE), BF16),
        compiler_params=params(),
        name="rebuild",
        cost_estimate=pl.CostEstimate(
            flops=2 * TOK * COL * LAT, bytes_accessed=COL * LAT * 2 + TOK * LAT * 2, transcendentals=0
        ),
    )(order, *chunks, dec_t, own_weights)


def error_rows(parts, offset):
    def body(parts_ref, offset_ref, out_ref):
        total = jnp.sum(parts_ref[...].astype(F32), axis=0)
        errors = total[:, :COL] + offset_ref[...]
        loss = 0.5 * jnp.sum(errors * errors, axis=1, keepdims=True) + SPARSITY * total[:, COL:COL + 1]
        high = loss.astype(BF16).astype(F32)
        low = loss - high
        lane = lax.broadcasted_iota(jnp.int32, (8, WIDE - COL), 1)
        tail = jnp.where(lane == 0, high, jnp.where(lane == 1, low, 0.0))
        out_ref[:, :, :COL] = jnp.broadcast_to(errors.astype(BF16)[None], (32, 8, COL))
        out_ref[:, :, COL:] = jnp.broadcast_to(tail.astype(BF16)[None], (32, 8, WIDE - COL))

    return pl.pallas_call(
        body,
        out_shape=jax.ShapeDtypeStruct((32, 8, WIDE), BF16),
        compiler_params=params(),
        name="error_rows",
    )(parts, offset)


def decoder_gradient(errors, chunks, order, dec_t, norms):
    def body(order_ref, errors_ref, *refs):
        feats, (dec_ref, norm_ref, out_ref, sum_ref) = refs[:8], refs[8:]
        step = pl.program_id(0)
        for k in range(8):
            @pl.when(step == k)
            def _():
                feat = feats[k][...]
                direct = dot(errors_ref[:, :COL], feat, ((0,), (0,)))
                totals = jnp.sum(feat.astype(F32), axis=0, keepdims=True)
                scale = SPARSITY * totals / norm_ref[...]
                out_ref[...] = (direct + scale * dec_ref[...].astype(F32)).astype(BF16)
                if k == 0:
                    sum_ref[...] = jnp.sum(errors_ref[...].astype(F32), axis=0, keepdims=True)

    block = pl.BlockSpec((COL, CHUNK), lambda i, order: (0, order[i]))
    return pl.pallas_call(
        body,
        grid_spec=pltpu.PrefetchScalarGridSpec(
            num_scalar_prefetch=1,
            grid=(8,),
            in_specs=[whole((TOK, WIDE))] + [whole((TOK, CHUNK))] * 8
            + [block, pl.BlockSpec((1, CHUNK), lambda i, order: (0, order[i]))],
            out_specs=[block, whole((1, WIDE))],
        ),
        out_shape=[jax.ShapeDtypeStruct((COL, LAT), BF16), jax.ShapeDtypeStruct((1, WIDE), F32)],
        compiler_params=params(),
        name="decoder_gradient",
        cost_estimate=pl.CostEstimate(
            flops=2 * TOK * COL * LAT, bytes_accessed=COL * LAT * 4 + TOK * LAT * 2, transcendentals=0
        ),
    )(order, errors, *chunks, dec_t, norms)


def encoder_gradient(act_t, chunks, order):
    def body(order_ref, act_ref, *refs):
        grads, (out_ref, sum_ref) = refs[:8], refs[8:]
        step = pl.program_id(0)
        for k in range(8):
            @pl.when(step == k)
            def _():
                grad = grads[k][...]
                out_ref[...] = dot(act_ref[...], grad, ((1,), (0,))).astype(BF16)
                sum_ref[...] = jnp.sum(grad.astype(F32), axis=0, keepdims=True)

    return pl.pallas_call(
        body,
        grid_spec=pltpu.PrefetchScalarGridSpec(
            num_scalar_prefetch=1,
            grid=(8,),
            in_specs=[whole((COL, TOK))] + [whole((TOK, CHUNK))] * 8,
            out_specs=[
                pl.BlockSpec((COL, CHUNK), lambda i, order: (0, order[i])),
                pl.BlockSpec((1, CHUNK), lambda i, order: (0, order[i])),
            ],
        ),
        out_shape=[jax.ShapeDtypeStruct((COL, LAT), BF16), jax.ShapeDtypeStruct((1, LAT), F32)],
        compiler_params=params(),
        name="encoder_gradient",
        cost_estimate=pl.CostEstimate(
            flops=2 * TOK * COL * LAT, bytes_accessed=COL * LAT * 2 + TOK * LAT * 2, transcendentals=0
        ),
    )(order, act_t, *chunks)


def gather_chunks(own):
    same = [own] + [on_width(own, x_shift(d)) for d in (1, 2, 3)]
    return same + [on_width(chunk, CORE_SWAP) for chunk in same]


def scatter_sums(send, keep, kind):
    pair = [mine + on_width(other, CORE_SWAP).astype(F32) for mine, other in zip(keep, send)]
    total = pair[0]
    for d in (2, 1, 3):
        total = total + on_width(pair[d].astype(kind), x_shift(d)).astype(F32)
    return total


def shards(activations, encoder, latent_bias, decoder, output_bias):
    act_t, dec_t = activations.T, decoder.T
    width_index = lax.axis_index("width")
    latent_index = lax.axis_index("latent")
    x, core = width_index // 2, width_index % 2
    hops = jnp.arange(4, dtype=jnp.int32)
    ahead, behind = (x + hops) % 4 * 2, (x - hops) % 4 * 2
    send_order = (ahead + 1 - core).astype(jnp.int32)
    keep_order = (ahead + core).astype(jnp.int32)
    gathered_order = jnp.concatenate([behind + core, behind + 1 - core]).astype(jnp.int32)
    own = width_index * CHUNK

    send = four_chunks(act_t, encoder, send_order, 0, F32, "preact_send")
    keep = four_chunks(act_t, encoder, keep_order, 0, F32, "preact_keep")
    preact = scatter_sums(send, keep, F32) + lax.dynamic_slice(latent_bias, (own,), (CHUNK,))[None, :]
    features = jnp.maximum(preact, 0.0).astype(BF16)

    squares = jnp.sum(jnp.square(dec_t.astype(F32)), axis=0).reshape(16, 128)
    squares = squares + on_width(squares, CORE_SWAP)
    squares = squares + on_width(squares, X_PAIR_NEAR)
    norms = jnp.sqrt(squares + EPSILON)
    weights = (norms + on_width(norms, X_PAIR_FAR)).reshape(1, LAT)
    own_weights = lax.dynamic_slice(weights, (0, own), (1, CHUNK))

    feature_chunks = gather_chunks(features)
    parts = rebuild(feature_chunks, gathered_order, dec_t, own_weights).reshape(32, 8, WIDE)
    parts = lax.all_to_all(parts, "latent", 0, 0)
    offset = output_bias[None, :] - lax.dynamic_slice(activations, (latent_index * 8, 0), (8, COL)).astype(F32)
    errors = lax.all_to_all(error_rows(parts, offset), "latent", 0, 0).reshape(TOK, WIDE)

    loss = jnp.sum(errors[:, COL:].astype(F32))
    loss = jnp.full((8, 128), loss)
    for pairs in (CORE_SWAP, X_PAIR_NEAR, X_PAIR_FAR):
        loss = loss + on_width(loss, pairs)
    loss_value = loss[0, 0] / (TOK * LAYERS * D)

    send = four_chunks(errors, dec_t, send_order, 1, BF16, "back_send")
    keep = four_chunks(errors, dec_t, keep_order, 1, F32, "back_keep")
    back = scatter_sums(send, keep, BF16)
    grad_pre = jnp.where(features > 0, back + SPARSITY * own_weights, 0.0).astype(BF16)
    decoder_grad, output_grad = decoder_gradient(
        errors, feature_chunks, gathered_order, dec_t, norms.reshape(1, LAT)
    )
    encoder_grad, latent_grad = encoder_gradient(act_t, gather_chunks(grad_pre), gathered_order)
    return (loss_value, encoder_grad, latent_grad[0], decoder_grad.T, output_grad[0, :COL])


def solution(mesh):
    placed = (P(None, "width"), P("width", "latent"), P("latent"), P("latent", "width"), P("width"))
    return jax.shard_map(
        shards,
        mesh=mesh,
        in_specs=placed,
        out_specs=(P(), P("width", "latent"), P("latent"), P("latent", "width"), P("width")),
        check_vma=False,
    )
```

time: 340 us -> 130 us (0.38)
  waiting for transfers between devices: 191 us -> 25.9 us
  blocking collectives: 103 us -> 15.8 us
  starting transfers between devices: 0.12 us -> 46.8 us
  Pallas kernels: 0 us -> 22.9 us
  matrix products: 15.4 us -> 0 us
  between operations: 16.9 us -> 2.71 us
  local copies, waits for them, and re-layouts: 2.37 us -> 8.38 us
    psum x3 -> x0, waiting for transfers between devices: 191 us -> none  [the longest x1 118 us: shards(): errors = lax.psum(partial_rebuild, 'latent') + output_bias - act_float]
    psum x2 -> x0, blocking collectives: 103 us -> none  [the longest x1 79.1 us: shards(): lax.psum(local_loss, ('width', 'latent')) / (token_count * LAYERS * D)]
    ppermute x0 -> x34, starting transfers between devices: none -> 35.5 us  [on_width(): return lax.ppermute(value, 'width', pairs)]
    pallas_call x0 -> x8, Pallas kernels: none -> 22.9 us  [the longest x4 8.17 us: four_chunks(): pl.pallas_call(body, grid_spec=pltpu.PrefetchScalarGridSpec(num_scalar_pr...]
    ppermute x0 -> x34, waiting for transfers between devices: none -> 16.3 us  [on_width(): return lax.ppermute(value, 'width', pairs)]
    all_to_all x0 -> x1, blocking collectives: none -> 15.8 us  [shards(): lax.all_to_all(error_rows(parts, offset), 'latent', 0, 0).reshape(TOK, WIDE)]
    dot_general x5 -> x0, matrix products: 15.4 us -> none  [the longest x1 4.19 us: shards(): lax.dot_general(decoder, error_half, SECOND_SECOND, preferred_element_typ...]
    all_to_all x0 -> x1, starting transfers between devices: none -> 11.2 us  [shards(): parts = lax.all_to_all(parts, 'latent', 0, 0)]
  transfers between devices with their start and end apart: 3 -> 35, of which waited for: 2 -> 7; matrix products, arithmetic and copies ran while one was open for 2% -> 9% of each run, Pallas kernels for 0% -> 7%
where the time goes in v1:
time: 130 us; the launch traced here: 129 us
  starting transfers between devices  46.8 us (36%)
  waiting for transfers between devices  25.9 us (20%)
  Pallas kernels  22.9 us (18%)
  blocking collectives  15.8 us (12%)
  local copies, waits for them, and re-layouts  8.38 us (6%)
  other arithmetic  7 us (5%)
  between operations  2.71 us (2%)
    ppermute x34, starting transfers between devices, on_width(): return lax.ppermute(value, 'width', pairs)  35.5 us
    ppermute x34, waiting for transfers between devices, on_width(): return lax.ppermute(value, 'width', pairs)  16.3 us
    all_to_all x1, blocking collectives, shards(): lax.all_to_all(error_rows(parts, offset), 'latent', 0, 0).reshape(TOK, WIDE)  15.8 us
    all_to_all x1, starting transfers between devices, shards(): parts = lax.all_to_all(parts, 'latent', 0, 0)  11.2 us
    all_to_all x1, waiting for transfers between devices, shards(): parts = lax.all_to_all(parts, 'latent', 0, 0)  9.66 us
    pallas_call x4, Pallas kernels, four_chunks(): pl.pallas_call(body, grid_spec=pltpu.PrefetchScalarGridSpec(num_scalar_pr...  8.17 us
    pallas_call x1, Pallas kernels, decoder_gradient(): pl.pallas_call(body, grid_spec=pltpu.PrefetchScalarGridSpec(num_scalar_pr...  5.24 us
    unnamed x29, local copies, waits for them, and re-layouts  5.08 us
  transfers between devices with their start and end apart: 35, of which 7 were waited for; matrix products, arithmetic and copies ran while one was open for 9% of the time, Pallas kernels for 7%

profile of v1, /device:TPU:1, one launch (start us, length us, event | category | flops | bytes accessed | tf_op | source)
XLA Modules:
  0.0 129.5 jit_solution(7897015464992925591)
XLA Ops:
  0.7 1.8 %copy-done.1 = bf16[576,2048]{1,0:T(8,128)(2,1)S(1)} copy-done((bf16[576,2048]{1,0:T(8,128)(2,1)S(1)}, bf16[576,2048]{1,0:T(8,128)(2,1)}, u32[]{:S(2)}) %copy-start.1) | copy-done | bytes 2359320
  2.5 1.0 copy-done.3
  3.5 2.1 %preact_send.1 = (f32[256,256]{1,0:T(8,128)S(1)}, f32[256,256]{1,0:T(8,128)S(1)}, f32[256,256]{1,0:T(8,128)S(1)}, f32[256,256]{1,0:T(8,128)S(1)}) custom-call(s32[4]{0:T(128)S(1)} %get-tuple-element.47.order_ref, bf16[576,256]{1,0:T(8,128)(2,1)S(1)} %bitcast.23, bf16[576,2048]{1,0:T(8,128)(2,1)S(1)} %copy-done.1), custom_call_target="tpu_custom_call" | custom-call | flops 301989888 | bytes 2228224 | tf_op jit(solution)/shard_map/preact_send/pallas_call | solution.py:60
  5.6 3.3 %collective-permute-start.1 = (f32[256,256]{1,0:T(8,128)S(1)}, f32[256,256]{1,0:T(8,128)S(1)}, u32[]{:S(2)}, u32[]{:S(2)}) collective-permute-start(f32[256,256]{1,0:T(8,128)S(1)} %get-tuple-element.28), channel_id=1, source_target_pairs={{0,32},{32,0},{64,96},{96,64},{128,160},{160,128},{192,224},{224,1... | collective-permute-start | bytes 786440 | tf_op jit(solution)/shard_map/ppermute | solution.py:31
  9.0 0.4 collective-permute-start.5
  9.4 0.5 multiply_reduce_fusion
  9.9 0.2 collective-permute-start.14
  10.1 0.4 collective-permute-start
  10.5 2.1 %preact_keep.1 = (f32[256,256]{1,0:T(8,128)S(1)}, f32[256,256]{1,0:T(8,128)S(1)}, f32[256,256]{1,0:T(8,128)S(1)}, f32[256,256]{1,0:T(8,128)S(1)}) custom-call(s32[4]{0:T(128)S(1)} %get-tuple-element.48.order_ref, bf16[576,256]{1,0:T(8,128)(2,1)S(1)} %bitcast.24, bf16[576,2048]{1,0:T(8,128)(2,1)S(1)} %copy-done.2), custom_call_target="tpu_custom_call" | custom-call | flops 301989888 | bytes 2228224 | tf_op jit(solution)/shard_map/preact_keep/pallas_call | solution.py:60
  12.7 0.7 add.136
  13.4 1.0 collective-permute-start.2
  14.5 0.7 add.138
  15.2 0.3 collective-permute-start.4
  15.5 0.7 add.140
  16.2 2.4 %collective-permute-start.6 = (f32[256,256]{1,0:T(8,128)}, f32[256,256]{1,0:T(8,128)}, u32[]{:S(2)}, u32[]{:S(2)}) collective-permute-start(f32[256,256]{1,0:T(8,128)} %add.140), channel_id=1, source_target_pairs={{0,192},{32,224},{64,0},{96,32},{128,64},{160,96},{192,128},{224,1... | collective-permute-start | bytes 786440 | tf_op jit(solution)/shard_map/ppermute | solution.py:31
  18.6 0.8 dynamic_slice.9
  19.5 3.7 %collective-permute-done.2 = f32[256,256]{1,0:T(8,128)} collective-permute-done((f32[256,256]{1,0:T(8,128)}, f32[256,256]{1,0:T(8,128)}, u32[]{:S(2)}, u32[]{:S(2)}) %collective-permute-start.2) | collective-permute-done | bytes 262176 | tf_op jit(solution)/shard_map/ppermute | solution.py:31
  23.2 6.0 %collective-permute-done.4 = f32[256,256]{1,0:T(8,128)} collective-permute-done((f32[256,256]{1,0:T(8,128)}, f32[256,256]{1,0:T(8,128)}, u32[]{:S(2)}, u32[]{:S(2)}) %collective-permute-start.4) | collective-permute-done | bytes 262176 | tf_op jit(solution)/shard_map/ppermute | solution.py:31
  29.1 1.2 maximum_convert_fusion.refs_0_
  30.4 0.8 collective-permute-start.9
  31.1 0.5 collective-permute-start.8
  31.7 0.6 collective-permute-start.7
  32.3 2.1 %collective-permute-start.16 = (f32[16,128]{1,0:T(8,128)S(1)}, f32[16,128]{1,0:T(8,128)S(1)}, u32[]{:S(2)}, u32[]{:S(2)}) collective-permute-start(f32[16,128]{1,0:T(8,128)S(1)} %add_sqrt_fusion), channel_id=1, source_target_pairs={{0,192},{32,224},{64,128},{96,160},{128,64},{160,96},{192,0},{224,... | collective-permute-start | bytes 24584 | tf_op jit(solution)/shard_map/ppermute | solution.py:31
  34.5 1.8 %collective-permute-start.10 = (bf16[256,256]{1,0:T(8,128)(2,1)S(1)}, bf16[256,256]{1,0:T(8,128)(2,1)S(1)}, u32[]{:S(2)}, u32[]{:S(2)}) collective-permute-start(bf16[256,256]{1,0:T(8,128)(2,1)S(1)} %maximum_convert_fusion.refs_0_), channel_id=1, source_target_pairs={{0,32},{32,0},{64,96},{96,64},{128,160},{160,128},{192,224},{224,1... | collective-permute-start | bytes 393224 | tf_op jit(solution)/shard_map/ppermute | solution.py:31
  36.2 1.0 collective-permute-start.13
  37.3 2.5 %collective-permute-start.12 = (bf16[256,256]{1,0:T(8,128)(2,1)S(1)}, bf16[256,256]{1,0:T(8,128)(2,1)S(1)}, u32[]{:S(2)}, u32[]{:S(2)}) collective-permute-start(bf16[256,256]{1,0:T(8,128)(2,1)S(1)} %collective-permute-done.8.refs_2_), channel_id=1, source_target_pairs={{0,32},{32,0},{64,96},{96,64},{128,160},{160,128},{192,224},{224,1... | collective-permute-start | bytes 393224 | tf_op jit(solution)/shard_map/ppermute | solution.py:31
  39.8 1.0 collective-permute-done.7.refs_1_
  40.8 0.7 collective-permute-start.11
  41.6 0.8 collective-permute-done.11.refs_5_
  42.4 4.4 %rebuild.1 = bf16[256,640]{1,0:T(8,128)(2,1)} custom-call(s32[8]{0:T(128)S(1)} %pad_add_fusion.order_ref, bf16[256,256]{1,0:T(8,128)(2,1)S(1)} %maximum_convert_fusion.refs_0_, bf16[256,256]{1,0:T(8,128)(2,1)S(1)} %collective-permute-done.7.refs_1_, bf16[256,256]{1,0:T(8,128)(2,1)S(1)} %collective-permute-done.8.refs_2_, ...), custom_call_target="tpu_custom_call" | custom-call | flops 603979776 | bytes 3407872 | tf_op jit(solution)/shard_map/rebuild/pallas_call | solution.py:96
  46.9 0.7 copy-done.9
  47.5 11.2 %all-to-all-start = ((bf16[32,8,640]{2,1,0:T(8,128)(2,1)}), bf16[32,8,640]{2,1,0:T(8,128)(2,1)S(1)}, u32[]{:S(2)}, u32[]{:S(2)}) async-start(bf16[32,8,640]{2,1,0:T(8,128)(2,1)} %bitcast.4), calls=%async_computation | async-start | bytes 655360 | tf_op jit(solution)/shard_map/all_to_all | solution.py:239
  58.7 0.8 constant_dynamic-slice_fusion
  59.5 1.6 %copy.11 = bf16[8,576]{1,0:T(8,128)(2,1)} copy(bf16[8,576]{0,1:T(8,128)(2,1)} %constant_dynamic-slice_fusion) | data formatting | bytes 18432
  61.1 0.7 convert_subtract_fusion.offset_ref
  61.8 9.7 %all-to-all-done.parts_ref = bf16[32,8,640]{2,1,0:T(8,128)(2,1)S(1)} async-done(((bf16[32,8,640]{2,1,0:T(8,128)(2,1)}), bf16[32,8,640]{2,1,0:T(8,128)(2,1)S(1)}, u32[]{:S(2)}, u32[]{:S(2)}) %all-to-all-start) | async-done | bytes 327712 | tf_op jit(solution)/shard_map/all_to_all | solution.py:239
  71.5 0.3 error_rows.1
  71.8 15.8 %all_to_all.10 = bf16[32,8,640]{2,1,0:T(8,128)(2,1)S(1)} all-to-all(bf16[32,8,640]{2,1,0:T(8,128)(2,1)S(1)} %error_rows.1), channel_id=1, replica_groups=mesh['width'=8,'latent'=32] {'latent'}, dimensions={0} | all-to-all | bytes 655360 | tf_op jit(solution)/shard_map/all_to_all | solution.py:241
  87.6 1.9 %back_send.1 = (bf16[256,256]{1,0:T(8,128)(2,1)S(1)}, bf16[256,256]{1,0:T(8,128)(2,1)S(1)}, bf16[256,256]{1,0:T(8,128)(2,1)S(1)}, bf16[256,256]{1,0:T(8,128)(2,1)S(1)}) custom-call(s32[4]{0:T(128)S(1)} %get-tuple-element.47.order_ref, bf16[256,640]{1,0:T(8,128)(2,1)S(1)} %bitcast.19, bf16[576,2048]{1,0:T(8,128)(2,1)S(1)} %bitcast.16), custom_call_target="tpu_custom_call" | custom-call | flops 301989888 | bytes 2228224 | tf_op jit(solution)/shard_map/back_send/pallas_call | solution.py:60
  89.5 3.8 %collective-permute-start.21 = (bf16[256,256]{1,0:T(8,128)(2,1)S(1)}, bf16[256,256]{1,0:T(8,128)(2,1)S(1)}, u32[]{:S(2)}, u32[]{:S(2)}) collective-permute-start(bf16[256,256]{1,0:T(8,128)(2,1)S(1)} %get-tuple-element.36), channel_id=1, source_target_pairs={{0,32},{32,0},{64,96},{96,64},{128,160},{160,128},{192,224},{224,1... | collective-permute-start | bytes 393224 | tf_op jit(solution)/shard_map/ppermute | solution.py:31
  93.4 0.4 collective-permute-start.23
  93.8 0.2 collective-permute-start.25
  94.0 2.0 %back_keep.1 = (f32[256,256]{1,0:T(8,128)S(1)}, f32[256,256]{1,0:T(8,128)S(1)}, f32[256,256]{1,0:T(8,128)S(1)}, f32[256,256]{1,0:T(8,128)S(1)}) custom-call(s32[4]{0:T(128)S(1)} %get-tuple-element.48.order_ref, bf16[256,640]{1,0:T(8,128)(2,1)S(1)} %bitcast.20, bf16[576,2048]{1,0:T(8,128)(2,1)S(1)} %bitcast.17), custom_call_target="tpu_custom_call" | custom-call | flops 301989888 | bytes 2228224 | tf_op jit(solution)/shard_map/back_keep/pallas_call | solution.py:60
  96.0 0.6 collective-permute-start.22
  96.7 0.5 collective-permute-start.24
  97.2 2.4 %collective-permute-start.26 = (bf16[256,256]{1,0:T(8,128)(2,1)S(1)}, bf16[256,256]{1,0:T(8,128)(2,1)S(1)}, u32[]{:S(2)}, u32[]{:S(2)}) collective-permute-start(bf16[256,256]{1,0:T(8,128)(2,1)S(1)} %add_convert_fusion), channel_id=1, source_target_pairs={{0,192},{32,224},{64,0},{96,32},{128,64},{160,96},{192,128},{224,1... | collective-permute-start | bytes 393224 | tf_op jit(solution)/shard_map/ppermute | solution.py:31
  99.5 0.7 convert_reduce_fusion
  100.2 0.6 broadcast_in_dim.3
  100.9 1.3 %collective-permute-start.17 = (f32[8,128]{1,0:T(8,128)S(1)}, f32[8,128]{1,0:T(8,128)S(1)}, u32[]{:S(2)}, u32[]{:S(2)}) collective-permute-start(f32[8,128]{1,0:T(8,128)S(1)} %broadcast_in_dim.3), channel_id=1, source_target_pairs={{0,32},{32,0},{64,96},{96,64},{128,160},{160,128},{192,224},{224,1... | collective-permute-start | bytes 12296 | tf_op jit(solution)/shard_map/ppermute | solution.py:31
  102.3 3.5 %collective-permute-done.24 = bf16[256,256]{1,0:T(8,128)(2,1)S(1)} collective-permute-done((bf16[256,256]{1,0:T(8,128)(2,1)S(1)}, bf16[256,256]{1,0:T(8,128)(2,1)S(1)}, u32[]{:S(2)}, u32[]{:S(2)}) %collective-permute-start.24) | collective-permute-done | bytes 131104 | tf_op jit(solution)/shard_map/ppermute | solution.py:31
  105.8 0.1 select_convert_fusion.refs_0_
  106.1 0.6 collective-permute-start.28
  106.7 0.8 collective-permute-start.27
  107.5 0.6 broadcast_add_fusion
  108.2 1.6 %collective-permute-start.18 = (f32[8,128]{1,0:T(8,128)S(1)}, f32[8,128]{1,0:T(8,128)S(1)}, u32[]{:S(2)}, u32[]{:S(2)}) collective-permute-start(f32[8,128]{1,0:T(8,128)S(1)} %broadcast_add_fusion), channel_id=1, source_target_pairs={{0,64},{32,96},{64,0},{96,32},{128,192},{160,224},{192,128},{224,1... | collective-permute-start | bytes 12296 | tf_op jit(solution)/shard_map/ppermute | solution.py:31
  109.8 5.2 %decoder_gradient.1 = (bf16[576,2048]{1,0:T(8,128)(2,1)}, f32[1,640]{1,0:T(1,128)S(1)}) custom-call(s32[8]{0:T(128)S(1)} %pad_add_fusion.order_ref, bf16[256,640]{1,0:T(8,128)(2,1)S(1)} %bitcast.22, bf16[256,256]{1,0:T(8,128)(2,1)S(1)} %maximum_convert_fusion.refs_0_, bf16[256,256]{1,0:T(8,128)(2,1)S(1)} %collective-permute-done.7.refs_1_, ...), custom_call_target="tpu_custom_call" | custom-call | flops 603979776 | bytes 5767168 | tf_op jit(solution)/shard_map/decoder_gradient/pallas_call | solution.py:151
  115.0 2.3 %collective-permute-start.30 = (bf16[256,256]{1,0:T(8,128)(2,1)S(1)}, bf16[256,256]{1,0:T(8,128)(2,1)S(1)}, u32[]{:S(2)}, u32[]{:S(2)}) collective-permute-start(bf16[256,256]{1,0:T(8,128)(2,1)S(1)} %select_convert_fusion.refs_0_), channel_id=1, source_target_pairs={{0,32},{32,0},{64,96},{96,64},{128,160},{160,128},{192,224},{224,1... | collective-permute-start | bytes 393224 | tf_op jit(solution)/shard_map/ppermute | solution.py:31
  117.3 0.5 collective-permute-start.32
  117.9 0.6 fusion.4
  118.6 2.0 %collective-permute-start.19 = (f32[8,128]{1,0:T(8,128)S(1)}, f32[8,128]{1,0:T(8,128)S(1)}, u32[]{:S(2)}, u32[]{:S(2)}) collective-permute-start(f32[8,128]{1,0:T(8,128)S(1)} %fusion.4), channel_id=1, source_target_pairs={{0,192},{32,224},{64,128},{96,160},{128,64},{160,96},{192,0},{224,... | collective-permute-start | bytes 12296 | tf_op jit(solution)/shard_map/ppermute | solution.py:31
  120.6 0.6 slice_reduce_fusion
  121.2 1.2 collective-permute-done.19
  122.3 0.5 slice.10
  123.5 4.8 %encoder_gradient.1 = (bf16[576,2048]{1,0:T(8,128)(2,1)}, f32[1,2048]{1,0:T(1,128)}) custom-call(s32[8]{0:T(128)S(1)} %pad_add_fusion.order_ref, bf16[576,256]{1,0:T(8,128)(2,1)S(1)} %bitcast.25, bf16[256,256]{1,0:T(8,128)(2,1)S(1)} %select_convert_fusion.refs_0_, bf16[256,256]{1,0:T(8,128)(2,1)S(1)} %collective-permute-done.27.refs_1_, ...), custom_call_target="tpu_custom_call" | custom-call | flops 603979776 | bytes 3407872 | tf_op jit(solution)/shard_map/encoder_gradient/pallas_call | solution.py:180
  (70 shorter events, 0.8 us)
Async XLA Ops:
  0.6 8.8 %copy-start = (bf16[2048,576]{0,1:T(8,128)(2,1)S(1)}, bf16[2048,576]{0,1:T(8,128)(2,1)}, u32[]{:S(2)}) copy-start(bf16[2048,576]{0,1:T(8,128)(2,1)} %param.8) | copy-start | bytes 7077892
  0.7 1.8 %copy-start.1 = (bf16[576,2048]{1,0:T(8,128)(2,1)S(1)}, bf16[576,2048]{1,0:T(8,128)(2,1)}, u32[]{:S(2)}) copy-start(bf16[576,2048]{1,0:T(8,128)(2,1)} %matrix_ref.3) | copy-start | bytes 7077892
  2.5 1.0 copy-start.3
  3.5 7.1 %copy-start.2 = (bf16[576,2048]{1,0:T(8,128)(2,1)S(1)}, bf16[576,2048]{1,0:T(8,128)(2,1)}, u32[]{:S(2)}) copy-start(bf16[576,2048]{1,0:T(8,128)(2,1)} %matrix_ref.3) | copy-start | bytes 7077892
  3.5 7.1 %copy-start.4 = (bf16[256,576]{0,1:T(8,128)(2,1)S(1)}, bf16[256,576]{0,1:T(8,128)(2,1)}, u32[]{:S(2)}) copy-start(bf16[256,576]{0,1:T(8,128)(2,1)} %param.5) | copy-start | bytes 884740
  5.6 7.1 %collective-permute-start.1 = (f32[256,256]{1,0:T(8,128)S(1)}, f32[256,256]{1,0:T(8,128)S(1)}, u32[]{:S(2)}, u32[]{:S(2)}) collective-permute-start(f32[256,256]{1,0:T(8,128)S(1)} %get-tuple-element.28), channel_id=1, source_target_pairs={{0,32},{32,0},{64,96},{96,64},{128,160},{160,128},{192,224},{224,1... | collective-permute-start | bytes 786440 | tf_op jit(solution)/shard_map/ppermute | solution.py:31
  8.9 5.5 %collective-permute-start.3 = (f32[256,256]{1,0:T(8,128)S(1)}, f32[256,256]{1,0:T(8,128)S(1)}, u32[]{:S(2)}, u32[]{:S(2)}) collective-permute-start(f32[256,256]{1,0:T(8,128)S(1)} %get-tuple-element.30), channel_id=1, source_target_pairs={{0,32},{32,0},{64,96},{96,64},{128,160},{160,128},{192,224},{224,1... | collective-permute-start | bytes 786440 | tf_op jit(solution)/shard_map/ppermute | solution.py:31
  9.0 6.5 %collective-permute-start.5 = (f32[256,256]{1,0:T(8,128)S(1)}, f32[256,256]{1,0:T(8,128)S(1)}, u32[]{:S(2)}, u32[]{:S(2)}) collective-permute-start(f32[256,256]{1,0:T(8,128)S(1)} %get-tuple-element.32), channel_id=1, source_target_pairs={{0,32},{32,0},{64,96},{96,64},{128,160},{160,128},{192,224},{224,1... | collective-permute-start | bytes 786440 | tf_op jit(solution)/shard_map/ppermute | solution.py:31
  9.9 9.5 %collective-permute-start.14 = (f32[16,128]{1,0:T(8,128)S(1)}, f32[16,128]{1,0:T(8,128)S(1)}, u32[]{:S(2)}, u32[]{:S(2)}) collective-permute-start(f32[16,128]{1,0:T(8,128)S(1)} %bitcast.27), channel_id=1, source_target_pairs={{0,32},{32,0},{64,96},{96,64},{128,160},{160,128},{192,224},{224,1... | collective-permute-start | bytes 24584 | tf_op jit(solution)/shard_map/ppermute | solution.py:31
  10.1 9.3 %collective-permute-start = (f32[256,256]{1,0:T(8,128)S(1)}, f32[256,256]{1,0:T(8,128)S(1)}, u32[]{:S(2)}, u32[]{:S(2)}) collective-permute-start(f32[256,256]{1,0:T(8,128)S(1)} %get-tuple-element.26), channel_id=1, source_target_pairs={{0,32},{32,0},{64,96},{96,64},{128,160},{160,128},{192,224},{224,1... | collective-permute-start | bytes 786440 | tf_op jit(solution)/shard_map/ppermute | solution.py:31
  13.4 9.7 %collective-permute-start.2 = (f32[256,256]{1,0:T(8,128)}, f32[256,256]{1,0:T(8,128)}, u32[]{:S(2)}, u32[]{:S(2)}) collective-permute-start(f32[256,256]{1,0:T(8,128)} %add.136), channel_id=1, source_target_pairs={{0,128},{32,160},{64,192},{96,224},{128,0},{160,32},{192,64},{224,... | collective-permute-start | bytes 786440 | tf_op jit(solution)/shard_map/ppermute | solution.py:31
  15.2 13.9 %collective-permute-start.4 = (f32[256,256]{1,0:T(8,128)}, f32[256,256]{1,0:T(8,128)}, u32[]{:S(2)}, u32[]{:S(2)}) collective-permute-start(f32[256,256]{1,0:T(8,128)} %add.138), channel_id=1, source_target_pairs={{0,64},{32,96},{64,128},{96,160},{128,192},{160,224},{192,0},{224,... | collective-permute-start | bytes 786440 | tf_op jit(solution)/shard_map/ppermute | solution.py:31
  16.2 12.9 %collective-permute-start.6 = (f32[256,256]{1,0:T(8,128)}, f32[256,256]{1,0:T(8,128)}, u32[]{:S(2)}, u32[]{:S(2)}) collective-permute-start(f32[256,256]{1,0:T(8,128)} %add.140), channel_id=1, source_target_pairs={{0,192},{32,224},{64,0},{96,32},{128,64},{160,96},{192,128},{224,1... | collective-permute-start | bytes 786440 | tf_op jit(solution)/shard_map/ppermute | solution.py:31
  19.4 12.9 %collective-permute-start.15 = (f32[16,128]{1,0:T(8,128)S(1)}, f32[16,128]{1,0:T(8,128)S(1)}, u32[]{:S(2)}, u32[]{:S(2)}) collective-permute-start(f32[16,128]{1,0:T(8,128)S(1)} %bitcast_add_fusion), channel_id=1, source_target_pairs={{0,64},{32,96},{64,0},{96,32},{128,192},{160,224},{192,128},{224,1... | collective-permute-start | bytes 24584 | tf_op jit(solution)/shard_map/ppermute | solution.py:31
  30.4 5.9 %collective-permute-start.9 = (bf16[256,256]{1,0:T(8,128)(2,1)S(1)}, bf16[256,256]{1,0:T(8,128)(2,1)S(1)}, u32[]{:S(2)}, u32[]{:S(2)}) collective-permute-start(bf16[256,256]{1,0:T(8,128)(2,1)S(1)} %maximum_convert_fusion.refs_0_), channel_id=1, source_target_pairs={{0,192},{32,224},{64,0},{96,32},{128,64},{160,96},{192,128},{224,1... | collective-permute-start | bytes 393224 | tf_op jit(solution)/shard_map/ppermute | solution.py:31
  31.1 6.1 %collective-permute-start.8 = (bf16[256,256]{1,0:T(8,128)(2,1)S(1)}, bf16[256,256]{1,0:T(8,128)(2,1)S(1)}, u32[]{:S(2)}, u32[]{:S(2)}) collective-permute-start(bf16[256,256]{1,0:T(8,128)(2,1)S(1)} %maximum_convert_fusion.refs_0_), channel_id=1, source_target_pairs={{0,128},{32,160},{64,192},{96,224},{128,0},{160,32},{192,64},{224,... | collective-permute-start | bytes 393224 | tf_op jit(solution)/shard_map/ppermute | solution.py:31
  31.7 9.1 %collective-permute-start.7 = (bf16[256,256]{1,0:T(8,128)(2,1)S(1)}, bf16[256,256]{1,0:T(8,128)(2,1)S(1)}, u32[]{:S(2)}, u32[]{:S(2)}) collective-permute-start(bf16[256,256]{1,0:T(8,128)(2,1)S(1)} %maximum_convert_fusion.refs_0_), channel_id=1, source_target_pairs={{0,64},{32,96},{64,128},{96,160},{128,192},{160,224},{192,0},{224,... | collective-permute-start | bytes 393224 | tf_op jit(solution)/shard_map/ppermute | solution.py:31
  32.3 9.2 %collective-permute-start.16 = (f32[16,128]{1,0:T(8,128)S(1)}, f32[16,128]{1,0:T(8,128)S(1)}, u32[]{:S(2)}, u32[]{:S(2)}) collective-permute-start(f32[16,128]{1,0:T(8,128)S(1)} %add_sqrt_fusion), channel_id=1, source_target_pairs={{0,192},{32,224},{64,128},{96,160},{128,64},{160,96},{192,0},{224,... | collective-permute-start | bytes 24584 | tf_op jit(solution)/shard_map/ppermute | solution.py:31
  34.5 7.1 %collective-permute-start.10 = (bf16[256,256]{1,0:T(8,128)(2,1)S(1)}, bf16[256,256]{1,0:T(8,128)(2,1)S(1)}, u32[]{:S(2)}, u32[]{:S(2)}) collective-permute-start(bf16[256,256]{1,0:T(8,128)(2,1)S(1)} %maximum_convert_fusion.refs_0_), channel_id=1, source_target_pairs={{0,32},{32,0},{64,96},{96,64},{128,160},{160,128},{192,224},{224,1... | collective-permute-start | bytes 393224 | tf_op jit(solution)/shard_map/ppermute | solution.py:31
  36.2 5.3 %collective-permute-start.13 = (bf16[256,256]{1,0:T(8,128)(2,1)S(1)}, bf16[256,256]{1,0:T(8,128)(2,1)S(1)}, u32[]{:S(2)}, u32[]{:S(2)}) collective-permute-start(bf16[256,256]{1,0:T(8,128)(2,1)S(1)} %collective-permute-done.9.refs_3_), channel_id=1, source_target_pairs={{0,32},{32,0},{64,96},{96,64},{128,160},{160,128},{192,224},{224,1... | collective-permute-start | bytes 393224 | tf_op jit(solution)/shard_map/ppermute | solution.py:31
  37.3 4.3 %collective-permute-start.12 = (bf16[256,256]{1,0:T(8,128)(2,1)S(1)}, bf16[256,256]{1,0:T(8,128)(2,1)S(1)}, u32[]{:S(2)}, u32[]{:S(2)}) collective-permute-start(bf16[256,256]{1,0:T(8,128)(2,1)S(1)} %collective-permute-done.8.refs_2_), channel_id=1, source_target_pairs={{0,32},{32,0},{64,96},{96,64},{128,160},{160,128},{192,224},{224,1... | collective-permute-start | bytes 393224 | tf_op jit(solution)/shard_map/ppermute | solution.py:31
  40.8 1.7 %collective-permute-start.11 = (bf16[256,256]{1,0:T(8,128)(2,1)S(1)}, bf16[256,256]{1,0:T(8,128)(2,1)S(1)}, u32[]{:S(2)}, u32[]{:S(2)}) collective-permute-start(bf16[256,256]{1,0:T(8,128)(2,1)S(1)} %collective-permute-done.7.refs_1_), channel_id=1, source_target_pairs={{0,32},{32,0},{64,96},{96,64},{128,160},{160,128},{192,224},{224,1... | collective-permute-start | bytes 393224 | tf_op jit(solution)/shard_map/ppermute | solution.py:31
  41.6 6.0 %copy-start.5 = (bf16[256,256]{1,0:T(8,128)(2,1)}, bf16[256,256]{1,0:T(8,128)(2,1)S(1)}, u32[]{:S(2)}) copy-start(bf16[256,256]{1,0:T(8,128)(2,1)S(1)} %collective-permute-done.10.refs_4_) | copy-start | bytes 393220
  41.6 5.9 %copy-start.7 = (bf16[256,256]{1,0:T(8,128)(2,1)}, bf16[256,256]{1,0:T(8,128)(2,1)S(1)}, u32[]{:S(2)}) copy-start(bf16[256,256]{1,0:T(8,128)(2,1)S(1)} %collective-permute-done.13.refs_7_) | copy-start | bytes 393220
  42.4 4.4 %copy-start.11 = (bf16[256,256]{1,0:T(8,128)(2,1)}, bf16[256,256]{1,0:T(8,128)(2,1)S(1)}, u32[]{:S(2)}) copy-start(bf16[256,256]{1,0:T(8,128)(2,1)S(1)} %collective-permute-done.11.refs_5_) | copy-start | bytes 393220
  42.4 18.7 %copy-start.13 = (f32[576]{0:T(1024)S(1)}, f32[576]{0:T(1024)}, u32[]{:S(2)}) copy-start(f32[576]{0:T(1024)} %param.9) | copy-start | bytes 6916
  46.8 0.7 copy-start.9
  47.5 24.0 %all-to-all-start = ((bf16[32,8,640]{2,1,0:T(8,128)(2,1)}), bf16[32,8,640]{2,1,0:T(8,128)(2,1)S(1)}, u32[]{:S(2)}, u32[]{:S(2)}) async-start(bf16[32,8,640]{2,1,0:T(8,128)(2,1)} %bitcast.4), calls=%async_computation | async-start | bytes 655360 | tf_op jit(solution)/shard_map/all_to_all | solution.py:239
  89.5 6.5 %collective-permute-start.21 = (bf16[256,256]{1,0:T(8,128)(2,1)S(1)}, bf16[256,256]{1,0:T(8,128)(2,1)S(1)}, u32[]{:S(2)}, u32[]{:S(2)}) collective-permute-start(bf16[256,256]{1,0:T(8,128)(2,1)S(1)} %get-tuple-element.36), channel_id=1, source_target_pairs={{0,32},{32,0},{64,96},{96,64},{128,160},{160,128},{192,224},{224,1... | collective-permute-start | bytes 393224 | tf_op jit(solution)/shard_map/ppermute | solution.py:31
  93.3 9.0 %collective-permute-start.20 = (bf16[256,256]{1,0:T(8,128)(2,1)S(1)}, bf16[256,256]{1,0:T(8,128)(2,1)S(1)}, u32[]{:S(2)}, u32[]{:S(2)}) collective-permute-start(bf16[256,256]{1,0:T(8,128)(2,1)S(1)} %get-tuple-element.34), channel_id=1, source_target_pairs={{0,32},{32,0},{64,96},{96,64},{128,160},{160,128},{192,224},{224,1... | collective-permute-start | bytes 393224 | tf_op jit(solution)/shard_map/ppermute | solution.py:31
  93.4 3.3 %collective-permute-start.23 = (bf16[256,256]{1,0:T(8,128)(2,1)S(1)}, bf16[256,256]{1,0:T(8,128)(2,1)S(1)}, u32[]{:S(2)}, u32[]{:S(2)}) collective-permute-start(bf16[256,256]{1,0:T(8,128)(2,1)S(1)} %get-tuple-element.38), channel_id=1, source_target_pairs={{0,32},{32,0},{64,96},{96,64},{128,160},{160,128},{192,224},{224,1... | collective-permute-start | bytes 393224 | tf_op jit(solution)/shard_map/ppermute | solution.py:31
  93.8 16.0 %copy-start.6 = (bf16[256,256]{1,0:T(8,128)(2,1)S(1)}, bf16[256,256]{1,0:T(8,128)(2,1)}, u32[]{:S(2)}) copy-start(bf16[256,256]{1,0:T(8,128)(2,1)} %copy-done.5) | copy-start | bytes 393220
  93.8 16.0 %copy-start.8 = (bf16[256,256]{1,0:T(8,128)(2,1)S(1)}, bf16[256,256]{1,0:T(8,128)(2,1)}, u32[]{:S(2)}) copy-start(bf16[256,256]{1,0:T(8,128)(2,1)} %copy-done.7) | copy-start | bytes 393220
  93.8 16.0 %copy-start.10 = (bf16[256,256]{1,0:T(8,128)(2,1)S(1)}, bf16[256,256]{1,0:T(8,128)(2,1)}, u32[]{:S(2)}) copy-start(bf16[256,256]{1,0:T(8,128)(2,1)} %copy-done.9) | copy-start | bytes 393220
  93.8 16.0 %copy-start.12 = (bf16[256,256]{1,0:T(8,128)(2,1)S(1)}, bf16[256,256]{1,0:T(8,128)(2,1)}, u32[]{:S(2)}) copy-start(bf16[256,256]{1,0:T(8,128)(2,1)} %copy-done.11) | copy-start | bytes 393220
  93.8 3.3 %collective-permute-start.25 = (bf16[256,256]{1,0:T(8,128)(2,1)S(1)}, bf16[256,256]{1,0:T(8,128)(2,1)S(1)}, u32[]{:S(2)}, u32[]{:S(2)}) collective-permute-start(bf16[256,256]{1,0:T(8,128)(2,1)S(1)} %get-tuple-element.40), channel_id=1, source_target_pairs={{0,32},{32,0},{64,96},{96,64},{128,160},{160,128},{192,224},{224,1... | collective-permute-start | bytes 393224 | tf_op jit(solution)/shard_map/ppermute | solution.py:31
  96.0 6.3 %collective-permute-start.22 = (bf16[256,256]{1,0:T(8,128)(2,1)S(1)}, bf16[256,256]{1,0:T(8,128)(2,1)S(1)}, u32[]{:S(2)}, u32[]{:S(2)}) collective-permute-start(bf16[256,256]{1,0:T(8,128)(2,1)S(1)} %add_convert_fusion.2), channel_id=1, source_target_pairs={{0,128},{32,160},{64,192},{96,224},{128,0},{160,32},{192,64},{224,... | collective-permute-start | bytes 393224 | tf_op jit(solution)/shard_map/ppermute | solution.py:31
  96.7 9.2 %collective-permute-start.24 = (bf16[256,256]{1,0:T(8,128)(2,1)S(1)}, bf16[256,256]{1,0:T(8,128)(2,1)S(1)}, u32[]{:S(2)}, u32[]{:S(2)}) collective-permute-start(bf16[256,256]{1,0:T(8,128)(2,1)S(1)} %add_convert_fusion.1), channel_id=1, source_target_pairs={{0,64},{32,96},{64,128},{96,160},{128,192},{160,224},{192,0},{224,... | collective-permute-start | bytes 393224 | tf_op jit(solution)/shard_map/ppermute | solution.py:31
  97.2 8.7 %collective-permute-start.26 = (bf16[256,256]{1,0:T(8,128)(2,1)S(1)}, bf16[256,256]{1,0:T(8,128)(2,1)S(1)}, u32[]{:S(2)}, u32[]{:S(2)}) collective-permute-start(bf16[256,256]{1,0:T(8,128)(2,1)S(1)} %add_convert_fusion), channel_id=1, source_target_pairs={{0,192},{32,224},{64,0},{96,32},{128,64},{160,96},{192,128},{224,1... | collective-permute-start | bytes 393224 | tf_op jit(solution)/shard_map/ppermute | solution.py:31
  100.9 6.6 %collective-permute-start.17 = (f32[8,128]{1,0:T(8,128)S(1)}, f32[8,128]{1,0:T(8,128)S(1)}, u32[]{:S(2)}, u32[]{:S(2)}) collective-permute-start(f32[8,128]{1,0:T(8,128)S(1)} %broadcast_in_dim.3), channel_id=1, source_target_pairs={{0,32},{32,0},{64,96},{96,64},{128,160},{160,128},{192,224},{224,1... | collective-permute-start | bytes 12296 | tf_op jit(solution)/shard_map/ppermute | solution.py:31
  106.0 11.3 %collective-permute-start.29 = (bf16[256,256]{1,0:T(8,128)(2,1)S(1)}, bf16[256,256]{1,0:T(8,128)(2,1)S(1)}, u32[]{:S(2)}, u32[]{:S(2)}) collective-permute-start(bf16[256,256]{1,0:T(8,128)(2,1)S(1)} %select_convert_fusion.refs_0_), channel_id=1, source_target_pairs={{0,192},{32,224},{64,0},{96,32},{128,64},{160,96},{192,128},{224,1... | collective-permute-start | bytes 393224 | tf_op jit(solution)/shard_map/ppermute | solution.py:31
  106.1 11.2 %collective-permute-start.28 = (bf16[256,256]{1,0:T(8,128)(2,1)S(1)}, bf16[256,256]{1,0:T(8,128)(2,1)S(1)}, u32[]{:S(2)}, u32[]{:S(2)}) collective-permute-start(bf16[256,256]{1,0:T(8,128)(2,1)S(1)} %select_convert_fusion.refs_0_), channel_id=1, source_target_pairs={{0,128},{32,160},{64,192},{96,224},{128,0},{160,32},{192,64},{224,... | collective-permute-start | bytes 393224 | tf_op jit(solution)/shard_map/ppermute | solution.py:31
  106.7 11.1 %collective-permute-start.27 = (bf16[256,256]{1,0:T(8,128)(2,1)S(1)}, bf16[256,256]{1,0:T(8,128)(2,1)S(1)}, u32[]{:S(2)}, u32[]{:S(2)}) collective-permute-start(bf16[256,256]{1,0:T(8,128)(2,1)S(1)} %select_convert_fusion.refs_0_), channel_id=1, source_target_pairs={{0,64},{32,96},{64,128},{96,160},{128,192},{160,224},{192,0},{224,... | collective-permute-start | bytes 393224 | tf_op jit(solution)/shard_map/ppermute | solution.py:31
  108.2 9.7 %collective-permute-start.18 = (f32[8,128]{1,0:T(8,128)S(1)}, f32[8,128]{1,0:T(8,128)S(1)}, u32[]{:S(2)}, u32[]{:S(2)}) collective-permute-start(f32[8,128]{1,0:T(8,128)S(1)} %broadcast_add_fusion), channel_id=1, source_target_pairs={{0,64},{32,96},{64,0},{96,32},{128,192},{160,224},{192,128},{224,1... | collective-permute-start | bytes 12296 | tf_op jit(solution)/shard_map/ppermute | solution.py:31
  115.0 8.5 %collective-permute-start.30 = (bf16[256,256]{1,0:T(8,128)(2,1)S(1)}, bf16[256,256]{1,0:T(8,128)(2,1)S(1)}, u32[]{:S(2)}, u32[]{:S(2)}) collective-permute-start(bf16[256,256]{1,0:T(8,128)(2,1)S(1)} %select_convert_fusion.refs_0_), channel_id=1, source_target_pairs={{0,32},{32,0},{64,96},{96,64},{128,160},{160,128},{192,224},{224,1... | collective-permute-start | bytes 393224 | tf_op jit(solution)/shard_map/ppermute | solution.py:31
  117.3 6.2 %collective-permute-start.33 = (bf16[256,256]{1,0:T(8,128)(2,1)S(1)}, bf16[256,256]{1,0:T(8,128)(2,1)S(1)}, u32[]{:S(2)}, u32[]{:S(2)}) collective-permute-start(bf16[256,256]{1,0:T(8,128)(2,1)S(1)} %collective-permute-done.29.refs_3_), channel_id=1, source_target_pairs={{0,32},{32,0},{64,96},{96,64},{128,160},{160,128},{192,224},{224,1... | collective-permute-start | bytes 393224 | tf_op jit(solution)/shard_map/ppermute | solution.py:31
  117.3 6.2 %collective-permute-start.32 = (bf16[256,256]{1,0:T(8,128)(2,1)S(1)}, bf16[256,256]{1,0:T(8,128)(2,1)S(1)}, u32[]{:S(2)}, u32[]{:S(2)}) collective-permute-start(bf16[256,256]{1,0:T(8,128)(2,1)S(1)} %collective-permute-done.28.refs_2_), channel_id=1, source_target_pairs={{0,32},{32,0},{64,96},{96,64},{128,160},{160,128},{192,224},{224,1... | collective-permute-start | bytes 393224 | tf_op jit(solution)/shard_map/ppermute | solution.py:31
  117.8 5.7 %collective-permute-start.31 = (bf16[256,256]{1,0:T(8,128)(2,1)S(1)}, bf16[256,256]{1,0:T(8,128)(2,1)S(1)}, u32[]{:S(2)}, u32[]{:S(2)}) collective-permute-start(bf16[256,256]{1,0:T(8,128)(2,1)S(1)} %collective-permute-done.27.refs_1_), channel_id=1, source_target_pairs={{0,32},{32,0},{64,96},{96,64},{128,160},{160,128},{192,224},{224,1... | collective-permute-start | bytes 393224 | tf_op jit(solution)/shard_map/ppermute | solution.py:31
  118.6 3.8 %collective-permute-start.19 = (f32[8,128]{1,0:T(8,128)S(1)}, f32[8,128]{1,0:T(8,128)S(1)}, u32[]{:S(2)}, u32[]{:S(2)}) collective-permute-start(f32[8,128]{1,0:T(8,128)S(1)} %fusion.4), channel_id=1, source_target_pairs={{0,192},{32,224},{64,128},{96,160},{128,64},{160,96},{192,0},{224,... | collective-permute-start | bytes 12296 | tf_op jit(solution)/shard_map/ppermute | solution.py:31

commit v2 on v0

v2 whole, which is shorter than its diff:
```python
import jax
import jax.numpy as jnp
from jax import lax
from jax.experimental import pallas as pl
from jax.experimental.pallas import tpu as pltpu
from jax.sharding import PartitionSpec as P

D = 2304
LAYERS = 2
SPARSITY = 0.5
EPSILON = 1e-06
F32 = jnp.float32
BF16 = jnp.bfloat16
TOK = 256
COL = 576
CHUNK = 256
WIDE = 640
LAT = 2048
ROWS = TOK + 16
SPAN = 250.0
LOWEST = 125.0
LN2 = 0.6931471805599453
HOPS = (2, 1, 3)
FIRST = 4
VMEM_BYTES = 16 * 1024 * 1024

CORE_SWAP = [(i, i ^ 1) for i in range(8)]


def x_shift(d):
    return [(i, (i + 2 * d) % 8) for i in range(8)]


def on_width(value, pairs):
    return lax.ppermute(value, "width", pairs)


def dot(a, b, dims):
    return lax.dot_general(a, b, (dims, ((), ())), preferred_element_type=F32)


IN_VMEM = pl.BlockSpec(memory_space=pltpu.VMEM)
ANYWHERE = pl.BlockSpec(memory_space=pl.ANY)


def call(body, name, args, in_specs, outs, out_specs=None, scratch=(), flops=0, moved=0):
    return pl.pallas_call(
        body,
        in_specs=in_specs,
        out_specs=out_specs or [IN_VMEM] * len(outs),
        out_shape=[jax.ShapeDtypeStruct(shape, kind) for shape, kind in outs],
        scratch_shapes=list(scratch),
        compiler_params=pltpu.CompilerParams(vmem_limit_bytes=VMEM_BYTES),
        name=name,
        cost_estimate=pl.CostEstimate(flops=flops, bytes_accessed=moved, transcendentals=0),
    )(*args)


def place():
    width_index = lax.axis_index("width")
    return width_index // 2, width_index % 2


def owner(x, core):
    return lax.rem(x + 4, 4) * 2 + core


def gathered_owners():
    x, core = place()
    return [owner(x - d, side) for d in (0, *HOPS) for side in (core, 1 - core)]


def columns(chunk):
    return pl.ds(pl.multiple_of(chunk * CHUNK, CHUNK), CHUNK)


def preact_send(act_t, encoder):
    def body(act_ref, enc_ref, *refs):
        outs, (act_out, act_buf, enc_buf, act_sem, sems) = refs[:4], refs[4:]
        x, core = place()
        act_copy = pltpu.make_async_copy(act_ref, act_buf, act_sem)
        act_copy.start()
        copies = []
        for d in range(4):
            span = columns(owner(x + d, 1 - core))
            copies.append(pltpu.make_async_copy(enc_ref.at[:, span], enc_buf.at[d], sems.at[d]))
            copies[d].start()
        act_copy.wait()
        act = act_buf[...].T
        act_out[...] = act
        for d in range(4):
            copies[d].wait()
            outs[d][...] = dot(act, enc_buf[d], ((1,), (0,)))

    act_t = pltpu.with_memory_space_constraint(act_t, pltpu.HBM)
    encoder = pltpu.with_memory_space_constraint(encoder, pltpu.HBM)
    found = call(
        body, "preact_send", (act_t, encoder), [ANYWHERE] * 2, [((TOK, CHUNK), F32)] * 4 + [((TOK, COL), BF16)],
        scratch=[
            pltpu.VMEM((COL, TOK), BF16), pltpu.VMEM((4, COL, CHUNK), BF16),
            pltpu.SemaphoreType.DMA, pltpu.SemaphoreType.DMA((4,)),
        ],
        flops=8 * TOK * COL * CHUNK, moved=8 * COL * CHUNK + 16 * TOK * CHUNK,
    )
    return found[:4], found[4]


def own_column(left, right, hops, swap, kind, name):
    def body(left_ref, right_ref, *outs):
        x, core = place()
        side = 1 - core if swap else core
        value = left_ref[:, :COL]
        for d, out in zip(hops, outs):
            out[...] = dot(value, right_ref[:, columns(owner(x + d, side))], ((1,), (0,))).astype(kind)

    count = len(hops)
    found = call(
        body, name, (left, right), [IN_VMEM] * 2, [((TOK, CHUNK), kind)] * count,
        flops=2 * count * TOK * COL * CHUNK, moved=2 * count * COL * CHUNK + 2 * count * TOK * CHUNK,
    )
    return dict(zip(hops, found))


def square_sums(dec_t):
    def body(dec_ref, out_ref):
        for chunk in range(8):
            span = slice(chunk * CHUNK, chunk * CHUNK + CHUNK)
            total = jnp.sum(jnp.square(dec_ref[:, span].astype(F32)), axis=0, keepdims=True)
            out_ref[:, span] = jnp.broadcast_to(total, (8, CHUNK))

    return call(body, "square_sums", (dec_t,), [IN_VMEM], [((8, LAT), F32)], flops=2 * COL * LAT, moved=2 * COL * LAT)[0]


def pieces(value, count):
    found = []
    for _ in range(count):
        piece = value.astype(BF16).astype(F32)
        found.append(piece)
        value = value - piece
    return found


def stack_rows(rows):
    index = lax.broadcasted_iota(jnp.int32, (16, rows[0].shape[1]), 0)
    out = jnp.zeros(index.shape, F32)
    for k, row in enumerate(rows):
        out = jnp.where(index == k, row, out)
    return out.astype(BF16)


def encode(mine, other, squares, d):
    def body(mine_ref, other_ref, square_ref, square_other_ref, out_ref):
        x, core = place()
        span = columns(owner(x + d, core))
        value = mine_ref[...] + other_ref[...]
        size = jnp.abs(value)
        largest = jnp.maximum(jnp.max(size, axis=1, keepdims=True), 1e-30) * (1.0 + 2.0 ** -7)
        largest = largest.astype(BF16).astype(F32)
        power = jnp.exp2(size * (SPAN / largest) - LOWEST)
        out_ref[:TOK] = jnp.where(value < 0, -power, power).astype(BF16)
        scale = jnp.broadcast_to(largest, (TOK, 128)).T[:1]
        out_ref[TOK:] = stack_rows([scale] + pieces(square_ref[:1, span] + square_other_ref[:1, span], 3))

    return call(
        body, "encode_sums", (mine, other, *squares), [IN_VMEM] * 4, [((ROWS, CHUNK), BF16)], moved=6 * TOK * CHUNK
    )[0]


def decode(ref):
    scale = jnp.broadcast_to(ref[TOK:TOK + 1].astype(F32), (128, TOK)).T[:, :1]
    power = ref[:TOK].astype(F32)
    size = (jnp.log(jnp.abs(power)) * (1.0 / LN2) + LOWEST) * (scale * (1.0 / SPAN))
    rows = ref[TOK:].astype(F32)
    return jnp.where(power < 0, -size, size), rows[1:2] + rows[2:3] + rows[3:4]


def own_features(mine, other, parts, squares, latent_bias):
    def body(mine_ref, other_ref, *refs):
        part_refs, (square_ref, square_other_ref, bias_ref, out_ref, weight_ref) = refs[:3], refs[3:]
        x, core = place()
        span = columns(owner(x, core))
        preact = mine_ref[...] + other_ref[...] + bias_ref[:, span]
        sources = [square_ref[:1, span] + square_other_ref[:1, span]]
        for ref in part_refs:
            value, square = decode(ref)
            preact += value
            sources.append(square)
        sums = [jnp.zeros((1, CHUNK), F32) for _ in range(LAYERS)]
        for d, square in zip((0, *HOPS), sources):
            layer = lax.rem(x - d + 4, 4) // 2
            sums = [have + jnp.where(layer == k, square, 0.0) for k, have in enumerate(sums)]
        norms = [jnp.sqrt(have + EPSILON) for have in sums]
        weight_ref[...] = jnp.broadcast_to(norms[0] + norms[1], (8, CHUNK))
        out_ref[:TOK] = jnp.maximum(preact, 0.0).astype(BF16)
        out_ref[TOK:] = stack_rows(pieces(norms[0], 3) + pieces(norms[1], 3))

    return call(
        body, "own_features", (mine, other, *parts, *squares, latent_bias), [IN_VMEM] * 8,
        [((ROWS, CHUNK), BF16), ((8, CHUNK), F32)], moved=16 * TOK * CHUNK,
    )


def rebuild_first(chunks, dec_t, own_weights):
    def body(*refs):
        feats, (dec_ref, weight_ref, out_ref) = refs[:FIRST], refs[FIRST:]
        acc = jnp.zeros((TOK, COL), F32)
        for feat, chunk in zip(feats, gathered_owners()):
            acc += dot(feat[:TOK], dec_ref[:, columns(chunk)], ((1,), (1,)))
        penalty = jnp.sum(feats[0][:TOK].astype(F32) * weight_ref[:1], axis=1, keepdims=True)
        out_ref[:, :COL] = acc
        out_ref[:, COL:] = jnp.broadcast_to(penalty, (TOK, WIDE - COL))

    return call(
        body, "rebuild_first", (*chunks, dec_t, own_weights), [IN_VMEM] * (FIRST + 2), [((TOK, WIDE), F32)],
        flops=2 * TOK * COL * CHUNK * FIRST, moved=2 * COL * LAT + 2 * TOK * LAT,
    )[0]


def rebuild_last(chunks, dec_t, partial):
    def body(*refs):
        feats, (dec_ref, partial_ref, out_ref) = refs[:8 - FIRST], refs[8 - FIRST:]
        acc = partial_ref[:, :COL]
        for feat, chunk in zip(feats, gathered_owners()[FIRST:]):
            acc += dot(feat[:TOK], dec_ref[:, columns(chunk)], ((1,), (1,)))
        out_ref[:, :COL] = acc.astype(BF16)
        out_ref[:, COL:] = partial_ref[:, COL:].astype(BF16)

    return call(
        body, "rebuild_last", (*chunks, dec_t, partial), [IN_VMEM] * (10 - FIRST), [((TOK, WIDE), BF16)],
        flops=2 * TOK * COL * CHUNK * (8 - FIRST), moved=2 * COL * LAT + 2 * TOK * LAT,
    )[0]


def error_rows(parts, act_t, output_bias):
    def body(parts_ref, act_ref, bias_ref, out_ref):
        first = lax.axis_index("latent") * 8
        token = lax.broadcasted_iota(jnp.int32, (8, TOK), 1)
        wanted = lax.broadcasted_iota(jnp.int32, (8, TOK), 0) + first
        pick = jnp.where(token == wanted, 1.0, 0.0).astype(BF16)
        act = dot(pick, act_ref[...], ((1,), (1,)))
        total = jnp.sum(parts_ref[...].astype(F32), axis=0)
        errors = total[:, :COL] + bias_ref[...] - act
        loss = 0.5 * jnp.sum(errors * errors, axis=1, keepdims=True) + SPARSITY * total[:, COL:COL + 1]
        lane = lax.broadcasted_iota(jnp.int32, (8, WIDE - COL), 1)
        tail = jnp.zeros((8, WIDE - COL), F32)
        for k, piece in enumerate(pieces(loss, 3)):
            tail = jnp.where(lane == k, piece, tail)
        out_ref[:, :, :COL] = jnp.broadcast_to(errors.astype(BF16)[None], (32, 8, COL))
        out_ref[:, :, COL:] = jnp.broadcast_to(tail.astype(BF16)[None], (32, 8, WIDE - COL))

    return call(
        body, "error_rows", (parts, act_t, output_bias), [IN_VMEM] * 3, [((32, 8, WIDE), BF16)], moved=4 * TOK * WIDE
    )[0]


def own_gradient(mine, other, parts, features, weights, errors):
    def body(mine_ref, other_ref, one_ref, two_ref, three_ref, feat_ref, weight_ref, tail_ref, out_ref):
        total = mine_ref[...] + other_ref[...].astype(F32)
        for ref in (one_ref, two_ref, three_ref):
            total += ref[...].astype(F32)
        total += SPARSITY * weight_ref[:1]
        out_ref[:TOK] = jnp.where(feat_ref[:TOK].astype(F32) > 0, total, 0.0).astype(BF16)
        loss = jnp.sum(jnp.sum(tail_ref[:, COL:].astype(F32), axis=0, keepdims=True), axis=1, keepdims=True)
        out_ref[TOK:] = stack_rows([jnp.broadcast_to(piece, (1, CHUNK)) for piece in pieces(loss, 3)])

    return call(
        body, "own_gradient", (mine, other, *parts, features, weights, errors), [IN_VMEM] * 8,
        [((ROWS, CHUNK), BF16)], moved=16 * TOK * CHUNK,
    )[0]


def store_chunks(values, owners, out_ref, buffer, sems):
    copies = []
    for k, chunk in enumerate(owners):
        buffer[k] = values(k, chunk)
        copies.append(pltpu.make_async_copy(buffer.at[k], out_ref.at[:, columns(chunk)], sems.at[k]))
        copies[-1].start()
    for copy in copies:
        copy.wait()


def decoder_gradient(errors, chunks, dec_t):
    def body(errors_ref, *refs):
        feats, (dec_ref, out_ref, sum_ref, buffer, sems) = refs[:8], refs[8:]
        x, _ = place()
        layer = x // 2
        error = errors_ref[:, :COL].T

        def values(k, chunk):
            feat = feats[k][:TOK]
            rows = feats[k][TOK:].astype(F32)
            norm = jnp.where(layer == 0, rows[0:1] + rows[1:2] + rows[2:3], rows[3:4] + rows[4:5] + rows[5:6])
            totals = jnp.sum(feat.astype(F32), axis=0, keepdims=True)
            scale = SPARSITY * totals / norm
            return (dot(error, feat, ((1,), (0,))) + scale * dec_ref[:, columns(chunk)].astype(F32)).astype(BF16)

        store_chunks(values, gathered_owners(), out_ref, buffer, sems)
        sum_ref[...] = jnp.sum(errors_ref[:, :COL].astype(F32), axis=0, keepdims=True)

    return call(
        body, "decoder_gradient", (errors, *chunks, dec_t), [IN_VMEM] * 10,
        [((COL, LAT), BF16), ((1, COL), F32)], out_specs=[ANYWHERE, IN_VMEM],
        scratch=[pltpu.VMEM((8, COL, CHUNK), BF16), pltpu.SemaphoreType.DMA((8,))],
        flops=2 * TOK * COL * LAT, moved=4 * COL * LAT + 2 * TOK * LAT,
    )


def loss_rows(grads):
    loss = jnp.zeros((1, 128), F32)
    for grad in grads:
        rows = grad[TOK:, :128].astype(F32)
        loss += rows[0:1] + rows[1:2] + rows[2:3]
    return loss * (1.0 / (TOK * LAYERS * D))


def encoder_gradient(act_t, chunks, start, before=None):
    count = len(chunks)

    def body(act_ref, *refs):
        grads, (out_ref, sum_ref, loss_ref, buffer, sems) = refs[:count], refs[-5:]
        owners = gathered_owners()[start:start + count]
        if before is None:
            sum_ref[...] = jnp.zeros((1, LAT), F32)
            loss_ref[...] = loss_rows(grads)
        else:
            sum_ref[...] = refs[count + 1][...]
            loss_ref[...] = refs[count + 2][...] + loss_rows(grads)

        def values(k, chunk):
            grad = grads[k][:TOK]
            sum_ref[:, columns(chunk)] = jnp.sum(grad.astype(F32), axis=0, keepdims=True)
            return dot(act_ref[...], grad, ((1,), (0,))).astype(BF16)

        store_chunks(values, owners, out_ref, buffer, sems)

    extra = () if before is None else tuple(before)
    return pl.pallas_call(
        body,
        in_specs=[IN_VMEM] * (1 + count) + [ANYWHERE, IN_VMEM, IN_VMEM][:len(extra)],
        out_specs=[ANYWHERE, IN_VMEM, IN_VMEM],
        out_shape=[
            jax.ShapeDtypeStruct((COL, LAT), BF16), jax.ShapeDtypeStruct((1, LAT), F32),
            jax.ShapeDtypeStruct((1, 128), F32),
        ],
        scratch_shapes=[pltpu.VMEM((count, COL, CHUNK), BF16), pltpu.SemaphoreType.DMA((count,))],
        input_output_aliases={1 + count: 0} if extra else {},
        compiler_params=pltpu.CompilerParams(vmem_limit_bytes=VMEM_BYTES),
        name="encoder_gradient_last" if extra else "encoder_gradient_first",
        cost_estimate=pl.CostEstimate(
            flops=2 * TOK * COL * CHUNK * count, bytes_accessed=2 * COL * CHUNK * count, transcendentals=0
        ),
    )(act_t, *chunks, *extra)


def gather_chunks(own, work):
    moved = [on_width(own, x_shift(d)) for d in HOPS]
    first = [chunk for part in (own, moved[0]) for chunk in (part, on_width(part, CORE_SWAP))]
    done = work(first)
    return first + [chunk for part in moved[1:] for chunk in (part, on_width(part, CORE_SWAP))], done


def shards(activations, encoder, latent_bias, decoder, output_bias):
    act_t, dec_t = activations.T, decoder.T

    send, act = preact_send(act_t, encoder)
    swapped = {d: on_width(send[d], CORE_SWAP) for d in (*HOPS, 0)}
    keep = own_column(act, encoder, (*HOPS, 0), False, F32, "preact_keep")
    squares = square_sums(dec_t)
    squares = (squares, on_width(squares, CORE_SWAP))
    coded = [on_width(encode(keep[d], swapped[d], squares, d), x_shift(d)) for d in HOPS]
    features, own_weights = own_features(keep[0], swapped[0], coded, squares, latent_bias[None, :])

    feature_chunks, partial = gather_chunks(features, lambda chunks: rebuild_first(chunks, dec_t, own_weights))
    parts = rebuild_last(feature_chunks[FIRST:], dec_t, partial).reshape(32, 8, WIDE)
    parts, bias_row = lax.optimization_barrier((parts, output_bias[None, :]))
    parts = lax.all_to_all(parts, "latent", 0, 0)
    errors = error_rows(parts, act_t, bias_row)
    errors = lax.all_to_all(errors, "latent", 0, 0).reshape(TOK, WIDE)

    far, rest = HOPS[:1], (*HOPS[1:], 0)
    send = own_column(errors, dec_t, far, True, BF16, "back_send_far")
    swapped = {d: on_width(send[d], CORE_SWAP) for d in far}
    keep = own_column(errors, dec_t, far, False, F32, "back_keep_far")
    send = own_column(errors, dec_t, rest, True, BF16, "back_send")
    swapped |= {d: on_width(send[d], CORE_SWAP) for d in rest}
    keep |= own_column(errors, dec_t, rest, False, F32, "back_keep")
    summed = [on_width((keep[d] + swapped[d].astype(F32)).astype(BF16), x_shift(d)) for d in HOPS]
    decoder_grad, output_grad = decoder_gradient(errors, feature_chunks, dec_t)
    decoder_grad, output_grad, features = lax.optimization_barrier((decoder_grad, output_grad[0], features))
    grad_pre = own_gradient(keep[0], swapped[0], summed, features, own_weights, errors)
    grad_chunks, first = gather_chunks(grad_pre, lambda chunks: encoder_gradient(act_t, chunks, 0))
    encoder_grad, latent_grad, loss_value = encoder_gradient(act_t, grad_chunks[FIRST:], FIRST, first)
    return (loss_value[0, 0], encoder_grad, latent_grad[0], decoder_grad.T, output_grad)


def solution(mesh):
    placed = (P(None, "width"), P("width", "latent"), P("latent"), P("latent", "width"), P("width"))
    return jax.shard_map(
        shards,
        mesh=mesh,
        in_specs=placed,
        out_specs=(P(), P("width", "latent"), P("latent"), P("latent", "width"), P("width")),
        check_vma=False,
    )
```

time: 340 us -> 102 us (0.30)
  waiting for transfers between devices: 191 us -> 14.1 us
  blocking collectives: 103 us -> 38.4 us
  starting transfers between devices: 0.12 us -> 34.5 us
  between operations: 16.9 us -> 1.01 us
  matrix products: 15.4 us -> 0 us
  Pallas kernels: 0 us -> 13.2 us
  other arithmetic: 10.3 us -> 0.69 us
    psum x3 -> x0, waiting for transfers between devices: 191 us -> none  [the longest x1 118 us: shards(): errors = lax.psum(partial_rebuild, 'latent') + output_bias - act_float]
    psum x2 -> x0, blocking collectives: 103 us -> none  [the longest x1 79.1 us: shards(): lax.psum(local_loss, ('width', 'latent')) / (token_count * LAYERS * D)]
    all_to_all x0 -> x2, blocking collectives: none -> 38.4 us  [the longest x1 22.6 us: shards(): parts = lax.all_to_all(parts, 'latent', 0, 0)]
    ppermute x0 -> x29, starting transfers between devices: none -> 34.5 us  [on_width(): return lax.ppermute(value, 'width', pairs)]
    dot_general x5 -> x0, matrix products: 15.4 us -> none  [the longest x1 4.19 us: shards(): lax.dot_general(decoder, error_half, SECOND_SECOND, preferred_element_typ...]
    ppermute x0 -> x29, waiting for transfers between devices: none -> 14.1 us  [on_width(): return lax.ppermute(value, 'width', pairs)]
    pallas_call x0 -> x18, Pallas kernels: none -> 13.2 us  [the longest x16 9.84 us: call(): pl.pallas_call(body, in_specs=in_specs, out_specs=out_specs or [IN_VMEM]...]
    reduce_sum x4 -> x0, other arithmetic: 7.43 us -> none  [the longest x1 2.93 us: shards(): latent_grad = jnp.sum(grad_pre.astype(jnp.float32), axis=1)]
  transfers between devices with their start and end apart: 3 -> 29, of which waited for: 2 -> 9; matrix products, arithmetic and copies ran while one was open for 2% -> 1% of each run, Pallas kernels for 0% -> 6%
where the time goes in v2:
time: 102 us
  blocking collectives  38.4 us (38%)
  starting transfers between devices  34.5 us (34%)
  waiting for transfers between devices  14.1 us (14%)
  Pallas kernels  13.2 us (13%)
    ppermute x29, starting transfers between devices, on_width(): return lax.ppermute(value, 'width', pairs)  34.5 us
    all_to_all x1, blocking collectives, shards(): parts = lax.all_to_all(parts, 'latent', 0, 0)  22.6 us
    all_to_all x1, blocking collectives, shards(): errors = lax.all_to_all(errors, 'latent', 0, 0).reshape(TOK, WIDE)  15.8 us
    ppermute x29, waiting for transfers between devices, on_width(): return lax.ppermute(value, 'width', pairs)  14.1 us
    pallas_call x16, Pallas kernels, call(): pl.pallas_call(body, in_specs=in_specs, out_specs=out_specs or [IN_VMEM]...  9.84 us
    pallas_call x2, Pallas kernels, encoder_gradient(): pl.pallas_call(body, in_specs=[IN_VMEM] * (1 + count) + [ANYWHERE, IN_VME...  3.36 us
  transfers between devices with their start and end apart: 29, of which 9 were waited for; matrix products, arithmetic and copies ran while one was open for 1% of the time, Pallas kernels for 6%

profile of v2, /device:TPU:1, one launch (start us, length us, event | category | flops | bytes accessed | tf_op | source)
XLA Modules:
  0.0 101.8 jit_solution(2033639397134779964)
XLA Ops:
  0.7 2.7 %preact_send.1 = (f32[256,256]{1,0:T(8,128)S(1)}, f32[256,256]{1,0:T(8,128)S(1)}, f32[256,256]{1,0:T(8,128)S(1)}, f32[256,256]{1,0:T(8,128)S(1)}, bf16[256,576]{1,0:T(8,128)(2,1)S(1)}) custom-call(bf16[576,256]{1,0:T(8,128)(2,1)} %bitcast.23, bf16[576,2048]{1,0:T(8,128)(2,1)} %right_ref.1), custom_call_target="tpu_custom_call" | custom-call | flops 301989888 | bytes 2228224 | tf_op jit(solution)/shard_map/preact_send/pallas_call | solution.py:47
  3.4 3.3 %collective-permute-start.1 = (f32[256,256]{1,0:T(8,128)S(1)}, f32[256,256]{1,0:T(8,128)S(1)}, u32[]{:S(2)}, u32[]{:S(2)}) collective-permute-start(f32[256,256]{1,0:T(8,128)S(1)} %get-tuple-element.39), channel_id=1, source_target_pairs={{0,32},{32,0},{64,96},{96,64},{128,160},{160,128},{192,224},{224,1... | collective-permute-start | bytes 786440 | tf_op jit(solution)/shard_map/ppermute | solution.py:35
  6.7 0.1 collective-permute-start.4
  6.8 0.4 collective-permute-start.6
  7.2 0.1 collective-permute-start
  7.3 0.1 square_sums.1.square_ref.refs_3_
  7.4 0.5 collective-permute-start.2
  7.9 0.6 preact_keep.1
  8.5 0.0 copy-start.4
  8.5 0.5 collective-permute-done.2.square_other_ref.refs_4_
  9.1 0.0 collective-permute-done.1.other_ref
  9.1 0.2 encode_sums.3
  9.3 1.1 %collective-permute-start.3 = (bf16[272,256]{1,0:T(8,128)(2,1)S(1)}, bf16[272,256]{1,0:T(8,128)(2,1)S(1)}, u32[]{:S(2)}, u32[]{:S(2)}) collective-permute-start(bf16[272,256]{1,0:T(8,128)(2,1)S(1)} %encode_sums.3), channel_id=1, source_target_pairs={{0,128},{32,160},{64,192},{96,224},{128,0},{160,32},{192,64},{224,... | collective-permute-start | bytes 417800 | tf_op jit(solution)/shard_map/ppermute | solution.py:35
  10.4 0.2 encode_sums.4
  10.6 0.4 collective-permute-start.5
  11.0 0.0 collective-permute-done.6.other_ref
  11.0 0.2 encode_sums.5
  11.2 2.4 %collective-permute-start.7 = (bf16[272,256]{1,0:T(8,128)(2,1)S(1)}, bf16[272,256]{1,0:T(8,128)(2,1)S(1)}, u32[]{:S(2)}, u32[]{:S(2)}) collective-permute-start(bf16[272,256]{1,0:T(8,128)(2,1)S(1)} %encode_sums.5), channel_id=1, source_target_pairs={{0,192},{32,224},{64,0},{96,32},{128,64},{160,96},{192,128},{224,1... | collective-permute-start | bytes 417800 | tf_op jit(solution)/shard_map/ppermute | solution.py:35
  13.6 0.0 collective-permute-done.other_ref
  13.6 2.2 %collective-permute-done.3.refs_0_ = bf16[272,256]{1,0:T(8,128)(2,1)S(1)} collective-permute-done((bf16[272,256]{1,0:T(8,128)(2,1)S(1)}, bf16[272,256]{1,0:T(8,128)(2,1)S(1)}, u32[]{:S(2)}, u32[]{:S(2)}) %collective-permute-start.3) | collective-permute-done | bytes 139296 | tf_op jit(solution)/shard_map/ppermute | solution.py:35
  15.7 3.7 %collective-permute-done.5.refs_1_ = bf16[272,256]{1,0:T(8,128)(2,1)S(1)} collective-permute-done((bf16[272,256]{1,0:T(8,128)(2,1)S(1)}, bf16[272,256]{1,0:T(8,128)(2,1)S(1)}, u32[]{:S(2)}, u32[]{:S(2)}) %collective-permute-start.5) | collective-permute-done | bytes 139296 | tf_op jit(solution)/shard_map/ppermute | solution.py:35
  19.4 0.5 own_features.1
  20.0 1.1 %collective-permute-start.13 = (bf16[272,256]{1,0:T(8,128)(2,1)S(1)}, bf16[272,256]{1,0:T(8,128)(2,1)S(1)}, u32[]{:S(2)}, u32[]{:S(2)}) collective-permute-start(bf16[272,256]{1,0:T(8,128)(2,1)S(1)} %get-tuple-element.56.refs_0_.feat_ref), channel_id=1, source_target_pairs={{0,128},{32,160},{64,192},{96,224},{128,0},{160,32},{192,64},{224,... | collective-permute-start | bytes 417800 | tf_op jit(solution)/shard_map/ppermute | solution.py:35
  21.1 0.3 collective-permute-start.10
  21.3 1.2 %collective-permute-start.8 = (bf16[272,256]{1,0:T(8,128)(2,1)S(1)}, bf16[272,256]{1,0:T(8,128)(2,1)S(1)}, u32[]{:S(2)}, u32[]{:S(2)}) collective-permute-start(bf16[272,256]{1,0:T(8,128)(2,1)S(1)} %get-tuple-element.56.refs_0_.feat_ref), channel_id=1, source_target_pairs={{0,64},{32,96},{64,128},{96,160},{128,192},{160,224},{192,0},{224,... | collective-permute-start | bytes 417800 | tf_op jit(solution)/shard_map/ppermute | solution.py:35
  22.5 1.3 %collective-permute-start.12 = (bf16[272,256]{1,0:T(8,128)(2,1)S(1)}, bf16[272,256]{1,0:T(8,128)(2,1)S(1)}, u32[]{:S(2)}, u32[]{:S(2)}) collective-permute-start(bf16[272,256]{1,0:T(8,128)(2,1)S(1)} %get-tuple-element.56.refs_0_.feat_ref), channel_id=1, source_target_pairs={{0,32},{32,0},{64,96},{96,64},{128,160},{160,128},{192,224},{224,1... | collective-permute-start | bytes 417800 | tf_op jit(solution)/shard_map/ppermute | solution.py:35
  23.9 2.4 %collective-permute-done.13.refs_2_ = bf16[272,256]{1,0:T(8,128)(2,1)S(1)} collective-permute-done((bf16[272,256]{1,0:T(8,128)(2,1)S(1)}, bf16[272,256]{1,0:T(8,128)(2,1)S(1)}, u32[]{:S(2)}, u32[]{:S(2)}) %collective-permute-start.13) | collective-permute-done | bytes 139296 | tf_op jit(solution)/shard_map/ppermute | solution.py:35
  26.3 2.3 %collective-permute-start.14 = (bf16[272,256]{1,0:T(8,128)(2,1)S(1)}, bf16[272,256]{1,0:T(8,128)(2,1)S(1)}, u32[]{:S(2)}, u32[]{:S(2)}) collective-permute-start(bf16[272,256]{1,0:T(8,128)(2,1)S(1)} %collective-permute-done.13.refs_2_), channel_id=1, source_target_pairs={{0,32},{32,0},{64,96},{96,64},{128,160},{160,128},{192,224},{224,1... | collective-permute-start | bytes 417800 | tf_op jit(solution)/shard_map/ppermute | solution.py:35
  28.6 0.1 collective-permute-start.11
  28.6 1.0 collective-permute-done.8.refs_0_.refs_4_
  29.6 1.0 collective-permute-start.9
  30.6 0.0 collective-permute-done.12.refs_1_
  30.6 0.6 rebuild_first.1.refs_5_
  31.2 0.0 copy-start.2
  31.3 0.4 collective-permute-done.9.refs_1_.refs_5_
  31.6 0.6 rebuild_last.1
  32.2 22.6 %all_to_all.10.parts_ref = bf16[32,8,640]{2,1,0:T(8,128)(2,1)S(1)} all-to-all(bf16[32,8,640]{2,1,0:T(8,128)(2,1)S(1)} %bitcast.27), channel_id=1, replica_groups=mesh['width'=8,'latent'=32] {'latent'}, dimensions={0} | all-to-all | bytes 655360 | tf_op jit(solution)/shard_map/all_to_all | solution.py:376
  54.8 0.4 error_rows.1
  55.2 15.8 %all_to_all.11 = bf16[32,8,640]{2,1,0:T(8,128)(2,1)S(1)} all-to-all(bf16[32,8,640]{2,1,0:T(8,128)(2,1)S(1)} %error_rows.1), channel_id=1, replica_groups=mesh['width'=8,'latent'=32] {'latent'}, dimensions={0} | all-to-all | bytes 655360 | tf_op jit(solution)/shard_map/all_to_all | solution.py:378
  71.0 0.3 back_send_far.1
  71.3 3.8 %collective-permute-start.16 = (bf16[256,256]{1,0:T(8,128)(2,1)S(1)}, bf16[256,256]{1,0:T(8,128)(2,1)S(1)}, u32[]{:S(2)}, u32[]{:S(2)}) collective-permute-start(bf16[256,256]{1,0:T(8,128)(2,1)S(1)} %back_send_far.1), channel_id=1, source_target_pairs={{0,32},{32,0},{64,96},{96,64},{128,160},{160,128},{192,224},{224,1... | collective-permute-start | bytes 393224 | tf_op jit(solution)/shard_map/ppermute | solution.py:35
  75.0 0.5 back_send.1
  75.5 0.1 collective-permute-start.15
  75.6 0.5 collective-permute-start.18
  76.1 0.1 collective-permute-start.20
  76.2 0.3 back_keep_far.1
  76.5 0.5 back_keep.1
  77.1 1.8 %collective-permute-start.17 = (bf16[256,256]{1,0:T(8,128)(2,1)S(1)}, bf16[256,256]{1,0:T(8,128)(2,1)S(1)}, u32[]{:S(2)}, u32[]{:S(2)}) collective-permute-start(bf16[256,256]{1,0:T(8,128)(2,1)S(1)} %add_convert_fusion.2), channel_id=1, source_target_pairs={{0,128},{32,160},{64,192},{96,224},{128,0},{160,32},{192,64},{224,... | collective-permute-start | bytes 393224 | tf_op jit(solution)/shard_map/ppermute | solution.py:35
  78.9 0.7 collective-permute-start.19
  79.6 2.1 %collective-permute-start.21 = (bf16[256,256]{1,0:T(8,128)(2,1)S(1)}, bf16[256,256]{1,0:T(8,128)(2,1)S(1)}, u32[]{:S(2)}, u32[]{:S(2)}) collective-permute-start(bf16[256,256]{1,0:T(8,128)(2,1)S(1)} %add_convert_fusion), channel_id=1, source_target_pairs={{0,192},{32,224},{64,0},{96,32},{128,64},{160,96},{192,128},{224,1... | collective-permute-start | bytes 393224 | tf_op jit(solution)/shard_map/ppermute | solution.py:35
  81.7 1.9 %decoder_gradient.1 = (bf16[576,2048]{1,0:T(8,128)(2,1)}, f32[1,576]{1,0:T(1,128)S(1)}) custom-call(bf16[256,640]{1,0:T(8,128)(2,1)S(1)} %bitcast.21, bf16[272,256]{1,0:T(8,128)(2,1)S(1)} %get-tuple-element.56.refs_0_.feat_ref, bf16[272,256]{1,0:T(8,128)(2,1)S(1)} %collective-permute-done.12.refs_1_, bf16[272,256]{1,0:T(8,128)(2,1)S(1)} %collective-permute-done.13.refs_2_, ...), custom_call_target="tpu_custom_call" | custom-call | flops 603979776 | bytes 5767168 | tf_op jit(solution)/shard_map/decoder_gradient/pallas_call | solution.py:47
  83.7 0.6 reduce
  84.3 2.3 %collective-permute-done.19.two_ref = bf16[256,256]{1,0:T(8,128)(2,1)S(1)} collective-permute-done((bf16[256,256]{1,0:T(8,128)(2,1)S(1)}, bf16[256,256]{1,0:T(8,128)(2,1)S(1)}, u32[]{:S(2)}, u32[]{:S(2)}) %collective-permute-start.19) | collective-permute-done | bytes 131104 | tf_op jit(solution)/shard_map/ppermute | solution.py:35
  86.6 0.3 own_gradient.1.refs_0_
  86.9 1.8 %collective-permute-start.27 = (bf16[272,256]{1,0:T(8,128)(2,1)S(1)}, bf16[272,256]{1,0:T(8,128)(2,1)S(1)}, u32[]{:S(2)}, u32[]{:S(2)}) collective-permute-start(bf16[272,256]{1,0:T(8,128)(2,1)S(1)} %own_gradient.1.refs_0_), channel_id=1, source_target_pairs={{0,128},{32,160},{64,192},{96,224},{128,0},{160,32},{192,64},{224,... | collective-permute-start | bytes 417800 | tf_op jit(solution)/shard_map/ppermute | solution.py:35
  88.7 1.7 %collective-permute-start.24 = (bf16[272,256]{1,0:T(8,128)(2,1)S(1)}, bf16[272,256]{1,0:T(8,128)(2,1)S(1)}, u32[]{:S(2)}, u32[]{:S(2)}) collective-permute-start(bf16[272,256]{1,0:T(8,128)(2,1)S(1)} %own_gradient.1.refs_0_), channel_id=1, source_target_pairs={{0,192},{32,224},{64,0},{96,32},{128,64},{160,96},{192,128},{224,1... | collective-permute-start | bytes 417800 | tf_op jit(solution)/shard_map/ppermute | solution.py:35
  90.5 1.2 %collective-permute-start.26 = (bf16[272,256]{1,0:T(8,128)(2,1)S(1)}, bf16[272,256]{1,0:T(8,128)(2,1)S(1)}, u32[]{:S(2)}, u32[]{:S(2)}) collective-permute-start(bf16[272,256]{1,0:T(8,128)(2,1)S(1)} %own_gradient.1.refs_0_), channel_id=1, source_target_pairs={{0,32},{32,0},{64,96},{96,64},{128,160},{160,128},{192,224},{224,1... | collective-permute-start | bytes 417800 | tf_op jit(solution)/shard_map/ppermute | solution.py:35
  91.6 1.3 %collective-permute-done.27.refs_2_ = bf16[272,256]{1,0:T(8,128)(2,1)S(1)} collective-permute-done((bf16[272,256]{1,0:T(8,128)(2,1)S(1)}, bf16[272,256]{1,0:T(8,128)(2,1)S(1)}, u32[]{:S(2)}, u32[]{:S(2)}) %collective-permute-start.27) | collective-permute-done | bytes 139296 | tf_op jit(solution)/shard_map/ppermute | solution.py:35
  93.0 2.8 %collective-permute-start.28 = (bf16[272,256]{1,0:T(8,128)(2,1)S(1)}, bf16[272,256]{1,0:T(8,128)(2,1)S(1)}, u32[]{:S(2)}, u32[]{:S(2)}) collective-permute-start(bf16[272,256]{1,0:T(8,128)(2,1)S(1)} %collective-permute-done.27.refs_2_), channel_id=1, source_target_pairs={{0,32},{32,0},{64,96},{96,64},{128,160},{160,128},{192,224},{224,1... | collective-permute-start | bytes 417800 | tf_op jit(solution)/shard_map/ppermute | solution.py:35
  95.8 0.8 collective-permute-start.25
  96.6 0.2 collective-permute-done.22.refs_0_
  96.8 1.5 %collective-permute-start.23 = (bf16[272,256]{1,0:T(8,128)(2,1)S(1)}, bf16[272,256]{1,0:T(8,128)(2,1)S(1)}, u32[]{:S(2)}, u32[]{:S(2)}) collective-permute-start(bf16[272,256]{1,0:T(8,128)(2,1)S(1)} %collective-permute-done.22.refs_0_), channel_id=1, source_target_pairs={{0,32},{32,0},{64,96},{96,64},{128,160},{160,128},{192,224},{224,1... | collective-permute-start | bytes 417800 | tf_op jit(solution)/shard_map/ppermute | solution.py:35
  98.3 1.4 %encoder_gradient_first.1 = (bf16[576,2048]{1,0:T(8,128)(2,1)}, f32[1,2048]{1,0:T(1,128)S(1)}, f32[1,128]{1,0:T(1,128)S(1)}) custom-call(bf16[576,256]{1,0:T(8,128)(2,1)S(1)} %bitcast.25, bf16[272,256]{1,0:T(8,128)(2,1)S(1)} %own_gradient.1.refs_0_, bf16[272,256]{1,0:T(8,128)(2,1)S(1)} %collective-permute-done.26.refs_1_, ...), custom_call_target="tpu_custom_call" | custom-call | flops 301989888 | bytes 1179648 | tf_op jit(solution)/shard_map/encoder_gradient_first/pallas_call | solution.py:337
  99.7 2.0 %encoder_gradient_last.1 = (bf16[576,2048]{1,0:T(8,128)(2,1)}, f32[1,2048]{1,0:T(1,128)}, f32[1,128]{1,0:T(1,128)}) custom-call(bf16[576,256]{1,0:T(8,128)(2,1)S(1)} %bitcast.26, bf16[272,256]{1,0:T(8,128)(2,1)S(1)} %collective-permute-done.22.refs_0_, bf16[272,256]{1,0:T(8,128)(2,1)S(1)} %collective-permute-done.23.refs_1_, ...), custom_call_target="tpu_custom_call", output_to_operand_aliasing={{0}: (5, {})} | custom-call | flops 301989888 | bytes 1179648 | tf_op jit(solution)/shard_map/encoder_gradient_last/pallas_call | solution.py:337
  (29 shorter events, 0.1 us)
Async XLA Ops:
  0.6 6.7 %copy-start = (bf16[2048,576]{0,1:T(8,128)(2,1)S(1)}, bf16[2048,576]{0,1:T(8,128)(2,1)}, u32[]{:S(2)}) copy-start(bf16[2048,576]{0,1:T(8,128)(2,1)} %param.8) | copy-start | bytes 7077892
  0.6 7.3 %copy-start.1 = (bf16[576,2048]{1,0:T(8,128)(2,1)S(1)}, bf16[576,2048]{1,0:T(8,128)(2,1)}, u32[]{:S(2)}) copy-start(bf16[576,2048]{1,0:T(8,128)(2,1)} %right_ref.1) | copy-start | bytes 7077892
  3.4 5.7 %collective-permute-start.1 = (f32[256,256]{1,0:T(8,128)S(1)}, f32[256,256]{1,0:T(8,128)S(1)}, u32[]{:S(2)}, u32[]{:S(2)}) collective-permute-start(f32[256,256]{1,0:T(8,128)S(1)} %get-tuple-element.39), channel_id=1, source_target_pairs={{0,32},{32,0},{64,96},{96,64},{128,160},{160,128},{192,224},{224,1... | collective-permute-start | bytes 786440 | tf_op jit(solution)/shard_map/ppermute | solution.py:35
  6.7 3.7 %collective-permute-start.4 = (f32[256,256]{1,0:T(8,128)S(1)}, f32[256,256]{1,0:T(8,128)S(1)}, u32[]{:S(2)}, u32[]{:S(2)}) collective-permute-start(f32[256,256]{1,0:T(8,128)S(1)} %get-tuple-element.41), channel_id=1, source_target_pairs={{0,32},{32,0},{64,96},{96,64},{128,160},{160,128},{192,224},{224,1... | collective-permute-start | bytes 786440 | tf_op jit(solution)/shard_map/ppermute | solution.py:35
  6.8 4.2 %collective-permute-start.6 = (f32[256,256]{1,0:T(8,128)S(1)}, f32[256,256]{1,0:T(8,128)S(1)}, u32[]{:S(2)}, u32[]{:S(2)}) collective-permute-start(f32[256,256]{1,0:T(8,128)S(1)} %get-tuple-element.43), channel_id=1, source_target_pairs={{0,32},{32,0},{64,96},{96,64},{128,160},{160,128},{192,224},{224,1... | collective-permute-start | bytes 786440 | tf_op jit(solution)/shard_map/ppermute | solution.py:35
  7.2 6.4 %collective-permute-start = (f32[256,256]{1,0:T(8,128)S(1)}, f32[256,256]{1,0:T(8,128)S(1)}, u32[]{:S(2)}, u32[]{:S(2)}) collective-permute-start(f32[256,256]{1,0:T(8,128)S(1)} %get-tuple-element.37), channel_id=1, source_target_pairs={{0,32},{32,0},{64,96},{96,64},{128,160},{160,128},{192,224},{224,1... | collective-permute-start | bytes 786440 | tf_op jit(solution)/shard_map/ppermute | solution.py:35
  7.4 1.6 %collective-permute-start.2 = (f32[8,2048]{1,0:T(8,128)S(1)}, f32[8,2048]{1,0:T(8,128)S(1)}, u32[]{:S(2)}, u32[]{:S(2)}) collective-permute-start(f32[8,2048]{1,0:T(8,128)S(1)} %square_sums.1.square_ref.refs_3_), channel_id=1, source_target_pairs={{0,32},{32,0},{64,96},{96,64},{128,160},{160,128},{192,224},{224,1... | collective-permute-start | bytes 196616 | tf_op jit(solution)/shard_map/ppermute | solution.py:35
  7.9 11.5 %copy-start.3 = (f32[2048]{0:T(1024)S(1)}, f32[2048]{0:T(1024)}, u32[]{:S(2)}) copy-start(f32[2048]{0:T(1024)} %param.7) | copy-start | bytes 24580
  8.5 22.1 %copy-start.4 = (f32[576]{0:T(1024)S(1)}, f32[576]{0:T(1024)}, u32[]{:S(2)}) copy-start(f32[576]{0:T(1024)} %param.9) | copy-start | bytes 6916
  9.3 6.5 %collective-permute-start.3 = (bf16[272,256]{1,0:T(8,128)(2,1)S(1)}, bf16[272,256]{1,0:T(8,128)(2,1)S(1)}, u32[]{:S(2)}, u32[]{:S(2)}) collective-permute-start(bf16[272,256]{1,0:T(8,128)(2,1)S(1)} %encode_sums.3), channel_id=1, source_target_pairs={{0,128},{32,160},{64,192},{96,224},{128,0},{160,32},{192,64},{224,... | collective-permute-start | bytes 417800 | tf_op jit(solution)/shard_map/ppermute | solution.py:35
  10.6 8.9 %collective-permute-start.5 = (bf16[272,256]{1,0:T(8,128)(2,1)S(1)}, bf16[272,256]{1,0:T(8,128)(2,1)S(1)}, u32[]{:S(2)}, u32[]{:S(2)}) collective-permute-start(bf16[272,256]{1,0:T(8,128)(2,1)S(1)} %encode_sums.4), channel_id=1, source_target_pairs={{0,64},{32,96},{64,128},{96,160},{128,192},{160,224},{192,0},{224,... | collective-permute-start | bytes 417800 | tf_op jit(solution)/shard_map/ppermute | solution.py:35
  11.2 8.3 %collective-permute-start.7 = (bf16[272,256]{1,0:T(8,128)(2,1)S(1)}, bf16[272,256]{1,0:T(8,128)(2,1)S(1)}, u32[]{:S(2)}, u32[]{:S(2)}) collective-permute-start(bf16[272,256]{1,0:T(8,128)(2,1)S(1)} %encode_sums.5), channel_id=1, source_target_pairs={{0,192},{32,224},{64,0},{96,32},{128,64},{160,96},{192,128},{224,1... | collective-permute-start | bytes 417800 | tf_op jit(solution)/shard_map/ppermute | solution.py:35
  20.0 6.3 %collective-permute-start.13 = (bf16[272,256]{1,0:T(8,128)(2,1)S(1)}, bf16[272,256]{1,0:T(8,128)(2,1)S(1)}, u32[]{:S(2)}, u32[]{:S(2)}) collective-permute-start(bf16[272,256]{1,0:T(8,128)(2,1)S(1)} %get-tuple-element.56.refs_0_.feat_ref), channel_id=1, source_target_pairs={{0,128},{32,160},{64,192},{96,224},{128,0},{160,32},{192,64},{224,... | collective-permute-start | bytes 417800 | tf_op jit(solution)/shard_map/ppermute | solution.py:35
  21.1 7.5 %collective-permute-start.10 = (bf16[272,256]{1,0:T(8,128)(2,1)S(1)}, bf16[272,256]{1,0:T(8,128)(2,1)S(1)}, u32[]{:S(2)}, u32[]{:S(2)}) collective-permute-start(bf16[272,256]{1,0:T(8,128)(2,1)S(1)} %get-tuple-element.56.refs_0_.feat_ref), channel_id=1, source_target_pairs={{0,192},{32,224},{64,0},{96,32},{128,64},{160,96},{192,128},{224,1... | collective-permute-start | bytes 417800 | tf_op jit(solution)/shard_map/ppermute | solution.py:35
  21.3 8.3 %collective-permute-start.8 = (bf16[272,256]{1,0:T(8,128)(2,1)S(1)}, bf16[272,256]{1,0:T(8,128)(2,1)S(1)}, u32[]{:S(2)}, u32[]{:S(2)}) collective-permute-start(bf16[272,256]{1,0:T(8,128)(2,1)S(1)} %get-tuple-element.56.refs_0_.feat_ref), channel_id=1, source_target_pairs={{0,64},{32,96},{64,128},{96,160},{128,192},{160,224},{192,0},{224,... | collective-permute-start | bytes 417800 | tf_op jit(solution)/shard_map/ppermute | solution.py:35
  22.5 8.1 %collective-permute-start.12 = (bf16[272,256]{1,0:T(8,128)(2,1)S(1)}, bf16[272,256]{1,0:T(8,128)(2,1)S(1)}, u32[]{:S(2)}, u32[]{:S(2)}) collective-permute-start(bf16[272,256]{1,0:T(8,128)(2,1)S(1)} %get-tuple-element.56.refs_0_.feat_ref), channel_id=1, source_target_pairs={{0,32},{32,0},{64,96},{96,64},{128,160},{160,128},{192,224},{224,1... | collective-permute-start | bytes 417800 | tf_op jit(solution)/shard_map/ppermute | solution.py:35
  26.3 4.3 %collective-permute-start.14 = (bf16[272,256]{1,0:T(8,128)(2,1)S(1)}, bf16[272,256]{1,0:T(8,128)(2,1)S(1)}, u32[]{:S(2)}, u32[]{:S(2)}) collective-permute-start(bf16[272,256]{1,0:T(8,128)(2,1)S(1)} %collective-permute-done.13.refs_2_), channel_id=1, source_target_pairs={{0,32},{32,0},{64,96},{96,64},{128,160},{160,128},{192,224},{224,1... | collective-permute-start | bytes 417800 | tf_op jit(solution)/shard_map/ppermute | solution.py:35
  28.6 2.7 %collective-permute-start.11 = (bf16[272,256]{1,0:T(8,128)(2,1)S(1)}, bf16[272,256]{1,0:T(8,128)(2,1)S(1)}, u32[]{:S(2)}, u32[]{:S(2)}) collective-permute-start(bf16[272,256]{1,0:T(8,128)(2,1)S(1)} %collective-permute-done.10.refs_2_.refs_6_), channel_id=1, source_target_pairs={{0,32},{32,0},{64,96},{96,64},{128,160},{160,128},{192,224},{224,1... | collective-permute-start | bytes 417800 | tf_op jit(solution)/shard_map/ppermute | solution.py:35
  29.6 2.0 %collective-permute-start.9 = (bf16[272,256]{1,0:T(8,128)(2,1)S(1)}, bf16[272,256]{1,0:T(8,128)(2,1)S(1)}, u32[]{:S(2)}, u32[]{:S(2)}) collective-permute-start(bf16[272,256]{1,0:T(8,128)(2,1)S(1)} %collective-permute-done.8.refs_0_.refs_4_), channel_id=1, source_target_pairs={{0,32},{32,0},{64,96},{96,64},{128,160},{160,128},{192,224},{224,1... | collective-permute-start | bytes 417800 | tf_op jit(solution)/shard_map/ppermute | solution.py:35
  31.2 23.5 %copy-start.2 = (bf16[256,576]{0,1:T(8,128)(2,1)S(1)}, bf16[256,576]{0,1:T(8,128)(2,1)}, u32[]{:S(2)}) copy-start(bf16[256,576]{0,1:T(8,128)(2,1)} %param.5) | copy-start | bytes 884740
  71.3 5.7 %collective-permute-start.16 = (bf16[256,256]{1,0:T(8,128)(2,1)S(1)}, bf16[256,256]{1,0:T(8,128)(2,1)S(1)}, u32[]{:S(2)}, u32[]{:S(2)}) collective-permute-start(bf16[256,256]{1,0:T(8,128)(2,1)S(1)} %back_send_far.1), channel_id=1, source_target_pairs={{0,32},{32,0},{64,96},{96,64},{128,160},{160,128},{192,224},{224,1... | collective-permute-start | bytes 393224 | tf_op jit(solution)/shard_map/ppermute | solution.py:35
  75.5 8.8 %collective-permute-start.15 = (bf16[256,256]{1,0:T(8,128)(2,1)S(1)}, bf16[256,256]{1,0:T(8,128)(2,1)S(1)}, u32[]{:S(2)}, u32[]{:S(2)}) collective-permute-start(bf16[256,256]{1,0:T(8,128)(2,1)S(1)} %get-tuple-element.49), channel_id=1, source_target_pairs={{0,32},{32,0},{64,96},{96,64},{128,160},{160,128},{192,224},{224,1... | collective-permute-start | bytes 393224 | tf_op jit(solution)/shard_map/ppermute | solution.py:35
  75.6 3.2 %collective-permute-start.18 = (bf16[256,256]{1,0:T(8,128)(2,1)S(1)}, bf16[256,256]{1,0:T(8,128)(2,1)S(1)}, u32[]{:S(2)}, u32[]{:S(2)}) collective-permute-start(bf16[256,256]{1,0:T(8,128)(2,1)S(1)} %get-tuple-element.51), channel_id=1, source_target_pairs={{0,32},{32,0},{64,96},{96,64},{128,160},{160,128},{192,224},{224,1... | collective-permute-start | bytes 393224 | tf_op jit(solution)/shard_map/ppermute | solution.py:35
  76.1 3.5 %collective-permute-start.20 = (bf16[256,256]{1,0:T(8,128)(2,1)S(1)}, bf16[256,256]{1,0:T(8,128)(2,1)S(1)}, u32[]{:S(2)}, u32[]{:S(2)}) collective-permute-start(bf16[256,256]{1,0:T(8,128)(2,1)S(1)} %get-tuple-element.53), channel_id=1, source_target_pairs={{0,32},{32,0},{64,96},{96,64},{128,160},{160,128},{192,224},{224,1... | collective-permute-start | bytes 393224 | tf_op jit(solution)/shard_map/ppermute | solution.py:35
  77.1 7.2 %collective-permute-start.17 = (bf16[256,256]{1,0:T(8,128)(2,1)S(1)}, bf16[256,256]{1,0:T(8,128)(2,1)S(1)}, u32[]{:S(2)}, u32[]{:S(2)}) collective-permute-start(bf16[256,256]{1,0:T(8,128)(2,1)S(1)} %add_convert_fusion.2), channel_id=1, source_target_pairs={{0,128},{32,160},{64,192},{96,224},{128,0},{160,32},{192,64},{224,... | collective-permute-start | bytes 393224 | tf_op jit(solution)/shard_map/ppermute | solution.py:35
  78.9 7.8 %collective-permute-start.19 = (bf16[256,256]{1,0:T(8,128)(2,1)S(1)}, bf16[256,256]{1,0:T(8,128)(2,1)S(1)}, u32[]{:S(2)}, u32[]{:S(2)}) collective-permute-start(bf16[256,256]{1,0:T(8,128)(2,1)S(1)} %add_convert_fusion.1), channel_id=1, source_target_pairs={{0,64},{32,96},{64,128},{96,160},{128,192},{160,224},{192,0},{224,... | collective-permute-start | bytes 393224 | tf_op jit(solution)/shard_map/ppermute | solution.py:35
  79.6 7.0 %collective-permute-start.21 = (bf16[256,256]{1,0:T(8,128)(2,1)S(1)}, bf16[256,256]{1,0:T(8,128)(2,1)S(1)}, u32[]{:S(2)}, u32[]{:S(2)}) collective-permute-start(bf16[256,256]{1,0:T(8,128)(2,1)S(1)} %add_convert_fusion), channel_id=1, source_target_pairs={{0,192},{32,224},{64,0},{96,32},{128,64},{160,96},{192,128},{224,1... | collective-permute-start | bytes 393224 | tf_op jit(solution)/shard_map/ppermute | solution.py:35
  86.9 6.1 %collective-permute-start.27 = (bf16[272,256]{1,0:T(8,128)(2,1)S(1)}, bf16[272,256]{1,0:T(8,128)(2,1)S(1)}, u32[]{:S(2)}, u32[]{:S(2)}) collective-permute-start(bf16[272,256]{1,0:T(8,128)(2,1)S(1)} %own_gradient.1.refs_0_), channel_id=1, source_target_pairs={{0,128},{32,160},{64,192},{96,224},{128,0},{160,32},{192,64},{224,... | collective-permute-start | bytes 417800 | tf_op jit(solution)/shard_map/ppermute | solution.py:35
  88.7 7.1 %collective-permute-start.24 = (bf16[272,256]{1,0:T(8,128)(2,1)S(1)}, bf16[272,256]{1,0:T(8,128)(2,1)S(1)}, u32[]{:S(2)}, u32[]{:S(2)}) collective-permute-start(bf16[272,256]{1,0:T(8,128)(2,1)S(1)} %own_gradient.1.refs_0_), channel_id=1, source_target_pairs={{0,192},{32,224},{64,0},{96,32},{128,64},{160,96},{192,128},{224,1... | collective-permute-start | bytes 417800 | tf_op jit(solution)/shard_map/ppermute | solution.py:35
  90.5 6.4 %collective-permute-start.22 = (bf16[272,256]{1,0:T(8,128)(2,1)S(1)}, bf16[272,256]{1,0:T(8,128)(2,1)S(1)}, u32[]{:S(2)}, u32[]{:S(2)}) collective-permute-start(bf16[272,256]{1,0:T(8,128)(2,1)S(1)} %own_gradient.1.refs_0_), channel_id=1, source_target_pairs={{0,64},{32,96},{64,128},{96,160},{128,192},{160,224},{192,0},{224,... | collective-permute-start | bytes 417800 | tf_op jit(solution)/shard_map/ppermute | solution.py:35
  90.5 7.8 %collective-permute-start.26 = (bf16[272,256]{1,0:T(8,128)(2,1)S(1)}, bf16[272,256]{1,0:T(8,128)(2,1)S(1)}, u32[]{:S(2)}, u32[]{:S(2)}) collective-permute-start(bf16[272,256]{1,0:T(8,128)(2,1)S(1)} %own_gradient.1.refs_0_), channel_id=1, source_target_pairs={{0,32},{32,0},{64,96},{96,64},{128,160},{160,128},{192,224},{224,1... | collective-permute-start | bytes 417800 | tf_op jit(solution)/shard_map/ppermute | solution.py:35
  93.0 5.3 %collective-permute-start.28 = (bf16[272,256]{1,0:T(8,128)(2,1)S(1)}, bf16[272,256]{1,0:T(8,128)(2,1)S(1)}, u32[]{:S(2)}, u32[]{:S(2)}) collective-permute-start(bf16[272,256]{1,0:T(8,128)(2,1)S(1)} %collective-permute-done.27.refs_2_), channel_id=1, source_target_pairs={{0,32},{32,0},{64,96},{96,64},{128,160},{160,128},{192,224},{224,1... | collective-permute-start | bytes 417800 | tf_op jit(solution)/shard_map/ppermute | solution.py:35
  95.8 3.9 %collective-permute-start.25 = (bf16[272,256]{1,0:T(8,128)(2,1)S(1)}, bf16[272,256]{1,0:T(8,128)(2,1)S(1)}, u32[]{:S(2)}, u32[]{:S(2)}) collective-permute-start(bf16[272,256]{1,0:T(8,128)(2,1)S(1)} %collective-permute-done.24.refs_2_), channel_id=1, source_target_pairs={{0,32},{32,0},{64,96},{96,64},{128,160},{160,128},{192,224},{224,1... | collective-permute-start | bytes 417800 | tf_op jit(solution)/shard_map/ppermute | solution.py:35
  96.8 2.9 %collective-permute-start.23 = (bf16[272,256]{1,0:T(8,128)(2,1)S(1)}, bf16[272,256]{1,0:T(8,128)(2,1)S(1)}, u32[]{:S(2)}, u32[]{:S(2)}) collective-permute-start(bf16[272,256]{1,0:T(8,128)(2,1)S(1)} %collective-permute-done.22.refs_0_), channel_id=1, source_target_pairs={{0,32},{32,0},{64,96},{96,64},{128,160},{160,128},{192,224},{224,1... | collective-permute-start | bytes 417800 | tf_op jit(solution)/shard_map/ppermute | solution.py:35

commit v3 on v2

--- a/solution.py
+++ b/solution.py
@@ -20,8 +20,11 @@
 SPAN = 250.0
 LOWEST = 125.0
 LN2 = 0.6931471805599453
-HOPS = (2, 1, 3)
-FIRST = 4
+FAR = 2
+HOPS = (FAR, 1, 3)
+BACKWARD = HOPS[::-1]
+REST = (1, 3, 0)
+FIRST_REBUILD = 4
 VMEM_BYTES = 16 * 1024 * 1024
 
 CORE_SWAP = [(i, i ^ 1) for i in range(8)]
@@ -65,60 +68,75 @@
     return lax.rem(x + 4, 4) * 2 + core
 
 
-def gathered_owners():
+def gathered_owners(hops=HOPS):
     x, core = place()
-    return [owner(x - d, side) for d in (0, *HOPS) for side in (core, 1 - core)]
+    return [owner(x - d, side) for d in (0, *hops) for side in (core, 1 - core)]
 
 
 def columns(chunk):
     return pl.ds(pl.multiple_of(chunk * CHUNK, CHUNK), CHUNK)
 
 
-def preact_send(act_t, encoder):
-    def body(act_ref, enc_ref, *refs):
-        outs, (act_out, act_buf, enc_buf, act_sem, sems) = refs[:4], refs[4:]
+def preact_far(act_t, encoder):
+    def body(act_ref, enc_ref, send_ref, keep_ref, act_out, enc_out, act_buf, act_sem, sems):
         x, core = place()
         act_copy = pltpu.make_async_copy(act_ref, act_buf, act_sem)
         act_copy.start()
+        spans = [columns(owner(x + d, side)) for d in (FAR, *REST) for side in (1 - core, core)]
         copies = []
-        for d in range(4):
-            span = columns(owner(x + d, 1 - core))
-            copies.append(pltpu.make_async_copy(enc_ref.at[:, span], enc_buf.at[d], sems.at[d]))
-            copies[d].start()
+        for k, span in enumerate(spans):
+            copies.append(pltpu.make_async_copy(enc_ref.at[:, span], enc_out.at[:, span], sems.at[k]))
+            copies[k].start()
         act_copy.wait()
         act = act_buf[...].T
         act_out[...] = act
-        for d in range(4):
-            copies[d].wait()
-            outs[d][...] = dot(act, enc_buf[d], ((1,), (0,)))
+        for copy, span, out in zip(copies, spans, (send_ref, keep_ref)):
+            copy.wait()
+            out[...] = dot(act, enc_out[:, span], ((1,), (0,)))
+        for copy in copies[2:]:
+            copy.wait()
 
     act_t = pltpu.with_memory_space_constraint(act_t, pltpu.HBM)
     encoder = pltpu.with_memory_space_constraint(encoder, pltpu.HBM)
-    found = call(
-        body, "preact_send", (act_t, encoder), [ANYWHERE] * 2, [((TOK, CHUNK), F32)] * 4 + [((TOK, COL), BF16)],
-        scratch=[
-            pltpu.VMEM((COL, TOK), BF16), pltpu.VMEM((4, COL, CHUNK), BF16),
-            pltpu.SemaphoreType.DMA, pltpu.SemaphoreType.DMA((4,)),
-        ],
-        flops=8 * TOK * COL * CHUNK, moved=8 * COL * CHUNK + 16 * TOK * CHUNK,
-    )
-    return found[:4], found[4]
-
-
-def own_column(left, right, hops, swap, kind, name):
-    def body(left_ref, right_ref, *outs):
+    return call(
+        body, "preact_far", (act_t, encoder), [ANYWHERE] * 2,
+        [((TOK, CHUNK), F32)] * 2 + [((TOK, COL), BF16), ((COL, LAT), BF16)],
+        scratch=[pltpu.VMEM((COL, TOK), BF16), pltpu.SemaphoreType.DMA, pltpu.SemaphoreType.DMA((8,))],
+        flops=2_400_000_000, moved=4 * COL * CHUNK + 8 * TOK * CHUNK,
+    )
+
+
+def back_far(errors, dec_t):
+    def body(errors_ref, dec_ref, send_ref, keep_ref):
+        x, core = place()
+        value = errors_ref[:, :COL]
+        send_ref[...] = dot(value, dec_ref[:, columns(owner(x + FAR, 1 - core))], ((1,), (0,))).astype(BF16)
+        keep_ref[...] = dot(value, dec_ref[:, columns(owner(x + FAR, core))], ((1,), (0,)))
+
+    return call(
+        body, "back_far", (errors, dec_t), [IN_VMEM] * 2, [((TOK, CHUNK), BF16), ((TOK, CHUNK), F32)],
+        flops=4 * TOK * COL * CHUNK, moved=4 * COL * CHUNK + 6 * TOK * CHUNK,
+    )
+
+
+def rest_parts(left, right, swap, kind, name):
+    def body(left_ref, right_ref, out):
         x, core = place()
         side = 1 - core if swap else core
         value = left_ref[:, :COL]
-        for d, out in zip(hops, outs):
-            out[...] = dot(value, right_ref[:, columns(owner(x + d, side))], ((1,), (0,))).astype(kind)
-
-    count = len(hops)
-    found = call(
-        body, name, (left, right), [IN_VMEM] * 2, [((TOK, CHUNK), kind)] * count,
-        flops=2 * count * TOK * COL * CHUNK, moved=2 * count * COL * CHUNK + 2 * count * TOK * CHUNK,
-    )
-    return dict(zip(hops, found))
+        for k, d in enumerate(REST):
+            part = dot(value, right_ref[:, columns(owner(x + d, side))], ((1,), (0,)))
+            out[k * TOK:(k + 1) * TOK] = part.astype(kind)
+
+    return call(
+        body, name, (left, right), [IN_VMEM] * 2, [((3 * TOK, CHUNK), kind)],
+        flops=6 * TOK * COL * CHUNK, moved=6 * COL * CHUNK + 6 * TOK * CHUNK,
+    )[0]
+
+
+def rows_of(d):
+    first = 0 if d == FAR else REST.index(d) * TOK
+    return slice(first, first + TOK)
 
 
 def square_sums(dec_t):
@@ -152,7 +170,7 @@
     def body(mine_ref, other_ref, square_ref, square_other_ref, out_ref):
         x, core = place()
         span = columns(owner(x + d, core))
-        value = mine_ref[...] + other_ref[...]
+        value = mine_ref[rows_of(d)] + other_ref[rows_of(d)]
         size = jnp.abs(value)
         largest = jnp.maximum(jnp.max(size, axis=1, keepdims=True), 1e-30) * (1.0 + 2.0 ** -7)
         largest = largest.astype(BF16).astype(F32)
@@ -179,7 +197,7 @@
         part_refs, (square_ref, square_other_ref, bias_ref, out_ref, weight_ref) = refs[:3], refs[3:]
         x, core = place()
         span = columns(owner(x, core))
-        preact = mine_ref[...] + other_ref[...] + bias_ref[:, span]
+        preact = mine_ref[rows_of(0)] + other_ref[rows_of(0)] + bias_ref[:, span]
         sources = [square_ref[:1, span] + square_other_ref[:1, span]]
         for ref in part_refs:
             value, square = decode(ref)
@@ -202,7 +220,7 @@
 
 def rebuild_first(chunks, dec_t, own_weights):
     def body(*refs):
-        feats, (dec_ref, weight_ref, out_ref) = refs[:FIRST], refs[FIRST:]
+        feats, (dec_ref, weight_ref, out_ref) = refs[:FIRST_REBUILD], refs[FIRST_REBUILD:]
         acc = jnp.zeros((TOK, COL), F32)
         for feat, chunk in zip(feats, gathered_owners()):
             acc += dot(feat[:TOK], dec_ref[:, columns(chunk)], ((1,), (1,)))
@@ -211,23 +229,23 @@
         out_ref[:, COL:] = jnp.broadcast_to(penalty, (TOK, WIDE - COL))
 
     return call(
-        body, "rebuild_first", (*chunks, dec_t, own_weights), [IN_VMEM] * (FIRST + 2), [((TOK, WIDE), F32)],
-        flops=2 * TOK * COL * CHUNK * FIRST, moved=2 * COL * LAT + 2 * TOK * LAT,
+        body, "rebuild_first", (*chunks, dec_t, own_weights), [IN_VMEM] * (FIRST_REBUILD + 2), [((TOK, WIDE), F32)],
+        flops=2 * TOK * COL * CHUNK * FIRST_REBUILD, moved=2 * COL * LAT + 2 * TOK * LAT,
     )[0]
 
 
 def rebuild_last(chunks, dec_t, partial):
     def body(*refs):
-        feats, (dec_ref, partial_ref, out_ref) = refs[:8 - FIRST], refs[8 - FIRST:]
+        feats, (dec_ref, partial_ref, out_ref) = refs[:8 - FIRST_REBUILD], refs[8 - FIRST_REBUILD:]
         acc = partial_ref[:, :COL]
-        for feat, chunk in zip(feats, gathered_owners()[FIRST:]):
+        for feat, chunk in zip(feats, gathered_owners()[FIRST_REBUILD:]):
             acc += dot(feat[:TOK], dec_ref[:, columns(chunk)], ((1,), (1,)))
         out_ref[:, :COL] = acc.astype(BF16)
         out_ref[:, COL:] = partial_ref[:, COL:].astype(BF16)
 
     return call(
-        body, "rebuild_last", (*chunks, dec_t, partial), [IN_VMEM] * (10 - FIRST), [((TOK, WIDE), BF16)],
-        flops=2 * TOK * COL * CHUNK * (8 - FIRST), moved=2 * COL * LAT + 2 * TOK * LAT,
+        body, "rebuild_last", (*chunks, dec_t, partial), [IN_VMEM] * (10 - FIRST_REBUILD), [((TOK, WIDE), BF16)],
+        flops=2 * TOK * COL * CHUNK * (8 - FIRST_REBUILD), moved=2 * COL * LAT + 2 * TOK * LAT,
     )[0]
 
 
@@ -255,7 +273,7 @@
 
 def own_gradient(mine, other, parts, features, weights, errors):
     def body(mine_ref, other_ref, one_ref, two_ref, three_ref, feat_ref, weight_ref, tail_ref, out_ref):
-        total = mine_ref[...] + other_ref[...].astype(F32)
+        total = mine_ref[rows_of(0)] + other_ref[rows_of(0)].astype(F32)
         for ref in (one_ref, two_ref, three_ref):
             total += ref[...].astype(F32)
         total += SPARSITY * weight_ref[:1]
@@ -313,83 +331,79 @@
     return loss * (1.0 / (TOK * LAYERS * D))
 
 
-def encoder_gradient(act_t, chunks, start, before=None):
-    count = len(chunks)
-
+def encoder_gradient(act_t, chunks):
     def body(act_ref, *refs):
-        grads, (out_ref, sum_ref, loss_ref, buffer, sems) = refs[:count], refs[-5:]
-        owners = gathered_owners()[start:start + count]
-        if before is None:
-            sum_ref[...] = jnp.zeros((1, LAT), F32)
-            loss_ref[...] = loss_rows(grads)
-        else:
-            sum_ref[...] = refs[count + 1][...]
-            loss_ref[...] = refs[count + 2][...] + loss_rows(grads)
-
-        def values(k, chunk):
-            grad = grads[k][:TOK]
-            sum_ref[:, columns(chunk)] = jnp.sum(grad.astype(F32), axis=0, keepdims=True)
-            return dot(act_ref[...], grad, ((1,), (0,))).astype(BF16)
-
-        store_chunks(values, owners, out_ref, buffer, sems)
-
-    extra = () if before is None else tuple(before)
-    return pl.pallas_call(
-        body,
-        in_specs=[IN_VMEM] * (1 + count) + [ANYWHERE, IN_VMEM, IN_VMEM][:len(extra)],
-        out_specs=[ANYWHERE, IN_VMEM, IN_VMEM],
-        out_shape=[
-            jax.ShapeDtypeStruct((COL, LAT), BF16), jax.ShapeDtypeStruct((1, LAT), F32),
-            jax.ShapeDtypeStruct((1, 128), F32),
+        grads, (out_ref, sum_ref, loss_ref, buffer, sum_buf, loss_buf, sems, small_sems) = refs[:8], refs[8:]
+        loss_buf[...] = loss_rows(grads)
+        for grad, chunk in zip(grads, gathered_owners(BACKWARD)):
+            sum_buf[:, columns(chunk)] = jnp.sum(grad[:TOK].astype(F32), axis=0, keepdims=True)
+        small = [
+            pltpu.make_async_copy(sum_buf, sum_ref, small_sems.at[0]),
+            pltpu.make_async_copy(loss_buf, loss_ref, small_sems.at[1]),
+        ]
+        for copy in small:
+            copy.start()
+        store_chunks(
+            lambda k, chunk: dot(act_ref[...], grads[k][:TOK], ((1,), (0,))).astype(BF16),
+            gathered_owners(BACKWARD), out_ref, buffer, sems,
+        )
+        for copy in small:
+            copy.wait()
+
+    return call(
+        body, "encoder_gradient", (act_t, *chunks), [IN_VMEM] * 9,
+        [((COL, LAT), BF16), ((1, LAT), F32), ((1, 128), F32)], out_specs=[ANYWHERE] * 3,
+        scratch=[
+            pltpu.VMEM((8, COL, CHUNK), BF16), pltpu.VMEM((1, LAT), F32), pltpu.VMEM((1, 128), F32),
+            pltpu.SemaphoreType.DMA((8,)), pltpu.SemaphoreType.DMA((2,)),
         ],
-        scratch_shapes=[pltpu.VMEM((count, COL, CHUNK), BF16), pltpu.SemaphoreType.DMA((count,))],
-        input_output_aliases={1 + count: 0} if extra else {},
-        compiler_params=pltpu.CompilerParams(vmem_limit_bytes=VMEM_BYTES),
-        name="encoder_gradient_last" if extra else "encoder_gradient_first",
-        cost_estimate=pl.CostEstimate(
-            flops=2 * TOK * COL * CHUNK * count, bytes_accessed=2 * COL * CHUNK * count, transcendentals=0
-        ),
-    )(act_t, *chunks, *extra)
-
-
-def gather_chunks(own, work):
-    moved = [on_width(own, x_shift(d)) for d in HOPS]
-    first = [chunk for part in (own, moved[0]) for chunk in (part, on_width(part, CORE_SWAP))]
-    done = work(first)
-    return first + [chunk for part in moved[1:] for chunk in (part, on_width(part, CORE_SWAP))], done
+        flops=2 * TOK * COL * LAT, moved=2 * COL * LAT + 2 * TOK * LAT,
+    )
+
+
+def gather_chunks(own, hops):
+    moved = [own] + [on_width(own, x_shift(d)) for d in hops]
+    return [chunk for part in moved for chunk in (part, on_width(part, CORE_SWAP))]
 
 
 def shards(activations, encoder, latent_bias, decoder, output_bias):
     act_t, dec_t = activations.T, decoder.T
 
-    send, act = preact_send(act_t, encoder)
-    swapped = {d: on_width(send[d], CORE_SWAP) for d in (*HOPS, 0)}
-    keep = own_column(act, encoder, (*HOPS, 0), False, F32, "preact_keep")
-    squares = square_sums(dec_t)
+    send, keep_far, act, enc = preact_far(act_t, encoder)
+    send, early_dec = lax.optimization_barrier((send, dec_t))
+    squares = square_sums(early_dec)
     squares = (squares, on_width(squares, CORE_SWAP))
-    coded = [on_width(encode(keep[d], swapped[d], squares, d), x_shift(d)) for d in HOPS]
-    features, own_weights = own_features(keep[0], swapped[0], coded, squares, latent_bias[None, :])
-
-    feature_chunks, partial = gather_chunks(features, lambda chunks: rebuild_first(chunks, dec_t, own_weights))
-    parts = rebuild_last(feature_chunks[FIRST:], dec_t, partial).reshape(32, 8, WIDE)
+    far = (keep_far, on_width(send, CORE_SWAP))
+    send = rest_parts(act, enc, True, F32, "preact_send")
+    keep = rest_parts(act, enc, False, F32, "preact_keep")
+    coded, send, keep = lax.optimization_barrier((encode(*far, squares, FAR), send, keep))
+    rest = (keep, on_width(send, CORE_SWAP))
+    coded = [on_width(coded, x_shift(FAR))] + [on_width(encode(*rest, squares, d), x_shift(d)) for d in HOPS[1:]]
+    features, own_weights = own_features(*rest, coded, squares, latent_bias[None, :])
+
+    feature_chunks = gather_chunks(features, HOPS)
+    partial = rebuild_first(feature_chunks[:FIRST_REBUILD], dec_t, own_weights)
+    parts = rebuild_last(feature_chunks[FIRST_REBUILD:], dec_t, partial).reshape(32, 8, WIDE)
     parts, bias_row = lax.optimization_barrier((parts, output_bias[None, :]))
     parts = lax.all_to_all(parts, "latent", 0, 0)
     errors = error_rows(parts, act_t, bias_row)
     errors = lax.all_to_all(errors, "latent", 0, 0).reshape(TOK, WIDE)
 
-    far, rest = HOPS[:1], (*HOPS[1:], 0)
-    send = own_column(errors, dec_t, far, True, BF16, "back_send_far")
-    swapped = {d: on_width(send[d], CORE_SWAP) for d in far}
-    keep = own_column(errors, dec_t, far, False, F32, "back_keep_far")
-    send = own_column(errors, dec_t, rest, True, BF16, "back_send")
-    swapped |= {d: on_width(send[d], CORE_SWAP) for d in rest}
-    keep |= own_column(errors, dec_t, rest, False, F32, "back_keep")
-    summed = [on_width((keep[d] + swapped[d].astype(F32)).astype(BF16), x_shift(d)) for d in HOPS]
+    send, keep_far = back_far(errors, dec_t)
+    send, keep_far, errors = lax.optimization_barrier((send, keep_far, errors))
+    summed = keep_far + on_width(send, CORE_SWAP).astype(F32)
+    send = rest_parts(errors, dec_t, True, BF16, "back_send")
+    keep = rest_parts(errors, dec_t, False, F32, "back_keep")
+    summed, send, keep = lax.optimization_barrier((summed.astype(BF16), send, keep))
+    summed = [on_width(summed, x_shift(FAR))]
+    rest = (keep, on_width(send, CORE_SWAP))
+    for d in HOPS[1:]:
+        total = rest[0][rows_of(d)] + rest[1][rows_of(d)].astype(F32)
+        summed.append(on_width(total.astype(BF16), x_shift(d)))
     decoder_grad, output_grad = decoder_gradient(errors, feature_chunks, dec_t)
     decoder_grad, output_grad, features = lax.optimization_barrier((decoder_grad, output_grad[0], features))
-    grad_pre = own_gradient(keep[0], swapped[0], summed, features, own_weights, errors)
-    grad_chunks, first = gather_chunks(grad_pre, lambda chunks: encoder_gradient(act_t, chunks, 0))
-    encoder_grad, latent_grad, loss_value = encoder_gradient(act_t, grad_chunks[FIRST:], FIRST, first)
+    grad_pre = own_gradient(*rest, summed, features, own_weights, errors)
+    encoder_grad, latent_grad, loss_value = encoder_gradient(act_t, gather_chunks(grad_pre, BACKWARD))
     return (loss_value[0, 0], encoder_grad, latent_grad[0], decoder_grad.T, output_grad)
 
 

time: 102 us -> 99.8 us (0.978)
  Pallas kernels: 13.2 us -> 11.2 us
    pallas_call x2 -> x0, Pallas kernels: 3.36 us -> none  [encoder_gradient(): pl.pallas_call(body, in_specs=[IN_VMEM] * (1 + count) + [ANYWHERE, IN_VME...]
    pallas_call x16 -> x17, Pallas kernels: 9.84 us -> 11.2 us  [call(): pl.pallas_call(body, in_specs=in_specs, out_specs=out_specs or [IN_VMEM]...]
    ppermute x29 -> x25, waiting for transfers between devices: 14.1 us -> 13.1 us  [on_width(): return lax.ppermute(value, 'width', pairs)]
    ppermute x29 -> x25, starting transfers between devices: 34.5 us -> 34.9 us  [on_width(): return lax.ppermute(value, 'width', pairs)]
  transfers between devices with their start and end apart: 29 -> 25, of which waited for: 9 -> 11; matrix products, arithmetic and copies ran while one was open for 1% -> 1% of each run, Pallas kernels for 6% -> 5%
where the time goes in v3:
time: 99.8 us; the launch traced here: 99.7 us
  blocking collectives  38.7 us (39%)
  starting transfers between devices  34.9 us (35%)
  waiting for transfers between devices  13.1 us (13%)
  Pallas kernels  11.2 us (11%)
    ppermute x25, starting transfers between devices, on_width(): return lax.ppermute(value, 'width', pairs)  34.9 us
    all_to_all x1, blocking collectives, shards(): parts = lax.all_to_all(parts, 'latent', 0, 0)  22.7 us
    all_to_all x1, blocking collectives, shards(): errors = lax.all_to_all(errors, 'latent', 0, 0).reshape(TOK, WIDE)  16 us
    ppermute x25, waiting for transfers between devices, on_width(): return lax.ppermute(value, 'width', pairs)  13.1 us
    pallas_call x17, Pallas kernels, call(): pl.pallas_call(body, in_specs=in_specs, out_specs=out_specs or [IN_VMEM]...  11.2 us
  transfers between devices with their start and end apart: 25, of which 11 were waited for; matrix products, arithmetic and copies ran while one was open for 1% of the time, Pallas kernels for 5%

profile of v3, /device:TPU:1, one launch (start us, length us, event | category | flops | bytes accessed | tf_op | source)
XLA Modules:
  0.0 99.7 jit_solution(11876293514086875928)
XLA Ops:
  0.6 2.1 %preact_far.1 = (f32[256,256]{1,0:T(8,128)S(1)}, f32[256,256]{1,0:T(8,128)S(1)}, bf16[256,576]{1,0:T(8,128)(2,1)S(1)}, bf16[576,2048]{1,0:T(8,128)(2,1)S(1)}) custom-call(bf16[576,256]{1,0:T(8,128)(2,1)} %bitcast.22, bf16[576,2048]{1,0:T(8,128)(2,1)} %enc_ref.1), custom_call_target="tpu_custom_call" | custom-call | flops 2400000000 | bytes 1114112 | tf_op jit(solution)/shard_map/preact_far/pallas_call | solution.py:50
  2.7 3.3 %collective-permute-start = (f32[256,256]{1,0:T(8,128)S(1)}, f32[256,256]{1,0:T(8,128)S(1)}, u32[]{:S(2)}, u32[]{:S(2)}) collective-permute-start(f32[256,256]{1,0:T(8,128)S(1)} %get-tuple-element.36), channel_id=1, source_target_pairs={{0,32},{32,0},{64,96},{96,64},{128,160},{160,128},{192,224},{224,1... | collective-permute-start | bytes 786440 | tf_op jit(solution)/shard_map/ppermute | solution.py:38
  6.0 0.1 square_sums.1.square_ref.refs_3_
  6.2 0.4 collective-permute-start.1
  6.6 0.5 preact_keep.1.mine_ref
  7.1 0.5 preact_send.1
  7.6 0.0 copy-start.2
  7.6 0.0 collective-permute-done.1.square_other_ref.refs_4_
  7.6 0.0 collective-permute-done.other_ref
  7.6 0.2 encode_sums.3
  7.8 0.3 collective-permute-start.2
  8.1 1.0 %collective-permute-start.3 = (bf16[272,256]{1,0:T(8,128)(2,1)S(1)}, bf16[272,256]{1,0:T(8,128)(2,1)S(1)}, u32[]{:S(2)}, u32[]{:S(2)}) collective-permute-start(bf16[272,256]{1,0:T(8,128)(2,1)S(1)} %encode_sums.3), channel_id=1, source_target_pairs={{0,128},{32,160},{64,192},{96,224},{128,0},{160,32},{192,64},{224,... | collective-permute-start | bytes 417800 | tf_op jit(solution)/shard_map/ppermute | solution.py:38
  9.1 1.0 %collective-permute-done.2.other_ref = f32[768,256]{1,0:T(8,128)S(1)} collective-permute-done((f32[768,256]{1,0:T(8,128)S(1)}, f32[768,256]{1,0:T(8,128)S(1)}, u32[]{:S(2)}, u32[]{:S(2)}) %collective-permute-start.2) | collective-permute-done | bytes 786464 | tf_op jit(solution)/shard_map/ppermute | solution.py:38
  10.2 0.2 encode_sums.4
  10.4 0.1 collective-permute-start.4
  10.5 0.2 encode_sums.5
  10.7 2.7 %collective-permute-start.5 = (bf16[272,256]{1,0:T(8,128)(2,1)S(1)}, bf16[272,256]{1,0:T(8,128)(2,1)S(1)}, u32[]{:S(2)}, u32[]{:S(2)}) collective-permute-start(bf16[272,256]{1,0:T(8,128)(2,1)S(1)} %encode_sums.5), channel_id=1, source_target_pairs={{0,192},{32,224},{64,0},{96,32},{128,64},{160,96},{192,128},{224,1... | collective-permute-start | bytes 417800 | tf_op jit(solution)/shard_map/ppermute | solution.py:38
  13.4 1.2 %collective-permute-done.3.refs_0_ = bf16[272,256]{1,0:T(8,128)(2,1)S(1)} collective-permute-done((bf16[272,256]{1,0:T(8,128)(2,1)S(1)}, bf16[272,256]{1,0:T(8,128)(2,1)S(1)}, u32[]{:S(2)}, u32[]{:S(2)}) %collective-permute-start.3) | collective-permute-done | bytes 139296 | tf_op jit(solution)/shard_map/ppermute | solution.py:38
  14.6 3.5 %collective-permute-done.4.refs_1_ = bf16[272,256]{1,0:T(8,128)(2,1)S(1)} collective-permute-done((bf16[272,256]{1,0:T(8,128)(2,1)S(1)}, bf16[272,256]{1,0:T(8,128)(2,1)S(1)}, u32[]{:S(2)}, u32[]{:S(2)}) %collective-permute-start.4) | collective-permute-done | bytes 139296 | tf_op jit(solution)/shard_map/ppermute | solution.py:38
  18.1 0.5 own_features.1
  18.6 1.2 %collective-permute-start.11 = (bf16[272,256]{1,0:T(8,128)(2,1)S(1)}, bf16[272,256]{1,0:T(8,128)(2,1)S(1)}, u32[]{:S(2)}, u32[]{:S(2)}) collective-permute-start(bf16[272,256]{1,0:T(8,128)(2,1)S(1)} %get-tuple-element.57.refs_0_.feat_ref), channel_id=1, source_target_pairs={{0,128},{32,160},{64,192},{96,224},{128,0},{160,32},{192,64},{224,... | collective-permute-start | bytes 417800 | tf_op jit(solution)/shard_map/ppermute | solution.py:38
  19.8 0.4 collective-permute-start.8
  20.2 1.1 %collective-permute-start.6 = (bf16[272,256]{1,0:T(8,128)(2,1)S(1)}, bf16[272,256]{1,0:T(8,128)(2,1)S(1)}, u32[]{:S(2)}, u32[]{:S(2)}) collective-permute-start(bf16[272,256]{1,0:T(8,128)(2,1)S(1)} %get-tuple-element.57.refs_0_.feat_ref), channel_id=1, source_target_pairs={{0,64},{32,96},{64,128},{96,160},{128,192},{160,224},{192,0},{224,... | collective-permute-start | bytes 417800 | tf_op jit(solution)/shard_map/ppermute | solution.py:38
  21.3 1.3 %collective-permute-start.10 = (bf16[272,256]{1,0:T(8,128)(2,1)S(1)}, bf16[272,256]{1,0:T(8,128)(2,1)S(1)}, u32[]{:S(2)}, u32[]{:S(2)}) collective-permute-start(bf16[272,256]{1,0:T(8,128)(2,1)S(1)} %get-tuple-element.57.refs_0_.feat_ref), channel_id=1, source_target_pairs={{0,32},{32,0},{64,96},{96,64},{128,160},{160,128},{192,224},{224,1... | collective-permute-start | bytes 417800 | tf_op jit(solution)/shard_map/ppermute | solution.py:38
  22.6 2.2 %collective-permute-done.11.refs_2_ = bf16[272,256]{1,0:T(8,128)(2,1)S(1)} collective-permute-done((bf16[272,256]{1,0:T(8,128)(2,1)S(1)}, bf16[272,256]{1,0:T(8,128)(2,1)S(1)}, u32[]{:S(2)}, u32[]{:S(2)}) %collective-permute-start.11) | collective-permute-done | bytes 139296 | tf_op jit(solution)/shard_map/ppermute | solution.py:38
  24.8 2.6 %collective-permute-start.12 = (bf16[272,256]{1,0:T(8,128)(2,1)S(1)}, bf16[272,256]{1,0:T(8,128)(2,1)S(1)}, u32[]{:S(2)}, u32[]{:S(2)}) collective-permute-start(bf16[272,256]{1,0:T(8,128)(2,1)S(1)} %collective-permute-done.11.refs_2_), channel_id=1, source_target_pairs={{0,32},{32,0},{64,96},{96,64},{128,160},{160,128},{192,224},{224,1... | collective-permute-start | bytes 417800 | tf_op jit(solution)/shard_map/ppermute | solution.py:38
  27.4 0.0 collective-permute-done.8.refs_2_.refs_6_
  27.4 0.8 collective-permute-start.9
  28.2 1.1 %collective-permute-start.7 = (bf16[272,256]{1,0:T(8,128)(2,1)S(1)}, bf16[272,256]{1,0:T(8,128)(2,1)S(1)}, u32[]{:S(2)}, u32[]{:S(2)}) collective-permute-start(bf16[272,256]{1,0:T(8,128)(2,1)S(1)} %collective-permute-done.6.refs_0_.refs_4_), channel_id=1, source_target_pairs={{0,32},{32,0},{64,96},{96,64},{128,160},{160,128},{192,224},{224,1... | collective-permute-start | bytes 417800 | tf_op jit(solution)/shard_map/ppermute | solution.py:38
  29.3 0.0 collective-permute-done.10.refs_1_
  29.3 0.6 rebuild_first.1.refs_5_
  29.9 0.0 copy-start.1
  29.9 0.4 collective-permute-done.7.refs_1_.refs_5_
  30.3 0.6 rebuild_last.1
  30.8 22.7 %all_to_all.10.parts_ref = bf16[32,8,640]{2,1,0:T(8,128)(2,1)S(1)} all-to-all(bf16[32,8,640]{2,1,0:T(8,128)(2,1)S(1)} %bitcast.21), channel_id=1, replica_groups=mesh['width'=8,'latent'=32] {'latent'}, dimensions={0} | all-to-all | bytes 655360 | tf_op jit(solution)/shard_map/all_to_all | solution.py:388
  53.6 0.4 error_rows.1
  54.0 16.0 %all_to_all.11 = bf16[32,8,640]{2,1,0:T(8,128)(2,1)S(1)} all-to-all(bf16[32,8,640]{2,1,0:T(8,128)(2,1)S(1)} %error_rows.1), channel_id=1, replica_groups=mesh['width'=8,'latent'=32] {'latent'}, dimensions={0} | all-to-all | bytes 655360 | tf_op jit(solution)/shard_map/all_to_all | solution.py:390
  70.0 0.4 back_far.1
  70.3 3.8 %collective-permute-start.13 = (bf16[256,256]{1,0:T(8,128)(2,1)S(1)}, bf16[256,256]{1,0:T(8,128)(2,1)S(1)}, u32[]{:S(2)}, u32[]{:S(2)}) collective-permute-start(bf16[256,256]{1,0:T(8,128)(2,1)S(1)} %get-tuple-element.50), channel_id=1, source_target_pairs={{0,32},{32,0},{64,96},{96,64},{128,160},{160,128},{192,224},{224,1... | collective-permute-start | bytes 393224 | tf_op jit(solution)/shard_map/ppermute | solution.py:38
  74.1 0.5 back_send.1
  74.6 0.5 back_keep.1.mine_ref
  75.1 0.0 collective-permute-done.13
  75.1 0.4 collective-permute-start.14
  75.6 2.2 %collective-permute-start.15 = (bf16[256,256]{1,0:T(8,128)(2,1)S(1)}, bf16[256,256]{1,0:T(8,128)(2,1)S(1)}, u32[]{:S(2)}, u32[]{:S(2)}) collective-permute-start(bf16[256,256]{1,0:T(8,128)(2,1)S(1)} %add_convert_fusion.2), channel_id=1, source_target_pairs={{0,128},{32,160},{64,192},{96,224},{128,0},{160,32},{192,64},{224,... | collective-permute-start | bytes 393224 | tf_op jit(solution)/shard_map/ppermute | solution.py:38
  77.8 0.1 add_convert_fusion
  77.9 1.1 %collective-permute-start.17 = (bf16[256,256]{1,0:T(8,128)(2,1)S(1)}, bf16[256,256]{1,0:T(8,128)(2,1)S(1)}, u32[]{:S(2)}, u32[]{:S(2)}) collective-permute-start(bf16[256,256]{1,0:T(8,128)(2,1)S(1)} %get-tuple-element.63), channel_id=1, source_target_pairs={{0,192},{32,224},{64,0},{96,32},{128,64},{160,96},{192,128},{224,1... | collective-permute-start | bytes 393224 | tf_op jit(solution)/shard_map/ppermute | solution.py:38
  78.9 0.5 collective-permute-start.16
  79.4 1.9 %decoder_gradient.1 = (bf16[576,2048]{1,0:T(8,128)(2,1)}, f32[1,576]{1,0:T(1,128)S(1)}) custom-call(bf16[256,640]{1,0:T(8,128)(2,1)S(1)} %bitcast.19, bf16[272,256]{1,0:T(8,128)(2,1)S(1)} %get-tuple-element.57.refs_0_.feat_ref, bf16[272,256]{1,0:T(8,128)(2,1)S(1)} %collective-permute-done.10.refs_1_, bf16[272,256]{1,0:T(8,128)(2,1)S(1)} %collective-permute-done.11.refs_2_, ...), custom_call_target="tpu_custom_call" | custom-call | flops 603979776 | bytes 5767168 | tf_op jit(solution)/shard_map/decoder_gradient/pallas_call | solution.py:50
  81.4 0.6 reduce
  82.0 0.1 collective-permute-done.15.one_ref
  82.0 2.2 %collective-permute-done.17.three_ref = bf16[256,256]{1,0:T(8,128)(2,1)S(1)} collective-permute-done((bf16[256,256]{1,0:T(8,128)(2,1)S(1)}, bf16[256,256]{1,0:T(8,128)(2,1)S(1)}, u32[]{:S(2)}, u32[]{:S(2)}) %collective-permute-start.17) | collective-permute-done | bytes 131104 | tf_op jit(solution)/shard_map/ppermute | solution.py:38
  84.2 0.5 collective-permute-done.16.two_ref
  84.7 0.3 own_gradient.1.refs_0_
  85.0 2.9 %collective-permute-start.23 = (bf16[272,256]{1,0:T(8,128)(2,1)S(1)}, bf16[272,256]{1,0:T(8,128)(2,1)S(1)}, u32[]{:S(2)}, u32[]{:S(2)}) collective-permute-start(bf16[272,256]{1,0:T(8,128)(2,1)S(1)} %own_gradient.1.refs_0_), channel_id=1, source_target_pairs={{0,128},{32,160},{64,192},{96,224},{128,0},{160,32},{192,64},{224,... | collective-permute-start | bytes 417800 | tf_op jit(solution)/shard_map/ppermute | solution.py:38
  87.9 0.1 collective-permute-start.21
  88.0 2.6 %collective-permute-start.19 = (bf16[272,256]{1,0:T(8,128)(2,1)S(1)}, bf16[272,256]{1,0:T(8,128)(2,1)S(1)}, u32[]{:S(2)}, u32[]{:S(2)}) collective-permute-start(bf16[272,256]{1,0:T(8,128)(2,1)S(1)} %own_gradient.1.refs_0_), channel_id=1, source_target_pairs={{0,192},{32,224},{64,0},{96,32},{128,64},{160,96},{192,128},{224,1... | collective-permute-start | bytes 417800 | tf_op jit(solution)/shard_map/ppermute | solution.py:38
  90.6 1.3 %collective-permute-start.18 = (bf16[272,256]{1,0:T(8,128)(2,1)S(1)}, bf16[272,256]{1,0:T(8,128)(2,1)S(1)}, u32[]{:S(2)}, u32[]{:S(2)}) collective-permute-start(bf16[272,256]{1,0:T(8,128)(2,1)S(1)} %own_gradient.1.refs_0_), channel_id=1, source_target_pairs={{0,32},{32,0},{64,96},{96,64},{128,160},{160,128},{192,224},{224,1... | collective-permute-start | bytes 417800 | tf_op jit(solution)/shard_map/ppermute | solution.py:38
  91.9 2.6 %collective-permute-start.24 = (bf16[272,256]{1,0:T(8,128)(2,1)S(1)}, bf16[272,256]{1,0:T(8,128)(2,1)S(1)}, u32[]{:S(2)}, u32[]{:S(2)}) collective-permute-start(bf16[272,256]{1,0:T(8,128)(2,1)S(1)} %collective-permute-done.23.refs_6_), channel_id=1, source_target_pairs={{0,32},{32,0},{64,96},{96,64},{128,160},{160,128},{192,224},{224,1... | collective-permute-start | bytes 417800 | tf_op jit(solution)/shard_map/ppermute | solution.py:38
  94.5 0.8 collective-permute-done.21.refs_4_
  95.3 1.0 %collective-permute-start.22 = (bf16[272,256]{1,0:T(8,128)(2,1)S(1)}, bf16[272,256]{1,0:T(8,128)(2,1)S(1)}, u32[]{:S(2)}, u32[]{:S(2)}) collective-permute-start(bf16[272,256]{1,0:T(8,128)(2,1)S(1)} %collective-permute-done.21.refs_4_), channel_id=1, source_target_pairs={{0,32},{32,0},{64,96},{96,64},{128,160},{160,128},{192,224},{224,1... | collective-permute-start | bytes 417800 | tf_op jit(solution)/shard_map/ppermute | solution.py:38
  96.3 0.0 collective-permute-start.20
  96.4 1.0 collective-permute-done.22.refs_5_
  97.3 0.4 collective-permute-done.20.refs_3_
  97.7 1.8 %encoder_gradient.1 = (bf16[576,2048]{1,0:T(8,128)(2,1)}, f32[1,2048]{1,0:T(1,128)}, f32[1,128]{1,0:T(1,128)}) custom-call(bf16[576,256]{1,0:T(8,128)(2,1)S(1)} %bitcast.24, bf16[272,256]{1,0:T(8,128)(2,1)S(1)} %own_gradient.1.refs_0_, bf16[272,256]{1,0:T(8,128)(2,1)S(1)} %collective-permute-done.18.refs_1_, ...), custom_call_target="tpu_custom_call" | custom-call | flops 603979776 | bytes 3407872 | tf_op jit(solution)/shard_map/encoder_gradient/pallas_call | solution.py:50
  (17 shorter events, 0.1 us)
Async XLA Ops:
  0.6 5.4 %copy-start = (bf16[2048,576]{0,1:T(8,128)(2,1)S(1)}, bf16[2048,576]{0,1:T(8,128)(2,1)}, u32[]{:S(2)}) copy-start(bf16[2048,576]{0,1:T(8,128)(2,1)} %param.8) | copy-start | bytes 7077892
  2.7 4.9 %collective-permute-start = (f32[256,256]{1,0:T(8,128)S(1)}, f32[256,256]{1,0:T(8,128)S(1)}, u32[]{:S(2)}, u32[]{:S(2)}) collective-permute-start(f32[256,256]{1,0:T(8,128)S(1)} %get-tuple-element.36), channel_id=1, source_target_pairs={{0,32},{32,0},{64,96},{96,64},{128,160},{160,128},{192,224},{224,1... | collective-permute-start | bytes 786440 | tf_op jit(solution)/shard_map/ppermute | solution.py:38
  6.2 1.4 %collective-permute-start.1 = (f32[8,2048]{1,0:T(8,128)S(1)}, f32[8,2048]{1,0:T(8,128)S(1)}, u32[]{:S(2)}, u32[]{:S(2)}) collective-permute-start(f32[8,2048]{1,0:T(8,128)S(1)} %square_sums.1.square_ref.refs_3_), channel_id=1, source_target_pairs={{0,32},{32,0},{64,96},{96,64},{128,160},{160,128},{192,224},{224,1... | collective-permute-start | bytes 196616 | tf_op jit(solution)/shard_map/ppermute | solution.py:38
  7.6 10.5 %copy-start.2 = (f32[2048]{0:T(1024)S(1)}, f32[2048]{0:T(1024)}, u32[]{:S(2)}) copy-start(f32[2048]{0:T(1024)} %param.7) | copy-start | bytes 24580
  7.8 2.4 %collective-permute-start.2 = (f32[768,256]{1,0:T(8,128)S(1)}, f32[768,256]{1,0:T(8,128)S(1)}, u32[]{:S(2)}, u32[]{:S(2)}) collective-permute-start(f32[768,256]{1,0:T(8,128)S(1)} %preact_send.1), channel_id=1, source_target_pairs={{0,32},{32,0},{64,96},{96,64},{128,160},{160,128},{192,224},{224,1... | collective-permute-start | bytes 2359304 | tf_op jit(solution)/shard_map/ppermute | solution.py:38
  8.1 6.5 %collective-permute-start.3 = (bf16[272,256]{1,0:T(8,128)(2,1)S(1)}, bf16[272,256]{1,0:T(8,128)(2,1)S(1)}, u32[]{:S(2)}, u32[]{:S(2)}) collective-permute-start(bf16[272,256]{1,0:T(8,128)(2,1)S(1)} %encode_sums.3), channel_id=1, source_target_pairs={{0,128},{32,160},{64,192},{96,224},{128,0},{160,32},{192,64},{224,... | collective-permute-start | bytes 417800 | tf_op jit(solution)/shard_map/ppermute | solution.py:38
  10.4 18.9 %copy-start.3 = (f32[576]{0:T(1024)S(1)}, f32[576]{0:T(1024)}, u32[]{:S(2)}) copy-start(f32[576]{0:T(1024)} %param.9) | copy-start | bytes 6916
  10.4 7.7 %collective-permute-start.4 = (bf16[272,256]{1,0:T(8,128)(2,1)S(1)}, bf16[272,256]{1,0:T(8,128)(2,1)S(1)}, u32[]{:S(2)}, u32[]{:S(2)}) collective-permute-start(bf16[272,256]{1,0:T(8,128)(2,1)S(1)} %encode_sums.4), channel_id=1, source_target_pairs={{0,64},{32,96},{64,128},{96,160},{128,192},{160,224},{192,0},{224,... | collective-permute-start | bytes 417800 | tf_op jit(solution)/shard_map/ppermute | solution.py:38
  10.7 7.4 %collective-permute-start.5 = (bf16[272,256]{1,0:T(8,128)(2,1)S(1)}, bf16[272,256]{1,0:T(8,128)(2,1)S(1)}, u32[]{:S(2)}, u32[]{:S(2)}) collective-permute-start(bf16[272,256]{1,0:T(8,128)(2,1)S(1)} %encode_sums.5), channel_id=1, source_target_pairs={{0,192},{32,224},{64,0},{96,32},{128,64},{160,96},{192,128},{224,1... | collective-permute-start | bytes 417800 | tf_op jit(solution)/shard_map/ppermute | solution.py:38
  18.6 6.2 %collective-permute-start.11 = (bf16[272,256]{1,0:T(8,128)(2,1)S(1)}, bf16[272,256]{1,0:T(8,128)(2,1)S(1)}, u32[]{:S(2)}, u32[]{:S(2)}) collective-permute-start(bf16[272,256]{1,0:T(8,128)(2,1)S(1)} %get-tuple-element.57.refs_0_.feat_ref), channel_id=1, source_target_pairs={{0,128},{32,160},{64,192},{96,224},{128,0},{160,32},{192,64},{224,... | collective-permute-start | bytes 417800 | tf_op jit(solution)/shard_map/ppermute | solution.py:38
  19.8 7.5 %collective-permute-start.8 = (bf16[272,256]{1,0:T(8,128)(2,1)S(1)}, bf16[272,256]{1,0:T(8,128)(2,1)S(1)}, u32[]{:S(2)}, u32[]{:S(2)}) collective-permute-start(bf16[272,256]{1,0:T(8,128)(2,1)S(1)} %get-tuple-element.57.refs_0_.feat_ref), channel_id=1, source_target_pairs={{0,192},{32,224},{64,0},{96,32},{128,64},{160,96},{192,128},{224,1... | collective-permute-start | bytes 417800 | tf_op jit(solution)/shard_map/ppermute | solution.py:38
  20.2 8.0 %collective-permute-start.6 = (bf16[272,256]{1,0:T(8,128)(2,1)S(1)}, bf16[272,256]{1,0:T(8,128)(2,1)S(1)}, u32[]{:S(2)}, u32[]{:S(2)}) collective-permute-start(bf16[272,256]{1,0:T(8,128)(2,1)S(1)} %get-tuple-element.57.refs_0_.feat_ref), channel_id=1, source_target_pairs={{0,64},{32,96},{64,128},{96,160},{128,192},{160,224},{192,0},{224,... | collective-permute-start | bytes 417800 | tf_op jit(solution)/shard_map/ppermute | solution.py:38
  21.3 8.0 %collective-permute-start.10 = (bf16[272,256]{1,0:T(8,128)(2,1)S(1)}, bf16[272,256]{1,0:T(8,128)(2,1)S(1)}, u32[]{:S(2)}, u32[]{:S(2)}) collective-permute-start(bf16[272,256]{1,0:T(8,128)(2,1)S(1)} %get-tuple-element.57.refs_0_.feat_ref), channel_id=1, source_target_pairs={{0,32},{32,0},{64,96},{96,64},{128,160},{160,128},{192,224},{224,1... | collective-permute-start | bytes 417800 | tf_op jit(solution)/shard_map/ppermute | solution.py:38
  24.8 4.5 %collective-permute-start.12 = (bf16[272,256]{1,0:T(8,128)(2,1)S(1)}, bf16[272,256]{1,0:T(8,128)(2,1)S(1)}, u32[]{:S(2)}, u32[]{:S(2)}) collective-permute-start(bf16[272,256]{1,0:T(8,128)(2,1)S(1)} %collective-permute-done.11.refs_2_), channel_id=1, source_target_pairs={{0,32},{32,0},{64,96},{96,64},{128,160},{160,128},{192,224},{224,1... | collective-permute-start | bytes 417800 | tf_op jit(solution)/shard_map/ppermute | solution.py:38
  27.4 2.5 %collective-permute-start.9 = (bf16[272,256]{1,0:T(8,128)(2,1)S(1)}, bf16[272,256]{1,0:T(8,128)(2,1)S(1)}, u32[]{:S(2)}, u32[]{:S(2)}) collective-permute-start(bf16[272,256]{1,0:T(8,128)(2,1)S(1)} %collective-permute-done.8.refs_2_.refs_6_), channel_id=1, source_target_pairs={{0,32},{32,0},{64,96},{96,64},{128,160},{160,128},{192,224},{224,1... | collective-permute-start | bytes 417800 | tf_op jit(solution)/shard_map/ppermute | solution.py:38
  28.2 2.1 %collective-permute-start.7 = (bf16[272,256]{1,0:T(8,128)(2,1)S(1)}, bf16[272,256]{1,0:T(8,128)(2,1)S(1)}, u32[]{:S(2)}, u32[]{:S(2)}) collective-permute-start(bf16[272,256]{1,0:T(8,128)(2,1)S(1)} %collective-permute-done.6.refs_0_.refs_4_), channel_id=1, source_target_pairs={{0,32},{32,0},{64,96},{96,64},{128,160},{160,128},{192,224},{224,1... | collective-permute-start | bytes 417800 | tf_op jit(solution)/shard_map/ppermute | solution.py:38
  29.9 23.7 %copy-start.1 = (bf16[256,576]{0,1:T(8,128)(2,1)S(1)}, bf16[256,576]{0,1:T(8,128)(2,1)}, u32[]{:S(2)}) copy-start(bf16[256,576]{0,1:T(8,128)(2,1)} %param.5) | copy-start | bytes 884740
  70.3 4.8 %collective-permute-start.13 = (bf16[256,256]{1,0:T(8,128)(2,1)S(1)}, bf16[256,256]{1,0:T(8,128)(2,1)S(1)}, u32[]{:S(2)}, u32[]{:S(2)}) collective-permute-start(bf16[256,256]{1,0:T(8,128)(2,1)S(1)} %get-tuple-element.50), channel_id=1, source_target_pairs={{0,32},{32,0},{64,96},{96,64},{128,160},{160,128},{192,224},{224,1... | collective-permute-start | bytes 393224 | tf_op jit(solution)/shard_map/ppermute | solution.py:38
  75.1 2.6 %collective-permute-start.14 = (bf16[768,256]{1,0:T(8,128)(2,1)S(1)}, bf16[768,256]{1,0:T(8,128)(2,1)S(1)}, u32[]{:S(2)}, u32[]{:S(2)}) collective-permute-start(bf16[768,256]{1,0:T(8,128)(2,1)S(1)} %back_send.1), channel_id=1, source_target_pairs={{0,32},{32,0},{64,96},{96,64},{128,160},{160,128},{192,224},{224,1... | collective-permute-start | bytes 1179656 | tf_op jit(solution)/shard_map/ppermute | solution.py:38
  75.6 6.4 %collective-permute-start.15 = (bf16[256,256]{1,0:T(8,128)(2,1)S(1)}, bf16[256,256]{1,0:T(8,128)(2,1)S(1)}, u32[]{:S(2)}, u32[]{:S(2)}) collective-permute-start(bf16[256,256]{1,0:T(8,128)(2,1)S(1)} %add_convert_fusion.2), channel_id=1, source_target_pairs={{0,128},{32,160},{64,192},{96,224},{128,0},{160,32},{192,64},{224,... | collective-permute-start | bytes 393224 | tf_op jit(solution)/shard_map/ppermute | solution.py:38
  77.9 6.3 %collective-permute-start.17 = (bf16[256,256]{1,0:T(8,128)(2,1)S(1)}, bf16[256,256]{1,0:T(8,128)(2,1)S(1)}, u32[]{:S(2)}, u32[]{:S(2)}) collective-permute-start(bf16[256,256]{1,0:T(8,128)(2,1)S(1)} %get-tuple-element.63), channel_id=1, source_target_pairs={{0,192},{32,224},{64,0},{96,32},{128,64},{160,96},{192,128},{224,1... | collective-permute-start | bytes 393224 | tf_op jit(solution)/shard_map/ppermute | solution.py:38
  78.9 5.7 %collective-permute-start.16 = (bf16[256,256]{1,0:T(8,128)(2,1)S(1)}, bf16[256,256]{1,0:T(8,128)(2,1)S(1)}, u32[]{:S(2)}, u32[]{:S(2)}) collective-permute-start(bf16[256,256]{1,0:T(8,128)(2,1)S(1)} %get-tuple-element.64), channel_id=1, source_target_pairs={{0,64},{32,96},{64,128},{96,160},{128,192},{160,224},{192,0},{224,... | collective-permute-start | bytes 393224 | tf_op jit(solution)/shard_map/ppermute | solution.py:38
  85.0 6.9 %collective-permute-start.23 = (bf16[272,256]{1,0:T(8,128)(2,1)S(1)}, bf16[272,256]{1,0:T(8,128)(2,1)S(1)}, u32[]{:S(2)}, u32[]{:S(2)}) collective-permute-start(bf16[272,256]{1,0:T(8,128)(2,1)S(1)} %own_gradient.1.refs_0_), channel_id=1, source_target_pairs={{0,128},{32,160},{64,192},{96,224},{128,0},{160,32},{192,64},{224,... | collective-permute-start | bytes 417800 | tf_op jit(solution)/shard_map/ppermute | solution.py:38
  87.9 7.4 %collective-permute-start.21 = (bf16[272,256]{1,0:T(8,128)(2,1)S(1)}, bf16[272,256]{1,0:T(8,128)(2,1)S(1)}, u32[]{:S(2)}, u32[]{:S(2)}) collective-permute-start(bf16[272,256]{1,0:T(8,128)(2,1)S(1)} %own_gradient.1.refs_0_), channel_id=1, source_target_pairs={{0,64},{32,96},{64,128},{96,160},{128,192},{160,224},{192,0},{224,... | collective-permute-start | bytes 417800 | tf_op jit(solution)/shard_map/ppermute | solution.py:38
  88.0 8.3 %collective-permute-start.19 = (bf16[272,256]{1,0:T(8,128)(2,1)S(1)}, bf16[272,256]{1,0:T(8,128)(2,1)S(1)}, u32[]{:S(2)}, u32[]{:S(2)}) collective-permute-start(bf16[272,256]{1,0:T(8,128)(2,1)S(1)} %own_gradient.1.refs_0_), channel_id=1, source_target_pairs={{0,192},{32,224},{64,0},{96,32},{128,64},{160,96},{192,128},{224,1... | collective-permute-start | bytes 417800 | tf_op jit(solution)/shard_map/ppermute | solution.py:38
  90.6 5.8 %collective-permute-start.18 = (bf16[272,256]{1,0:T(8,128)(2,1)S(1)}, bf16[272,256]{1,0:T(8,128)(2,1)S(1)}, u32[]{:S(2)}, u32[]{:S(2)}) collective-permute-start(bf16[272,256]{1,0:T(8,128)(2,1)S(1)} %own_gradient.1.refs_0_), channel_id=1, source_target_pairs={{0,32},{32,0},{64,96},{96,64},{128,160},{160,128},{192,224},{224,1... | collective-permute-start | bytes 417800 | tf_op jit(solution)/shard_map/ppermute | solution.py:38
  91.9 4.4 %collective-permute-start.24 = (bf16[272,256]{1,0:T(8,128)(2,1)S(1)}, bf16[272,256]{1,0:T(8,128)(2,1)S(1)}, u32[]{:S(2)}, u32[]{:S(2)}) collective-permute-start(bf16[272,256]{1,0:T(8,128)(2,1)S(1)} %collective-permute-done.23.refs_6_), channel_id=1, source_target_pairs={{0,32},{32,0},{64,96},{96,64},{128,160},{160,128},{192,224},{224,1... | collective-permute-start | bytes 417800 | tf_op jit(solution)/shard_map/ppermute | solution.py:38
  95.3 2.0 %collective-permute-start.22 = (bf16[272,256]{1,0:T(8,128)(2,1)S(1)}, bf16[272,256]{1,0:T(8,128)(2,1)S(1)}, u32[]{:S(2)}, u32[]{:S(2)}) collective-permute-start(bf16[272,256]{1,0:T(8,128)(2,1)S(1)} %collective-permute-done.21.refs_4_), channel_id=1, source_target_pairs={{0,32},{32,0},{64,96},{96,64},{128,160},{160,128},{192,224},{224,1... | collective-permute-start | bytes 417800 | tf_op jit(solution)/shard_map/ppermute | solution.py:38
  96.3 1.4 %collective-permute-start.20 = (bf16[272,256]{1,0:T(8,128)(2,1)S(1)}, bf16[272,256]{1,0:T(8,128)(2,1)S(1)}, u32[]{:S(2)}, u32[]{:S(2)}) collective-permute-start(bf16[272,256]{1,0:T(8,128)(2,1)S(1)} %collective-permute-done.19.refs_2_), channel_id=1, source_target_pairs={{0,32},{32,0},{64,96},{96,64},{128,160},{160,128},{192,224},{224,1... | collective-permute-start | bytes 417800 | tf_op jit(solution)/shard_map/ppermute | solution.py:38

commit v4 on v3

--- a/solution.py
+++ b/solution.py
@@ -172,10 +172,10 @@
         span = columns(owner(x + d, core))
         value = mine_ref[rows_of(d)] + other_ref[rows_of(d)]
         size = jnp.abs(value)
-        largest = jnp.maximum(jnp.max(size, axis=1, keepdims=True), 1e-30) * (1.0 + 2.0 ** -7)
+        largest = jnp.maximum(jnp.max(size, axis=1, keepdims=True), 1e-36) * (1.0 + 2.0 ** -7)
         largest = largest.astype(BF16).astype(F32)
         power = jnp.exp2(size * (SPAN / largest) - LOWEST)
-        out_ref[:TOK] = jnp.where(value < 0, -power, power).astype(BF16)
+        out_ref[:TOK] = jnp.where(value == 0, 0.0, jnp.where(value < 0, -power, power)).astype(BF16)
         scale = jnp.broadcast_to(largest, (TOK, 128)).T[:1]
         out_ref[TOK:] = stack_rows([scale] + pieces(square_ref[:1, span] + square_other_ref[:1, span], 3))
 
@@ -187,9 +187,9 @@
 def decode(ref):
     scale = jnp.broadcast_to(ref[TOK:TOK + 1].astype(F32), (128, TOK)).T[:, :1]
     power = ref[:TOK].astype(F32)
-    size = (jnp.log(jnp.abs(power)) * (1.0 / LN2) + LOWEST) * (scale * (1.0 / SPAN))
+    size = (jnp.log(jnp.maximum(jnp.abs(power), 2e-38)) * (1.0 / LN2) + LOWEST) * (scale * (1.0 / SPAN))
     rows = ref[TOK:].astype(F32)
-    return jnp.where(power < 0, -size, size), rows[1:2] + rows[2:3] + rows[3:4]
+    return jnp.where(power == 0, 0.0, jnp.where(power < 0, -size, size)), rows[1:2] + rows[2:3] + rows[3:4]
 
 
 def own_features(mine, other, parts, squares, latent_bias):

time: 99.8 us -> 99.7 us (level)
  no operation moved by 1% of the time
where the time goes in v4:
time: 99.7 us; the launch traced here: 99.6 us
  blocking collectives  38.5 us (39%)
  starting transfers between devices  34.9 us (35%)
  waiting for transfers between devices  13.1 us (13%)
  Pallas kernels  11.4 us (11%)
  between operations  1 us (1%)
    ppermute x25, starting transfers between devices, on_width(): return lax.ppermute(value, 'width', pairs)  34.9 us
    all_to_all x1, blocking collectives, shards(): parts = lax.all_to_all(parts, 'latent', 0, 0)  22.7 us
    all_to_all x1, blocking collectives, shards(): errors = lax.all_to_all(errors, 'latent', 0, 0).reshape(TOK, WIDE)  15.8 us
    ppermute x25, waiting for transfers between devices, on_width(): return lax.ppermute(value, 'width', pairs)  13.1 us
    pallas_call x17, Pallas kernels, call(): pl.pallas_call(body, in_specs=in_specs, out_specs=out_specs or [IN_VMEM]...  11.4 us
  transfers between devices with their start and end apart: 25, of which 11 were waited for; matrix products, arithmetic and copies ran while one was open for 1% of the time, Pallas kernels for 5%

profile of v4, /device:TPU:1, one launch (start us, length us, event | category | flops | bytes accessed | tf_op | source)
XLA Modules:
  0.0 99.6 jit_solution(18096552460864111472)
XLA Ops:
  0.6 2.1 %preact_far.1 = (f32[256,256]{1,0:T(8,128)S(1)}, f32[256,256]{1,0:T(8,128)S(1)}, bf16[256,576]{1,0:T(8,128)(2,1)S(1)}, bf16[576,2048]{1,0:T(8,128)(2,1)S(1)}) custom-call(bf16[576,256]{1,0:T(8,128)(2,1)} %bitcast.22, bf16[576,2048]{1,0:T(8,128)(2,1)} %enc_ref.1), custom_call_target="tpu_custom_call" | custom-call | flops 2400000000 | bytes 1114112 | tf_op jit(solution)/shard_map/preact_far/pallas_call | solution.py:50
  2.7 3.3 %collective-permute-start = (f32[256,256]{1,0:T(8,128)S(1)}, f32[256,256]{1,0:T(8,128)S(1)}, u32[]{:S(2)}, u32[]{:S(2)}) collective-permute-start(f32[256,256]{1,0:T(8,128)S(1)} %get-tuple-element.36), channel_id=1, source_target_pairs={{0,32},{32,0},{64,96},{96,64},{128,160},{160,128},{192,224},{224,1... | collective-permute-start | bytes 786440 | tf_op jit(solution)/shard_map/ppermute | solution.py:38
  6.0 0.1 square_sums.1.square_ref.refs_3_
  6.2 0.4 collective-permute-start.1
  6.6 0.5 preact_keep.1.mine_ref
  7.1 0.5 preact_send.1
  7.6 0.0 copy-start.2
  7.6 0.2 encode_sums.3
  7.8 0.3 collective-permute-start.2
  8.1 1.0 %collective-permute-start.3 = (bf16[272,256]{1,0:T(8,128)(2,1)S(1)}, bf16[272,256]{1,0:T(8,128)(2,1)S(1)}, u32[]{:S(2)}, u32[]{:S(2)}) collective-permute-start(bf16[272,256]{1,0:T(8,128)(2,1)S(1)} %encode_sums.3), channel_id=1, source_target_pairs={{0,128},{32,160},{64,192},{96,224},{128,0},{160,32},{192,64},{224,... | collective-permute-start | bytes 417800 | tf_op jit(solution)/shard_map/ppermute | solution.py:38
  9.1 1.0 %collective-permute-done.2.other_ref = f32[768,256]{1,0:T(8,128)S(1)} collective-permute-done((f32[768,256]{1,0:T(8,128)S(1)}, f32[768,256]{1,0:T(8,128)S(1)}, u32[]{:S(2)}, u32[]{:S(2)}) %collective-permute-start.2) | collective-permute-done | bytes 786464 | tf_op jit(solution)/shard_map/ppermute | solution.py:38
  10.2 0.2 encode_sums.4
  10.4 0.1 collective-permute-start.4
  10.5 0.2 encode_sums.5
  10.7 2.7 %collective-permute-start.5 = (bf16[272,256]{1,0:T(8,128)(2,1)S(1)}, bf16[272,256]{1,0:T(8,128)(2,1)S(1)}, u32[]{:S(2)}, u32[]{:S(2)}) collective-permute-start(bf16[272,256]{1,0:T(8,128)(2,1)S(1)} %encode_sums.5), channel_id=1, source_target_pairs={{0,192},{32,224},{64,0},{96,32},{128,64},{160,96},{192,128},{224,1... | collective-permute-start | bytes 417800 | tf_op jit(solution)/shard_map/ppermute | solution.py:38
  13.5 1.2 %collective-permute-done.3.refs_0_ = bf16[272,256]{1,0:T(8,128)(2,1)S(1)} collective-permute-done((bf16[272,256]{1,0:T(8,128)(2,1)S(1)}, bf16[272,256]{1,0:T(8,128)(2,1)S(1)}, u32[]{:S(2)}, u32[]{:S(2)}) %collective-permute-start.3) | collective-permute-done | bytes 139296 | tf_op jit(solution)/shard_map/ppermute | solution.py:38
  14.6 3.5 %collective-permute-done.4.refs_1_ = bf16[272,256]{1,0:T(8,128)(2,1)S(1)} collective-permute-done((bf16[272,256]{1,0:T(8,128)(2,1)S(1)}, bf16[272,256]{1,0:T(8,128)(2,1)S(1)}, u32[]{:S(2)}, u32[]{:S(2)}) %collective-permute-start.4) | collective-permute-done | bytes 139296 | tf_op jit(solution)/shard_map/ppermute | solution.py:38
  18.1 0.6 own_features.1
  18.7 1.2 %collective-permute-start.11 = (bf16[272,256]{1,0:T(8,128)(2,1)S(1)}, bf16[272,256]{1,0:T(8,128)(2,1)S(1)}, u32[]{:S(2)}, u32[]{:S(2)}) collective-permute-start(bf16[272,256]{1,0:T(8,128)(2,1)S(1)} %get-tuple-element.57.refs_0_.feat_ref), channel_id=1, source_target_pairs={{0,128},{32,160},{64,192},{96,224},{128,0},{160,32},{192,64},{224,... | collective-permute-start | bytes 417800 | tf_op jit(solution)/shard_map/ppermute | solution.py:38
  19.9 0.3 collective-permute-start.8
  20.3 1.1 %collective-permute-start.6 = (bf16[272,256]{1,0:T(8,128)(2,1)S(1)}, bf16[272,256]{1,0:T(8,128)(2,1)S(1)}, u32[]{:S(2)}, u32[]{:S(2)}) collective-permute-start(bf16[272,256]{1,0:T(8,128)(2,1)S(1)} %get-tuple-element.57.refs_0_.feat_ref), channel_id=1, source_target_pairs={{0,64},{32,96},{64,128},{96,160},{128,192},{160,224},{192,0},{224,... | collective-permute-start | bytes 417800 | tf_op jit(solution)/shard_map/ppermute | solution.py:38
  21.4 1.3 %collective-permute-start.10 = (bf16[272,256]{1,0:T(8,128)(2,1)S(1)}, bf16[272,256]{1,0:T(8,128)(2,1)S(1)}, u32[]{:S(2)}, u32[]{:S(2)}) collective-permute-start(bf16[272,256]{1,0:T(8,128)(2,1)S(1)} %get-tuple-element.57.refs_0_.feat_ref), channel_id=1, source_target_pairs={{0,32},{32,0},{64,96},{96,64},{128,160},{160,128},{192,224},{224,1... | collective-permute-start | bytes 417800 | tf_op jit(solution)/shard_map/ppermute | solution.py:38
  22.7 2.1 %collective-permute-done.11.refs_2_ = bf16[272,256]{1,0:T(8,128)(2,1)S(1)} collective-permute-done((bf16[272,256]{1,0:T(8,128)(2,1)S(1)}, bf16[272,256]{1,0:T(8,128)(2,1)S(1)}, u32[]{:S(2)}, u32[]{:S(2)}) %collective-permute-start.11) | collective-permute-done | bytes 139296 | tf_op jit(solution)/shard_map/ppermute | solution.py:38
  24.9 2.6 %collective-permute-start.12 = (bf16[272,256]{1,0:T(8,128)(2,1)S(1)}, bf16[272,256]{1,0:T(8,128)(2,1)S(1)}, u32[]{:S(2)}, u32[]{:S(2)}) collective-permute-start(bf16[272,256]{1,0:T(8,128)(2,1)S(1)} %collective-permute-done.11.refs_2_), channel_id=1, source_target_pairs={{0,32},{32,0},{64,96},{96,64},{128,160},{160,128},{192,224},{224,1... | collective-permute-start | bytes 417800 | tf_op jit(solution)/shard_map/ppermute | solution.py:38
  27.4 0.0 collective-permute-done.8.refs_2_.refs_6_
  27.5 0.8 collective-permute-start.9
  28.3 0.0 collective-permute-done.6.refs_0_.refs_4_
  28.3 1.0 %collective-permute-start.7 = (bf16[272,256]{1,0:T(8,128)(2,1)S(1)}, bf16[272,256]{1,0:T(8,128)(2,1)S(1)}, u32[]{:S(2)}, u32[]{:S(2)}) collective-permute-start(bf16[272,256]{1,0:T(8,128)(2,1)S(1)} %collective-permute-done.6.refs_0_.refs_4_), channel_id=1, source_target_pairs={{0,32},{32,0},{64,96},{96,64},{128,160},{160,128},{192,224},{224,1... | collective-permute-start | bytes 417800 | tf_op jit(solution)/shard_map/ppermute | solution.py:38
  29.3 0.0 collective-permute-done.12.refs_3_
  29.4 0.6 rebuild_first.1.refs_5_
  30.0 0.0 copy-start.1
  30.0 0.4 collective-permute-done.7.refs_1_.refs_5_
  30.3 0.6 rebuild_last.1
  30.9 22.7 %all_to_all.10.parts_ref = bf16[32,8,640]{2,1,0:T(8,128)(2,1)S(1)} all-to-all(bf16[32,8,640]{2,1,0:T(8,128)(2,1)S(1)} %bitcast.21), channel_id=1, replica_groups=mesh['width'=8,'latent'=32] {'latent'}, dimensions={0} | all-to-all | bytes 655360 | tf_op jit(solution)/shard_map/all_to_all | solution.py:388
  53.6 0.4 error_rows.1
  54.1 15.8 %all_to_all.11 = bf16[32,8,640]{2,1,0:T(8,128)(2,1)S(1)} all-to-all(bf16[32,8,640]{2,1,0:T(8,128)(2,1)S(1)} %error_rows.1), channel_id=1, replica_groups=mesh['width'=8,'latent'=32] {'latent'}, dimensions={0} | all-to-all | bytes 655360 | tf_op jit(solution)/shard_map/all_to_all | solution.py:390
  69.9 0.4 back_far.1
  70.2 3.8 %collective-permute-start.13 = (bf16[256,256]{1,0:T(8,128)(2,1)S(1)}, bf16[256,256]{1,0:T(8,128)(2,1)S(1)}, u32[]{:S(2)}, u32[]{:S(2)}) collective-permute-start(bf16[256,256]{1,0:T(8,128)(2,1)S(1)} %get-tuple-element.50), channel_id=1, source_target_pairs={{0,32},{32,0},{64,96},{96,64},{128,160},{160,128},{192,224},{224,1... | collective-permute-start | bytes 393224 | tf_op jit(solution)/shard_map/ppermute | solution.py:38
  74.0 0.5 back_send.1
  74.5 0.5 back_keep.1.mine_ref
  75.0 0.0 collective-permute-done.13
  75.1 0.4 collective-permute-start.14
  75.5 2.2 %collective-permute-start.15 = (bf16[256,256]{1,0:T(8,128)(2,1)S(1)}, bf16[256,256]{1,0:T(8,128)(2,1)S(1)}, u32[]{:S(2)}, u32[]{:S(2)}) collective-permute-start(bf16[256,256]{1,0:T(8,128)(2,1)S(1)} %add_convert_fusion.2), channel_id=1, source_target_pairs={{0,128},{32,160},{64,192},{96,224},{128,0},{160,32},{192,64},{224,... | collective-permute-start | bytes 393224 | tf_op jit(solution)/shard_map/ppermute | solution.py:38
  77.7 0.1 add_convert_fusion
  77.8 1.0 %collective-permute-start.17 = (bf16[256,256]{1,0:T(8,128)(2,1)S(1)}, bf16[256,256]{1,0:T(8,128)(2,1)S(1)}, u32[]{:S(2)}, u32[]{:S(2)}) collective-permute-start(bf16[256,256]{1,0:T(8,128)(2,1)S(1)} %get-tuple-element.63), channel_id=1, source_target_pairs={{0,192},{32,224},{64,0},{96,32},{128,64},{160,96},{192,128},{224,1... | collective-permute-start | bytes 393224 | tf_op jit(solution)/shard_map/ppermute | solution.py:38
  78.8 0.5 collective-permute-start.16
  79.3 1.9 %decoder_gradient.1 = (bf16[576,2048]{1,0:T(8,128)(2,1)}, f32[1,576]{1,0:T(1,128)S(1)}) custom-call(bf16[256,640]{1,0:T(8,128)(2,1)S(1)} %bitcast.19, bf16[272,256]{1,0:T(8,128)(2,1)S(1)} %get-tuple-element.57.refs_0_.feat_ref, bf16[272,256]{1,0:T(8,128)(2,1)S(1)} %collective-permute-done.10.refs_1_, bf16[272,256]{1,0:T(8,128)(2,1)S(1)} %collective-permute-done.11.refs_2_, ...), custom_call_target="tpu_custom_call" | custom-call | flops 603979776 | bytes 5767168 | tf_op jit(solution)/shard_map/decoder_gradient/pallas_call | solution.py:50
  81.3 0.6 reduce
  81.9 0.1 collective-permute-done.15.one_ref
  81.9 2.2 %collective-permute-done.17.three_ref = bf16[256,256]{1,0:T(8,128)(2,1)S(1)} collective-permute-done((bf16[256,256]{1,0:T(8,128)(2,1)S(1)}, bf16[256,256]{1,0:T(8,128)(2,1)S(1)}, u32[]{:S(2)}, u32[]{:S(2)}) %collective-permute-start.17) | collective-permute-done | bytes 131104 | tf_op jit(solution)/shard_map/ppermute | solution.py:38
  84.1 0.5 collective-permute-done.16.two_ref
  84.6 0.3 own_gradient.1.refs_0_
  84.9 2.9 %collective-permute-start.23 = (bf16[272,256]{1,0:T(8,128)(2,1)S(1)}, bf16[272,256]{1,0:T(8,128)(2,1)S(1)}, u32[]{:S(2)}, u32[]{:S(2)}) collective-permute-start(bf16[272,256]{1,0:T(8,128)(2,1)S(1)} %own_gradient.1.refs_0_), channel_id=1, source_target_pairs={{0,128},{32,160},{64,192},{96,224},{128,0},{160,32},{192,64},{224,... | collective-permute-start | bytes 417800 | tf_op jit(solution)/shard_map/ppermute | solution.py:38
  87.8 0.1 collective-permute-start.21
  87.9 2.6 %collective-permute-start.19 = (bf16[272,256]{1,0:T(8,128)(2,1)S(1)}, bf16[272,256]{1,0:T(8,128)(2,1)S(1)}, u32[]{:S(2)}, u32[]{:S(2)}) collective-permute-start(bf16[272,256]{1,0:T(8,128)(2,1)S(1)} %own_gradient.1.refs_0_), channel_id=1, source_target_pairs={{0,192},{32,224},{64,0},{96,32},{128,64},{160,96},{192,128},{224,1... | collective-permute-start | bytes 417800 | tf_op jit(solution)/shard_map/ppermute | solution.py:38
  90.5 1.3 %collective-permute-start.18 = (bf16[272,256]{1,0:T(8,128)(2,1)S(1)}, bf16[272,256]{1,0:T(8,128)(2,1)S(1)}, u32[]{:S(2)}, u32[]{:S(2)}) collective-permute-start(bf16[272,256]{1,0:T(8,128)(2,1)S(1)} %own_gradient.1.refs_0_), channel_id=1, source_target_pairs={{0,32},{32,0},{64,96},{96,64},{128,160},{160,128},{192,224},{224,1... | collective-permute-start | bytes 417800 | tf_op jit(solution)/shard_map/ppermute | solution.py:38
  91.8 2.6 %collective-permute-start.24 = (bf16[272,256]{1,0:T(8,128)(2,1)S(1)}, bf16[272,256]{1,0:T(8,128)(2,1)S(1)}, u32[]{:S(2)}, u32[]{:S(2)}) collective-permute-start(bf16[272,256]{1,0:T(8,128)(2,1)S(1)} %collective-permute-done.23.refs_6_), channel_id=1, source_target_pairs={{0,32},{32,0},{64,96},{96,64},{128,160},{160,128},{192,224},{224,1... | collective-permute-start | bytes 417800 | tf_op jit(solution)/shard_map/ppermute | solution.py:38
  94.4 0.8 collective-permute-done.21.refs_4_
  95.2 1.0 %collective-permute-start.22 = (bf16[272,256]{1,0:T(8,128)(2,1)S(1)}, bf16[272,256]{1,0:T(8,128)(2,1)S(1)}, u32[]{:S(2)}, u32[]{:S(2)}) collective-permute-start(bf16[272,256]{1,0:T(8,128)(2,1)S(1)} %collective-permute-done.21.refs_4_), channel_id=1, source_target_pairs={{0,32},{32,0},{64,96},{96,64},{128,160},{160,128},{192,224},{224,1... | collective-permute-start | bytes 417800 | tf_op jit(solution)/shard_map/ppermute | solution.py:38
  96.2 0.0 collective-permute-done.19.refs_2_
  96.2 0.0 collective-permute-start.20
  96.3 1.0 collective-permute-done.22.refs_5_
  97.2 0.4 collective-permute-done.20.refs_3_
  97.6 1.8 %encoder_gradient.1 = (bf16[576,2048]{1,0:T(8,128)(2,1)}, f32[1,2048]{1,0:T(1,128)}, f32[1,128]{1,0:T(1,128)}) custom-call(bf16[576,256]{1,0:T(8,128)(2,1)S(1)} %bitcast.24, bf16[272,256]{1,0:T(8,128)(2,1)S(1)} %own_gradient.1.refs_0_, bf16[272,256]{1,0:T(8,128)(2,1)S(1)} %collective-permute-done.18.refs_1_, ...), custom_call_target="tpu_custom_call" | custom-call | flops 603979776 | bytes 3407872 | tf_op jit(solution)/shard_map/encoder_gradient/pallas_call | solution.py:50
  (17 shorter events, 0.1 us)
Async XLA Ops:
  0.6 5.4 %copy-start = (bf16[2048,576]{0,1:T(8,128)(2,1)S(1)}, bf16[2048,576]{0,1:T(8,128)(2,1)}, u32[]{:S(2)}) copy-start(bf16[2048,576]{0,1:T(8,128)(2,1)} %param.8) | copy-start | bytes 7077892
  2.7 4.9 %collective-permute-start = (f32[256,256]{1,0:T(8,128)S(1)}, f32[256,256]{1,0:T(8,128)S(1)}, u32[]{:S(2)}, u32[]{:S(2)}) collective-permute-start(f32[256,256]{1,0:T(8,128)S(1)} %get-tuple-element.36), channel_id=1, source_target_pairs={{0,32},{32,0},{64,96},{96,64},{128,160},{160,128},{192,224},{224,1... | collective-permute-start | bytes 786440 | tf_op jit(solution)/shard_map/ppermute | solution.py:38
  6.2 1.4 %collective-permute-start.1 = (f32[8,2048]{1,0:T(8,128)S(1)}, f32[8,2048]{1,0:T(8,128)S(1)}, u32[]{:S(2)}, u32[]{:S(2)}) collective-permute-start(f32[8,2048]{1,0:T(8,128)S(1)} %square_sums.1.square_ref.refs_3_), channel_id=1, source_target_pairs={{0,32},{32,0},{64,96},{96,64},{128,160},{160,128},{192,224},{224,1... | collective-permute-start | bytes 196616 | tf_op jit(solution)/shard_map/ppermute | solution.py:38
  7.6 10.5 %copy-start.2 = (f32[2048]{0:T(1024)S(1)}, f32[2048]{0:T(1024)}, u32[]{:S(2)}) copy-start(f32[2048]{0:T(1024)} %param.7) | copy-start | bytes 24580
  7.8 2.4 %collective-permute-start.2 = (f32[768,256]{1,0:T(8,128)S(1)}, f32[768,256]{1,0:T(8,128)S(1)}, u32[]{:S(2)}, u32[]{:S(2)}) collective-permute-start(f32[768,256]{1,0:T(8,128)S(1)} %preact_send.1), channel_id=1, source_target_pairs={{0,32},{32,0},{64,96},{96,64},{128,160},{160,128},{192,224},{224,1... | collective-permute-start | bytes 2359304 | tf_op jit(solution)/shard_map/ppermute | solution.py:38
  8.1 6.5 %collective-permute-start.3 = (bf16[272,256]{1,0:T(8,128)(2,1)S(1)}, bf16[272,256]{1,0:T(8,128)(2,1)S(1)}, u32[]{:S(2)}, u32[]{:S(2)}) collective-permute-start(bf16[272,256]{1,0:T(8,128)(2,1)S(1)} %encode_sums.3), channel_id=1, source_target_pairs={{0,128},{32,160},{64,192},{96,224},{128,0},{160,32},{192,64},{224,... | collective-permute-start | bytes 417800 | tf_op jit(solution)/shard_map/ppermute | solution.py:38
  10.4 18.9 %copy-start.3 = (f32[576]{0:T(1024)S(1)}, f32[576]{0:T(1024)}, u32[]{:S(2)}) copy-start(f32[576]{0:T(1024)} %param.9) | copy-start | bytes 6916
  10.4 7.7 %collective-permute-start.4 = (bf16[272,256]{1,0:T(8,128)(2,1)S(1)}, bf16[272,256]{1,0:T(8,128)(2,1)S(1)}, u32[]{:S(2)}, u32[]{:S(2)}) collective-permute-start(bf16[272,256]{1,0:T(8,128)(2,1)S(1)} %encode_sums.4), channel_id=1, source_target_pairs={{0,64},{32,96},{64,128},{96,160},{128,192},{160,224},{192,0},{224,... | collective-permute-start | bytes 417800 | tf_op jit(solution)/shard_map/ppermute | solution.py:38
  10.7 7.4 %collective-permute-start.5 = (bf16[272,256]{1,0:T(8,128)(2,1)S(1)}, bf16[272,256]{1,0:T(8,128)(2,1)S(1)}, u32[]{:S(2)}, u32[]{:S(2)}) collective-permute-start(bf16[272,256]{1,0:T(8,128)(2,1)S(1)} %encode_sums.5), channel_id=1, source_target_pairs={{0,192},{32,224},{64,0},{96,32},{128,64},{160,96},{192,128},{224,1... | collective-permute-start | bytes 417800 | tf_op jit(solution)/shard_map/ppermute | solution.py:38
  18.7 6.2 %collective-permute-start.11 = (bf16[272,256]{1,0:T(8,128)(2,1)S(1)}, bf16[272,256]{1,0:T(8,128)(2,1)S(1)}, u32[]{:S(2)}, u32[]{:S(2)}) collective-permute-start(bf16[272,256]{1,0:T(8,128)(2,1)S(1)} %get-tuple-element.57.refs_0_.feat_ref), channel_id=1, source_target_pairs={{0,128},{32,160},{64,192},{96,224},{128,0},{160,32},{192,64},{224,... | collective-permute-start | bytes 417800 | tf_op jit(solution)/shard_map/ppermute | solution.py:38
  19.9 7.5 %collective-permute-start.8 = (bf16[272,256]{1,0:T(8,128)(2,1)S(1)}, bf16[272,256]{1,0:T(8,128)(2,1)S(1)}, u32[]{:S(2)}, u32[]{:S(2)}) collective-permute-start(bf16[272,256]{1,0:T(8,128)(2,1)S(1)} %get-tuple-element.57.refs_0_.feat_ref), channel_id=1, source_target_pairs={{0,192},{32,224},{64,0},{96,32},{128,64},{160,96},{192,128},{224,1... | collective-permute-start | bytes 417800 | tf_op jit(solution)/shard_map/ppermute | solution.py:38
  20.3 8.1 %collective-permute-start.6 = (bf16[272,256]{1,0:T(8,128)(2,1)S(1)}, bf16[272,256]{1,0:T(8,128)(2,1)S(1)}, u32[]{:S(2)}, u32[]{:S(2)}) collective-permute-start(bf16[272,256]{1,0:T(8,128)(2,1)S(1)} %get-tuple-element.57.refs_0_.feat_ref), channel_id=1, source_target_pairs={{0,64},{32,96},{64,128},{96,160},{128,192},{160,224},{192,0},{224,... | collective-permute-start | bytes 417800 | tf_op jit(solution)/shard_map/ppermute | solution.py:38
  21.4 8.0 %collective-permute-start.10 = (bf16[272,256]{1,0:T(8,128)(2,1)S(1)}, bf16[272,256]{1,0:T(8,128)(2,1)S(1)}, u32[]{:S(2)}, u32[]{:S(2)}) collective-permute-start(bf16[272,256]{1,0:T(8,128)(2,1)S(1)} %get-tuple-element.57.refs_0_.feat_ref), channel_id=1, source_target_pairs={{0,32},{32,0},{64,96},{96,64},{128,160},{160,128},{192,224},{224,1... | collective-permute-start | bytes 417800 | tf_op jit(solution)/shard_map/ppermute | solution.py:38
  24.9 4.5 %collective-permute-start.12 = (bf16[272,256]{1,0:T(8,128)(2,1)S(1)}, bf16[272,256]{1,0:T(8,128)(2,1)S(1)}, u32[]{:S(2)}, u32[]{:S(2)}) collective-permute-start(bf16[272,256]{1,0:T(8,128)(2,1)S(1)} %collective-permute-done.11.refs_2_), channel_id=1, source_target_pairs={{0,32},{32,0},{64,96},{96,64},{128,160},{160,128},{192,224},{224,1... | collective-permute-start | bytes 417800 | tf_op jit(solution)/shard_map/ppermute | solution.py:38
  27.5 2.5 %collective-permute-start.9 = (bf16[272,256]{1,0:T(8,128)(2,1)S(1)}, bf16[272,256]{1,0:T(8,128)(2,1)S(1)}, u32[]{:S(2)}, u32[]{:S(2)}) collective-permute-start(bf16[272,256]{1,0:T(8,128)(2,1)S(1)} %collective-permute-done.8.refs_2_.refs_6_), channel_id=1, source_target_pairs={{0,32},{32,0},{64,96},{96,64},{128,160},{160,128},{192,224},{224,1... | collective-permute-start | bytes 417800 | tf_op jit(solution)/shard_map/ppermute | solution.py:38
  28.3 2.0 %collective-permute-start.7 = (bf16[272,256]{1,0:T(8,128)(2,1)S(1)}, bf16[272,256]{1,0:T(8,128)(2,1)S(1)}, u32[]{:S(2)}, u32[]{:S(2)}) collective-permute-start(bf16[272,256]{1,0:T(8,128)(2,1)S(1)} %collective-permute-done.6.refs_0_.refs_4_), channel_id=1, source_target_pairs={{0,32},{32,0},{64,96},{96,64},{128,160},{160,128},{192,224},{224,1... | collective-permute-start | bytes 417800 | tf_op jit(solution)/shard_map/ppermute | solution.py:38
  30.0 23.7 %copy-start.1 = (bf16[256,576]{0,1:T(8,128)(2,1)S(1)}, bf16[256,576]{0,1:T(8,128)(2,1)}, u32[]{:S(2)}) copy-start(bf16[256,576]{0,1:T(8,128)(2,1)} %param.5) | copy-start | bytes 884740
  70.2 4.8 %collective-permute-start.13 = (bf16[256,256]{1,0:T(8,128)(2,1)S(1)}, bf16[256,256]{1,0:T(8,128)(2,1)S(1)}, u32[]{:S(2)}, u32[]{:S(2)}) collective-permute-start(bf16[256,256]{1,0:T(8,128)(2,1)S(1)} %get-tuple-element.50), channel_id=1, source_target_pairs={{0,32},{32,0},{64,96},{96,64},{128,160},{160,128},{192,224},{224,1... | collective-permute-start | bytes 393224 | tf_op jit(solution)/shard_map/ppermute | solution.py:38
  75.1 2.6 %collective-permute-start.14 = (bf16[768,256]{1,0:T(8,128)(2,1)S(1)}, bf16[768,256]{1,0:T(8,128)(2,1)S(1)}, u32[]{:S(2)}, u32[]{:S(2)}) collective-permute-start(bf16[768,256]{1,0:T(8,128)(2,1)S(1)} %back_send.1), channel_id=1, source_target_pairs={{0,32},{32,0},{64,96},{96,64},{128,160},{160,128},{192,224},{224,1... | collective-permute-start | bytes 1179656 | tf_op jit(solution)/shard_map/ppermute | solution.py:38
  75.5 6.4 %collective-permute-start.15 = (bf16[256,256]{1,0:T(8,128)(2,1)S(1)}, bf16[256,256]{1,0:T(8,128)(2,1)S(1)}, u32[]{:S(2)}, u32[]{:S(2)}) collective-permute-start(bf16[256,256]{1,0:T(8,128)(2,1)S(1)} %add_convert_fusion.2), channel_id=1, source_target_pairs={{0,128},{32,160},{64,192},{96,224},{128,0},{160,32},{192,64},{224,... | collective-permute-start | bytes 393224 | tf_op jit(solution)/shard_map/ppermute | solution.py:38
  77.8 6.3 %collective-permute-start.17 = (bf16[256,256]{1,0:T(8,128)(2,1)S(1)}, bf16[256,256]{1,0:T(8,128)(2,1)S(1)}, u32[]{:S(2)}, u32[]{:S(2)}) collective-permute-start(bf16[256,256]{1,0:T(8,128)(2,1)S(1)} %get-tuple-element.63), channel_id=1, source_target_pairs={{0,192},{32,224},{64,0},{96,32},{128,64},{160,96},{192,128},{224,1... | collective-permute-start | bytes 393224 | tf_op jit(solution)/shard_map/ppermute | solution.py:38
  78.8 5.8 %collective-permute-start.16 = (bf16[256,256]{1,0:T(8,128)(2,1)S(1)}, bf16[256,256]{1,0:T(8,128)(2,1)S(1)}, u32[]{:S(2)}, u32[]{:S(2)}) collective-permute-start(bf16[256,256]{1,0:T(8,128)(2,1)S(1)} %get-tuple-element.64), channel_id=1, source_target_pairs={{0,64},{32,96},{64,128},{96,160},{128,192},{160,224},{192,0},{224,... | collective-permute-start | bytes 393224 | tf_op jit(solution)/shard_map/ppermute | solution.py:38
  84.9 7.0 %collective-permute-start.23 = (bf16[272,256]{1,0:T(8,128)(2,1)S(1)}, bf16[272,256]{1,0:T(8,128)(2,1)S(1)}, u32[]{:S(2)}, u32[]{:S(2)}) collective-permute-start(bf16[272,256]{1,0:T(8,128)(2,1)S(1)} %own_gradient.1.refs_0_), channel_id=1, source_target_pairs={{0,128},{32,160},{64,192},{96,224},{128,0},{160,32},{192,64},{224,... | collective-permute-start | bytes 417800 | tf_op jit(solution)/shard_map/ppermute | solution.py:38
  87.8 7.4 %collective-permute-start.21 = (bf16[272,256]{1,0:T(8,128)(2,1)S(1)}, bf16[272,256]{1,0:T(8,128)(2,1)S(1)}, u32[]{:S(2)}, u32[]{:S(2)}) collective-permute-start(bf16[272,256]{1,0:T(8,128)(2,1)S(1)} %own_gradient.1.refs_0_), channel_id=1, source_target_pairs={{0,64},{32,96},{64,128},{96,160},{128,192},{160,224},{192,0},{224,... | collective-permute-start | bytes 417800 | tf_op jit(solution)/shard_map/ppermute | solution.py:38
  87.9 8.3 %collective-permute-start.19 = (bf16[272,256]{1,0:T(8,128)(2,1)S(1)}, bf16[272,256]{1,0:T(8,128)(2,1)S(1)}, u32[]{:S(2)}, u32[]{:S(2)}) collective-permute-start(bf16[272,256]{1,0:T(8,128)(2,1)S(1)} %own_gradient.1.refs_0_), channel_id=1, source_target_pairs={{0,192},{32,224},{64,0},{96,32},{128,64},{160,96},{192,128},{224,1... | collective-permute-start | bytes 417800 | tf_op jit(solution)/shard_map/ppermute | solution.py:38
  90.5 5.8 %collective-permute-start.18 = (bf16[272,256]{1,0:T(8,128)(2,1)S(1)}, bf16[272,256]{1,0:T(8,128)(2,1)S(1)}, u32[]{:S(2)}, u32[]{:S(2)}) collective-permute-start(bf16[272,256]{1,0:T(8,128)(2,1)S(1)} %own_gradient.1.refs_0_), channel_id=1, source_target_pairs={{0,32},{32,0},{64,96},{96,64},{128,160},{160,128},{192,224},{224,1... | collective-permute-start | bytes 417800 | tf_op jit(solution)/shard_map/ppermute | solution.py:38
  91.8 4.4 %collective-permute-start.24 = (bf16[272,256]{1,0:T(8,128)(2,1)S(1)}, bf16[272,256]{1,0:T(8,128)(2,1)S(1)}, u32[]{:S(2)}, u32[]{:S(2)}) collective-permute-start(bf16[272,256]{1,0:T(8,128)(2,1)S(1)} %collective-permute-done.23.refs_6_), channel_id=1, source_target_pairs={{0,32},{32,0},{64,96},{96,64},{128,160},{160,128},{192,224},{224,1... | collective-permute-start | bytes 417800 | tf_op jit(solution)/shard_map/ppermute | solution.py:38
  95.2 2.0 %collective-permute-start.22 = (bf16[272,256]{1,0:T(8,128)(2,1)S(1)}, bf16[272,256]{1,0:T(8,128)(2,1)S(1)}, u32[]{:S(2)}, u32[]{:S(2)}) collective-permute-start(bf16[272,256]{1,0:T(8,128)(2,1)S(1)} %collective-permute-done.21.refs_4_), channel_id=1, source_target_pairs={{0,32},{32,0},{64,96},{96,64},{128,160},{160,128},{192,224},{224,1... | collective-permute-start | bytes 417800 | tf_op jit(solution)/shard_map/ppermute | solution.py:38
  96.2 1.4 %collective-permute-start.20 = (bf16[272,256]{1,0:T(8,128)(2,1)S(1)}, bf16[272,256]{1,0:T(8,128)(2,1)S(1)}, u32[]{:S(2)}, u32[]{:S(2)}) collective-permute-start(bf16[272,256]{1,0:T(8,128)(2,1)S(1)} %collective-permute-done.19.refs_2_), channel_id=1, source_target_pairs={{0,32},{32,0},{64,96},{96,64},{128,160},{160,128},{192,224},{224,1... | collective-permute-start | bytes 417800 | tf_op jit(solution)/shard_map/ppermute | solution.py:38

commit v5 on v4

--- a/solution.py
+++ b/solution.py
@@ -107,15 +107,29 @@
 
 
 def back_far(errors, dec_t):
-    def body(errors_ref, dec_ref, send_ref, keep_ref):
+    def body(errors_ref, dec_ref, send_ref):
+        x, core = place()
+        span = columns(owner(x + FAR, 1 - core))
+        send_ref[...] = dot(errors_ref[:, :COL], dec_ref[:, span], ((1,), (0,))).astype(BF16)
+
+    return call(
+        body, "back_far", (errors, dec_t), [IN_VMEM] * 2, [((TOK, CHUNK), BF16)],
+        flops=2 * TOK * COL * CHUNK, moved=2 * COL * CHUNK + 2 * TOK * CHUNK,
+    )[0]
+
+
+def back_keep(errors, dec_t):
+    def body(errors_ref, dec_ref, far_ref, out_ref):
         x, core = place()
         value = errors_ref[:, :COL]
-        send_ref[...] = dot(value, dec_ref[:, columns(owner(x + FAR, 1 - core))], ((1,), (0,))).astype(BF16)
-        keep_ref[...] = dot(value, dec_ref[:, columns(owner(x + FAR, core))], ((1,), (0,)))
-
-    return call(
-        body, "back_far", (errors, dec_t), [IN_VMEM] * 2, [((TOK, CHUNK), BF16), ((TOK, CHUNK), F32)],
-        flops=4 * TOK * COL * CHUNK, moved=4 * COL * CHUNK + 6 * TOK * CHUNK,
+        far_ref[...] = dot(value, dec_ref[:, columns(owner(x + FAR, core))], ((1,), (0,)))
+        for k, d in enumerate(REST):
+            part = dot(value, dec_ref[:, columns(owner(x + d, core))], ((1,), (0,)))
+            out_ref[k * TOK:(k + 1) * TOK] = part
+
+    return call(
+        body, "back_keep", (errors, dec_t), [IN_VMEM] * 2, [((TOK, CHUNK), F32), ((3 * TOK, CHUNK), F32)],
+        flops=8 * TOK * COL * CHUNK, moved=8 * COL * CHUNK + 16 * TOK * CHUNK,
     )
 
 
@@ -249,15 +263,21 @@
     )[0]
 
 
-def error_rows(parts, act_t, output_bias):
-    def body(parts_ref, act_ref, bias_ref, out_ref):
+def offset_rows(act_t, output_bias):
+    def body(act_ref, bias_ref, out_ref):
         first = lax.axis_index("latent") * 8
         token = lax.broadcasted_iota(jnp.int32, (8, TOK), 1)
         wanted = lax.broadcasted_iota(jnp.int32, (8, TOK), 0) + first
         pick = jnp.where(token == wanted, 1.0, 0.0).astype(BF16)
-        act = dot(pick, act_ref[...], ((1,), (1,)))
+        out_ref[...] = bias_ref[...] - dot(pick, act_ref[...], ((1,), (1,)))
+
+    return call(body, "offset_rows", (act_t, output_bias), [IN_VMEM] * 2, [((8, COL), F32)], moved=2 * TOK * COL)[0]
+
+
+def error_rows(parts, offset):
+    def body(parts_ref, offset_ref, out_ref):
         total = jnp.sum(parts_ref[...].astype(F32), axis=0)
-        errors = total[:, :COL] + bias_ref[...] - act
+        errors = total[:, :COL] + offset_ref[...]
         loss = 0.5 * jnp.sum(errors * errors, axis=1, keepdims=True) + SPARSITY * total[:, COL:COL + 1]
         lane = lax.broadcasted_iota(jnp.int32, (8, WIDE - COL), 1)
         tail = jnp.zeros((8, WIDE - COL), F32)
@@ -267,7 +287,7 @@
         out_ref[:, :, COL:] = jnp.broadcast_to(tail.astype(BF16)[None], (32, 8, WIDE - COL))
 
     return call(
-        body, "error_rows", (parts, act_t, output_bias), [IN_VMEM] * 3, [((32, 8, WIDE), BF16)], moved=4 * TOK * WIDE
+        body, "error_rows", (parts, offset), [IN_VMEM] * 2, [((32, 8, WIDE), BF16)], moved=4 * TOK * WIDE
     )[0]
 
 
@@ -384,16 +404,16 @@
     feature_chunks = gather_chunks(features, HOPS)
     partial = rebuild_first(feature_chunks[:FIRST_REBUILD], dec_t, own_weights)
     parts = rebuild_last(feature_chunks[FIRST_REBUILD:], dec_t, partial).reshape(32, 8, WIDE)
-    parts, bias_row = lax.optimization_barrier((parts, output_bias[None, :]))
+    parts, offset = lax.optimization_barrier((parts, offset_rows(act_t, output_bias[None, :])))
     parts = lax.all_to_all(parts, "latent", 0, 0)
-    errors = error_rows(parts, act_t, bias_row)
+    errors = error_rows(parts, offset)
     errors = lax.all_to_all(errors, "latent", 0, 0).reshape(TOK, WIDE)
 
-    send, keep_far = back_far(errors, dec_t)
-    send, keep_far, errors = lax.optimization_barrier((send, keep_far, errors))
+    send = back_far(errors, dec_t)
+    send, errors = lax.optimization_barrier((send, errors))
+    keep_far, keep = back_keep(errors, dec_t)
     summed = keep_far + on_width(send, CORE_SWAP).astype(F32)
     send = rest_parts(errors, dec_t, True, BF16, "back_send")
-    keep = rest_parts(errors, dec_t, False, F32, "back_keep")
     summed, send, keep = lax.optimization_barrier((summed.astype(BF16), send, keep))
     summed = [on_width(summed, x_shift(FAR))]
     rest = (keep, on_width(send, CORE_SWAP))

time: 99.7 us -> 99.4 us (level)
    pallas_call x17 -> x18, Pallas kernels: 11.4 us -> 11.4 us  [call(): pl.pallas_call(body, in_specs=in_specs, out_specs=out_specs or [IN_VMEM]...]
  transfers between devices with their start and end apart: 25 -> 25, of which waited for: 11 -> 10; matrix products, arithmetic and copies ran while one was open for 1% -> 1% of each run, Pallas kernels for 5% -> 5%
where the time goes in v5:
time: 99.4 us; the launch traced here: 99.3 us
  blocking collectives  38.5 us (39%)
  starting transfers between devices  35 us (35%)
  waiting for transfers between devices  12.7 us (13%)
  Pallas kernels  11.4 us (11%)
  between operations  1 us (1%)
    ppermute x25, starting transfers between devices, on_width(): return lax.ppermute(value, 'width', pairs)  35 us
    all_to_all x1, blocking collectives, shards(): parts = lax.all_to_all(parts, 'latent', 0, 0)  22.7 us
    all_to_all x1, blocking collectives, shards(): errors = lax.all_to_all(errors, 'latent', 0, 0).reshape(TOK, WIDE)  15.8 us
    ppermute x25, waiting for transfers between devices, on_width(): return lax.ppermute(value, 'width', pairs)  12.7 us
    pallas_call x18, Pallas kernels, call(): pl.pallas_call(body, in_specs=in_specs, out_specs=out_specs or [IN_VMEM]...  11.4 us
  transfers between devices with their start and end apart: 25, of which 10 were waited for; matrix products, arithmetic and copies ran while one was open for 1% of the time, Pallas kernels for 5%

profile of v5, /device:TPU:1, one launch (start us, length us, event | category | flops | bytes accessed | tf_op | source)
XLA Modules:
  0.0 99.3 jit_solution(12409690284559805603)
XLA Ops:
  0.6 2.1 %preact_far.1 = (f32[256,256]{1,0:T(8,128)S(1)}, f32[256,256]{1,0:T(8,128)S(1)}, bf16[256,576]{1,0:T(8,128)(2,1)S(1)}, bf16[576,2048]{1,0:T(8,128)(2,1)S(1)}) custom-call(bf16[576,256]{1,0:T(8,128)(2,1)} %bitcast.22, bf16[576,2048]{1,0:T(8,128)(2,1)} %enc_ref.1), custom_call_target="tpu_custom_call" | custom-call | flops 2400000000 | bytes 1114112 | tf_op jit(solution)/shard_map/preact_far/pallas_call | solution.py:50
  2.7 3.3 %collective-permute-start = (f32[256,256]{1,0:T(8,128)S(1)}, f32[256,256]{1,0:T(8,128)S(1)}, u32[]{:S(2)}, u32[]{:S(2)}) collective-permute-start(f32[256,256]{1,0:T(8,128)S(1)} %get-tuple-element.35), channel_id=1, source_target_pairs={{0,32},{32,0},{64,96},{96,64},{128,160},{160,128},{192,224},{224,1... | collective-permute-start | bytes 786440 | tf_op jit(solution)/shard_map/ppermute | solution.py:38
  6.0 0.1 square_sums.1.square_ref.refs_3_
  6.2 0.4 collective-permute-start.1
  6.6 0.5 preact_keep.1.mine_ref
  7.1 0.5 preact_send.1
  7.6 0.0 copy-start.2
  7.6 0.0 collective-permute-done.1.square_other_ref.refs_4_
  7.6 0.2 encode_sums.3
  7.8 0.3 collective-permute-start.2
  8.1 1.0 %collective-permute-start.3 = (bf16[272,256]{1,0:T(8,128)(2,1)S(1)}, bf16[272,256]{1,0:T(8,128)(2,1)S(1)}, u32[]{:S(2)}, u32[]{:S(2)}) collective-permute-start(bf16[272,256]{1,0:T(8,128)(2,1)S(1)} %encode_sums.3), channel_id=1, source_target_pairs={{0,128},{32,160},{64,192},{96,224},{128,0},{160,32},{192,64},{224,... | collective-permute-start | bytes 417800 | tf_op jit(solution)/shard_map/ppermute | solution.py:38
  9.1 1.0 %collective-permute-done.2.other_ref = f32[768,256]{1,0:T(8,128)S(1)} collective-permute-done((f32[768,256]{1,0:T(8,128)S(1)}, f32[768,256]{1,0:T(8,128)S(1)}, u32[]{:S(2)}, u32[]{:S(2)}) %collective-permute-start.2) | collective-permute-done | bytes 786464 | tf_op jit(solution)/shard_map/ppermute | solution.py:38
  10.2 0.2 encode_sums.4
  10.4 0.0 copy-start.1
  10.4 0.1 collective-permute-start.4
  10.5 0.2 encode_sums.5
  10.7 2.7 %collective-permute-start.5 = (bf16[272,256]{1,0:T(8,128)(2,1)S(1)}, bf16[272,256]{1,0:T(8,128)(2,1)S(1)}, u32[]{:S(2)}, u32[]{:S(2)}) collective-permute-start(bf16[272,256]{1,0:T(8,128)(2,1)S(1)} %encode_sums.5), channel_id=1, source_target_pairs={{0,192},{32,224},{64,0},{96,32},{128,64},{160,96},{192,128},{224,1... | collective-permute-start | bytes 417800 | tf_op jit(solution)/shard_map/ppermute | solution.py:38
  13.5 1.2 %collective-permute-done.3.refs_0_ = bf16[272,256]{1,0:T(8,128)(2,1)S(1)} collective-permute-done((bf16[272,256]{1,0:T(8,128)(2,1)S(1)}, bf16[272,256]{1,0:T(8,128)(2,1)S(1)}, u32[]{:S(2)}, u32[]{:S(2)}) %collective-permute-start.3) | collective-permute-done | bytes 139296 | tf_op jit(solution)/shard_map/ppermute | solution.py:38
  14.6 3.5 %collective-permute-done.4.refs_1_ = bf16[272,256]{1,0:T(8,128)(2,1)S(1)} collective-permute-done((bf16[272,256]{1,0:T(8,128)(2,1)S(1)}, bf16[272,256]{1,0:T(8,128)(2,1)S(1)}, u32[]{:S(2)}, u32[]{:S(2)}) %collective-permute-start.4) | collective-permute-done | bytes 139296 | tf_op jit(solution)/shard_map/ppermute | solution.py:38
  18.1 0.0 collective-permute-done.5.refs_2_
  18.1 0.6 own_features.1
  18.7 1.2 %collective-permute-start.11 = (bf16[272,256]{1,0:T(8,128)(2,1)S(1)}, bf16[272,256]{1,0:T(8,128)(2,1)S(1)}, u32[]{:S(2)}, u32[]{:S(2)}) collective-permute-start(bf16[272,256]{1,0:T(8,128)(2,1)S(1)} %get-tuple-element.55.refs_0_.feat_ref), channel_id=1, source_target_pairs={{0,128},{32,160},{64,192},{96,224},{128,0},{160,32},{192,64},{224,... | collective-permute-start | bytes 417800 | tf_op jit(solution)/shard_map/ppermute | solution.py:38
  19.9 0.3 collective-permute-start.8
  20.2 1.1 %collective-permute-start.6 = (bf16[272,256]{1,0:T(8,128)(2,1)S(1)}, bf16[272,256]{1,0:T(8,128)(2,1)S(1)}, u32[]{:S(2)}, u32[]{:S(2)}) collective-permute-start(bf16[272,256]{1,0:T(8,128)(2,1)S(1)} %get-tuple-element.55.refs_0_.feat_ref), channel_id=1, source_target_pairs={{0,64},{32,96},{64,128},{96,160},{128,192},{160,224},{192,0},{224,... | collective-permute-start | bytes 417800 | tf_op jit(solution)/shard_map/ppermute | solution.py:38
  21.4 1.3 %collective-permute-start.10 = (bf16[272,256]{1,0:T(8,128)(2,1)S(1)}, bf16[272,256]{1,0:T(8,128)(2,1)S(1)}, u32[]{:S(2)}, u32[]{:S(2)}) collective-permute-start(bf16[272,256]{1,0:T(8,128)(2,1)S(1)} %get-tuple-element.55.refs_0_.feat_ref), channel_id=1, source_target_pairs={{0,32},{32,0},{64,96},{96,64},{128,160},{160,128},{192,224},{224,1... | collective-permute-start | bytes 417800 | tf_op jit(solution)/shard_map/ppermute | solution.py:38
  22.7 2.1 %collective-permute-done.11.refs_2_ = bf16[272,256]{1,0:T(8,128)(2,1)S(1)} collective-permute-done((bf16[272,256]{1,0:T(8,128)(2,1)S(1)}, bf16[272,256]{1,0:T(8,128)(2,1)S(1)}, u32[]{:S(2)}, u32[]{:S(2)}) %collective-permute-start.11) | collective-permute-done | bytes 139296 | tf_op jit(solution)/shard_map/ppermute | solution.py:38
  24.8 2.6 %collective-permute-start.12 = (bf16[272,256]{1,0:T(8,128)(2,1)S(1)}, bf16[272,256]{1,0:T(8,128)(2,1)S(1)}, u32[]{:S(2)}, u32[]{:S(2)}) collective-permute-start(bf16[272,256]{1,0:T(8,128)(2,1)S(1)} %collective-permute-done.11.refs_2_), channel_id=1, source_target_pairs={{0,32},{32,0},{64,96},{96,64},{128,160},{160,128},{192,224},{224,1... | collective-permute-start | bytes 417800 | tf_op jit(solution)/shard_map/ppermute | solution.py:38
  27.4 0.0 collective-permute-done.8.refs_2_.refs_6_
  27.5 0.9 collective-permute-start.9
  28.3 0.0 collective-permute-done.6.refs_0_.refs_4_
  28.3 1.0 %collective-permute-start.7 = (bf16[272,256]{1,0:T(8,128)(2,1)S(1)}, bf16[272,256]{1,0:T(8,128)(2,1)S(1)}, u32[]{:S(2)}, u32[]{:S(2)}) collective-permute-start(bf16[272,256]{1,0:T(8,128)(2,1)S(1)} %collective-permute-done.6.refs_0_.refs_4_), channel_id=1, source_target_pairs={{0,32},{32,0},{64,96},{96,64},{128,160},{160,128},{192,224},{224,1... | collective-permute-start | bytes 417800 | tf_op jit(solution)/shard_map/ppermute | solution.py:38
  29.3 0.2 offset_rows.1.offset_ref
  29.5 0.0 collective-permute-done.12.refs_3_
  29.5 0.6 rebuild_first.1.refs_5_
  30.2 0.2 collective-permute-done.7.refs_1_.refs_5_
  30.3 0.6 rebuild_last.1
  30.9 22.7 %all_to_all.10.parts_ref = bf16[32,8,640]{2,1,0:T(8,128)(2,1)S(1)} all-to-all(bf16[32,8,640]{2,1,0:T(8,128)(2,1)S(1)} %bitcast.21), channel_id=1, replica_groups=mesh['width'=8,'latent'=32] {'latent'}, dimensions={0} | all-to-all | bytes 655360 | tf_op jit(solution)/shard_map/all_to_all | solution.py:408
  53.6 0.3 error_rows.1
  53.9 15.8 %all_to_all.11 = bf16[32,8,640]{2,1,0:T(8,128)(2,1)S(1)} all-to-all(bf16[32,8,640]{2,1,0:T(8,128)(2,1)S(1)} %error_rows.1), channel_id=1, replica_groups=mesh['width'=8,'latent'=32] {'latent'}, dimensions={0} | all-to-all | bytes 655360 | tf_op jit(solution)/shard_map/all_to_all | solution.py:410
  69.7 0.3 back_far.1
  70.0 3.8 %collective-permute-start.13 = (bf16[256,256]{1,0:T(8,128)(2,1)S(1)}, bf16[256,256]{1,0:T(8,128)(2,1)S(1)}, u32[]{:S(2)}, u32[]{:S(2)}) collective-permute-start(bf16[256,256]{1,0:T(8,128)(2,1)S(1)} %back_far.1), channel_id=1, source_target_pairs={{0,32},{32,0},{64,96},{96,64},{128,160},{160,128},{192,224},{224,1... | collective-permute-start | bytes 393224 | tf_op jit(solution)/shard_map/ppermute | solution.py:38
  73.8 0.5 back_send.1
  74.2 0.6 back_keep.1
  74.9 0.3 collective-permute-start.14
  75.2 2.2 %collective-permute-start.15 = (bf16[256,256]{1,0:T(8,128)(2,1)S(1)}, bf16[256,256]{1,0:T(8,128)(2,1)S(1)}, u32[]{:S(2)}, u32[]{:S(2)}) collective-permute-start(bf16[256,256]{1,0:T(8,128)(2,1)S(1)} %add_convert_fusion.2), channel_id=1, source_target_pairs={{0,128},{32,160},{64,192},{96,224},{128,0},{160,32},{192,64},{224,... | collective-permute-start | bytes 393224 | tf_op jit(solution)/shard_map/ppermute | solution.py:38
  77.4 0.1 add_convert_fusion
  77.5 1.0 %collective-permute-start.17 = (bf16[256,256]{1,0:T(8,128)(2,1)S(1)}, bf16[256,256]{1,0:T(8,128)(2,1)S(1)}, u32[]{:S(2)}, u32[]{:S(2)}) collective-permute-start(bf16[256,256]{1,0:T(8,128)(2,1)S(1)} %get-tuple-element.61), channel_id=1, source_target_pairs={{0,192},{32,224},{64,0},{96,32},{128,64},{160,96},{192,128},{224,1... | collective-permute-start | bytes 393224 | tf_op jit(solution)/shard_map/ppermute | solution.py:38
  78.5 0.5 collective-permute-start.16
  79.1 1.9 %decoder_gradient.1 = (bf16[576,2048]{1,0:T(8,128)(2,1)}, f32[1,576]{1,0:T(1,128)S(1)}) custom-call(bf16[256,640]{1,0:T(8,128)(2,1)S(1)} %bitcast.19, bf16[272,256]{1,0:T(8,128)(2,1)S(1)} %get-tuple-element.55.refs_0_.feat_ref, bf16[272,256]{1,0:T(8,128)(2,1)S(1)} %collective-permute-done.10.refs_1_, bf16[272,256]{1,0:T(8,128)(2,1)S(1)} %collective-permute-done.11.refs_2_, ...), custom_call_target="tpu_custom_call" | custom-call | flops 603979776 | bytes 5767168 | tf_op jit(solution)/shard_map/decoder_gradient/pallas_call | solution.py:50
  81.0 0.6 reduce
  81.6 2.0 %collective-permute-done.17.three_ref = bf16[256,256]{1,0:T(8,128)(2,1)S(1)} collective-permute-done((bf16[256,256]{1,0:T(8,128)(2,1)S(1)}, bf16[256,256]{1,0:T(8,128)(2,1)S(1)}, u32[]{:S(2)}, u32[]{:S(2)}) %collective-permute-start.17) | collective-permute-done | bytes 131104 | tf_op jit(solution)/shard_map/ppermute | solution.py:38
  83.6 0.5 collective-permute-done.16.two_ref
  84.1 0.3 own_gradient.1.refs_0_
  84.4 3.1 %collective-permute-start.23 = (bf16[272,256]{1,0:T(8,128)(2,1)S(1)}, bf16[272,256]{1,0:T(8,128)(2,1)S(1)}, u32[]{:S(2)}, u32[]{:S(2)}) collective-permute-start(bf16[272,256]{1,0:T(8,128)(2,1)S(1)} %own_gradient.1.refs_0_), channel_id=1, source_target_pairs={{0,128},{32,160},{64,192},{96,224},{128,0},{160,32},{192,64},{224,... | collective-permute-start | bytes 417800 | tf_op jit(solution)/shard_map/ppermute | solution.py:38
  87.5 0.0 collective-permute-start.21
  87.6 2.7 %collective-permute-start.19 = (bf16[272,256]{1,0:T(8,128)(2,1)S(1)}, bf16[272,256]{1,0:T(8,128)(2,1)S(1)}, u32[]{:S(2)}, u32[]{:S(2)}) collective-permute-start(bf16[272,256]{1,0:T(8,128)(2,1)S(1)} %own_gradient.1.refs_0_), channel_id=1, source_target_pairs={{0,192},{32,224},{64,0},{96,32},{128,64},{160,96},{192,128},{224,1... | collective-permute-start | bytes 417800 | tf_op jit(solution)/shard_map/ppermute | solution.py:38
  90.2 1.3 %collective-permute-start.18 = (bf16[272,256]{1,0:T(8,128)(2,1)S(1)}, bf16[272,256]{1,0:T(8,128)(2,1)S(1)}, u32[]{:S(2)}, u32[]{:S(2)}) collective-permute-start(bf16[272,256]{1,0:T(8,128)(2,1)S(1)} %own_gradient.1.refs_0_), channel_id=1, source_target_pairs={{0,32},{32,0},{64,96},{96,64},{128,160},{160,128},{192,224},{224,1... | collective-permute-start | bytes 417800 | tf_op jit(solution)/shard_map/ppermute | solution.py:38
  91.6 2.5 %collective-permute-start.24 = (bf16[272,256]{1,0:T(8,128)(2,1)S(1)}, bf16[272,256]{1,0:T(8,128)(2,1)S(1)}, u32[]{:S(2)}, u32[]{:S(2)}) collective-permute-start(bf16[272,256]{1,0:T(8,128)(2,1)S(1)} %collective-permute-done.23.refs_6_), channel_id=1, source_target_pairs={{0,32},{32,0},{64,96},{96,64},{128,160},{160,128},{192,224},{224,1... | collective-permute-start | bytes 417800 | tf_op jit(solution)/shard_map/ppermute | solution.py:38
  94.1 0.8 collective-permute-done.21.refs_4_
  94.9 1.0 %collective-permute-start.22 = (bf16[272,256]{1,0:T(8,128)(2,1)S(1)}, bf16[272,256]{1,0:T(8,128)(2,1)S(1)}, u32[]{:S(2)}, u32[]{:S(2)}) collective-permute-start(bf16[272,256]{1,0:T(8,128)(2,1)S(1)} %collective-permute-done.21.refs_4_), channel_id=1, source_target_pairs={{0,32},{32,0},{64,96},{96,64},{128,160},{160,128},{192,224},{224,1... | collective-permute-start | bytes 417800 | tf_op jit(solution)/shard_map/ppermute | solution.py:38
  95.9 0.0 collective-permute-start.20
  96.0 1.0 collective-permute-done.22.refs_5_
  96.9 0.4 collective-permute-done.20.refs_3_
  97.3 1.8 %encoder_gradient.1 = (bf16[576,2048]{1,0:T(8,128)(2,1)}, f32[1,2048]{1,0:T(1,128)}, f32[1,128]{1,0:T(1,128)}) custom-call(bf16[576,256]{1,0:T(8,128)(2,1)S(1)} %bitcast.24, bf16[272,256]{1,0:T(8,128)(2,1)S(1)} %own_gradient.1.refs_0_, bf16[272,256]{1,0:T(8,128)(2,1)S(1)} %collective-permute-done.18.refs_1_, ...), custom_call_target="tpu_custom_call" | custom-call | flops 603979776 | bytes 3407872 | tf_op jit(solution)/shard_map/encoder_gradient/pallas_call | solution.py:50
  (18 shorter events, 0.1 us)
Async XLA Ops:
  0.6 5.4 %copy-start = (bf16[2048,576]{0,1:T(8,128)(2,1)S(1)}, bf16[2048,576]{0,1:T(8,128)(2,1)}, u32[]{:S(2)}) copy-start(bf16[2048,576]{0,1:T(8,128)(2,1)} %param.8) | copy-start | bytes 7077892
  2.7 4.9 %collective-permute-start = (f32[256,256]{1,0:T(8,128)S(1)}, f32[256,256]{1,0:T(8,128)S(1)}, u32[]{:S(2)}, u32[]{:S(2)}) collective-permute-start(f32[256,256]{1,0:T(8,128)S(1)} %get-tuple-element.35), channel_id=1, source_target_pairs={{0,32},{32,0},{64,96},{96,64},{128,160},{160,128},{192,224},{224,1... | collective-permute-start | bytes 786440 | tf_op jit(solution)/shard_map/ppermute | solution.py:38
  6.2 1.4 %collective-permute-start.1 = (f32[8,2048]{1,0:T(8,128)S(1)}, f32[8,2048]{1,0:T(8,128)S(1)}, u32[]{:S(2)}, u32[]{:S(2)}) collective-permute-start(f32[8,2048]{1,0:T(8,128)S(1)} %square_sums.1.square_ref.refs_3_), channel_id=1, source_target_pairs={{0,32},{32,0},{64,96},{96,64},{128,160},{160,128},{192,224},{224,1... | collective-permute-start | bytes 196616 | tf_op jit(solution)/shard_map/ppermute | solution.py:38
  7.6 10.5 %copy-start.2 = (f32[2048]{0:T(1024)S(1)}, f32[2048]{0:T(1024)}, u32[]{:S(2)}) copy-start(f32[2048]{0:T(1024)} %param.7) | copy-start | bytes 24580
  7.8 2.4 %collective-permute-start.2 = (f32[768,256]{1,0:T(8,128)S(1)}, f32[768,256]{1,0:T(8,128)S(1)}, u32[]{:S(2)}, u32[]{:S(2)}) collective-permute-start(f32[768,256]{1,0:T(8,128)S(1)} %preact_send.1), channel_id=1, source_target_pairs={{0,32},{32,0},{64,96},{96,64},{128,160},{160,128},{192,224},{224,1... | collective-permute-start | bytes 2359304 | tf_op jit(solution)/shard_map/ppermute | solution.py:38
  8.1 6.5 %collective-permute-start.3 = (bf16[272,256]{1,0:T(8,128)(2,1)S(1)}, bf16[272,256]{1,0:T(8,128)(2,1)S(1)}, u32[]{:S(2)}, u32[]{:S(2)}) collective-permute-start(bf16[272,256]{1,0:T(8,128)(2,1)S(1)} %encode_sums.3), channel_id=1, source_target_pairs={{0,128},{32,160},{64,192},{96,224},{128,0},{160,32},{192,64},{224,... | collective-permute-start | bytes 417800 | tf_op jit(solution)/shard_map/ppermute | solution.py:38
  10.4 18.9 %copy-start.3 = (f32[576]{0:T(1024)S(1)}, f32[576]{0:T(1024)}, u32[]{:S(2)}) copy-start(f32[576]{0:T(1024)} %param.9) | copy-start | bytes 6916
  10.4 18.9 %copy-start.1 = (bf16[256,576]{0,1:T(8,128)(2,1)S(1)}, bf16[256,576]{0,1:T(8,128)(2,1)}, u32[]{:S(2)}) copy-start(bf16[256,576]{0,1:T(8,128)(2,1)} %param.5) | copy-start | bytes 884740
  10.4 7.6 %collective-permute-start.4 = (bf16[272,256]{1,0:T(8,128)(2,1)S(1)}, bf16[272,256]{1,0:T(8,128)(2,1)S(1)}, u32[]{:S(2)}, u32[]{:S(2)}) collective-permute-start(bf16[272,256]{1,0:T(8,128)(2,1)S(1)} %encode_sums.4), channel_id=1, source_target_pairs={{0,64},{32,96},{64,128},{96,160},{128,192},{160,224},{192,0},{224,... | collective-permute-start | bytes 417800 | tf_op jit(solution)/shard_map/ppermute | solution.py:38
  10.7 7.3 %collective-permute-start.5 = (bf16[272,256]{1,0:T(8,128)(2,1)S(1)}, bf16[272,256]{1,0:T(8,128)(2,1)S(1)}, u32[]{:S(2)}, u32[]{:S(2)}) collective-permute-start(bf16[272,256]{1,0:T(8,128)(2,1)S(1)} %encode_sums.5), channel_id=1, source_target_pairs={{0,192},{32,224},{64,0},{96,32},{128,64},{160,96},{192,128},{224,1... | collective-permute-start | bytes 417800 | tf_op jit(solution)/shard_map/ppermute | solution.py:38
  18.7 6.2 %collective-permute-start.11 = (bf16[272,256]{1,0:T(8,128)(2,1)S(1)}, bf16[272,256]{1,0:T(8,128)(2,1)S(1)}, u32[]{:S(2)}, u32[]{:S(2)}) collective-permute-start(bf16[272,256]{1,0:T(8,128)(2,1)S(1)} %get-tuple-element.55.refs_0_.feat_ref), channel_id=1, source_target_pairs={{0,128},{32,160},{64,192},{96,224},{128,0},{160,32},{192,64},{224,... | collective-permute-start | bytes 417800 | tf_op jit(solution)/shard_map/ppermute | solution.py:38
  19.9 7.5 %collective-permute-start.8 = (bf16[272,256]{1,0:T(8,128)(2,1)S(1)}, bf16[272,256]{1,0:T(8,128)(2,1)S(1)}, u32[]{:S(2)}, u32[]{:S(2)}) collective-permute-start(bf16[272,256]{1,0:T(8,128)(2,1)S(1)} %get-tuple-element.55.refs_0_.feat_ref), channel_id=1, source_target_pairs={{0,192},{32,224},{64,0},{96,32},{128,64},{160,96},{192,128},{224,1... | collective-permute-start | bytes 417800 | tf_op jit(solution)/shard_map/ppermute | solution.py:38
  20.2 8.1 %collective-permute-start.6 = (bf16[272,256]{1,0:T(8,128)(2,1)S(1)}, bf16[272,256]{1,0:T(8,128)(2,1)S(1)}, u32[]{:S(2)}, u32[]{:S(2)}) collective-permute-start(bf16[272,256]{1,0:T(8,128)(2,1)S(1)} %get-tuple-element.55.refs_0_.feat_ref), channel_id=1, source_target_pairs={{0,64},{32,96},{64,128},{96,160},{128,192},{160,224},{192,0},{224,... | collective-permute-start | bytes 417800 | tf_op jit(solution)/shard_map/ppermute | solution.py:38
  21.4 8.1 %collective-permute-start.10 = (bf16[272,256]{1,0:T(8,128)(2,1)S(1)}, bf16[272,256]{1,0:T(8,128)(2,1)S(1)}, u32[]{:S(2)}, u32[]{:S(2)}) collective-permute-start(bf16[272,256]{1,0:T(8,128)(2,1)S(1)} %get-tuple-element.55.refs_0_.feat_ref), channel_id=1, source_target_pairs={{0,32},{32,0},{64,96},{96,64},{128,160},{160,128},{192,224},{224,1... | collective-permute-start | bytes 417800 | tf_op jit(solution)/shard_map/ppermute | solution.py:38
  24.8 4.7 %collective-permute-start.12 = (bf16[272,256]{1,0:T(8,128)(2,1)S(1)}, bf16[272,256]{1,0:T(8,128)(2,1)S(1)}, u32[]{:S(2)}, u32[]{:S(2)}) collective-permute-start(bf16[272,256]{1,0:T(8,128)(2,1)S(1)} %collective-permute-done.11.refs_2_), channel_id=1, source_target_pairs={{0,32},{32,0},{64,96},{96,64},{128,160},{160,128},{192,224},{224,1... | collective-permute-start | bytes 417800 | tf_op jit(solution)/shard_map/ppermute | solution.py:38
  27.5 2.7 %collective-permute-start.9 = (bf16[272,256]{1,0:T(8,128)(2,1)S(1)}, bf16[272,256]{1,0:T(8,128)(2,1)S(1)}, u32[]{:S(2)}, u32[]{:S(2)}) collective-permute-start(bf16[272,256]{1,0:T(8,128)(2,1)S(1)} %collective-permute-done.8.refs_2_.refs_6_), channel_id=1, source_target_pairs={{0,32},{32,0},{64,96},{96,64},{128,160},{160,128},{192,224},{224,1... | collective-permute-start | bytes 417800 | tf_op jit(solution)/shard_map/ppermute | solution.py:38
  28.3 2.0 %collective-permute-start.7 = (bf16[272,256]{1,0:T(8,128)(2,1)S(1)}, bf16[272,256]{1,0:T(8,128)(2,1)S(1)}, u32[]{:S(2)}, u32[]{:S(2)}) collective-permute-start(bf16[272,256]{1,0:T(8,128)(2,1)S(1)} %collective-permute-done.6.refs_0_.refs_4_), channel_id=1, source_target_pairs={{0,32},{32,0},{64,96},{96,64},{128,160},{160,128},{192,224},{224,1... | collective-permute-start | bytes 417800 | tf_op jit(solution)/shard_map/ppermute | solution.py:38
  70.0 4.9 %collective-permute-start.13 = (bf16[256,256]{1,0:T(8,128)(2,1)S(1)}, bf16[256,256]{1,0:T(8,128)(2,1)S(1)}, u32[]{:S(2)}, u32[]{:S(2)}) collective-permute-start(bf16[256,256]{1,0:T(8,128)(2,1)S(1)} %back_far.1), channel_id=1, source_target_pairs={{0,32},{32,0},{64,96},{96,64},{128,160},{160,128},{192,224},{224,1... | collective-permute-start | bytes 393224 | tf_op jit(solution)/shard_map/ppermute | solution.py:38
  74.9 2.5 %collective-permute-start.14 = (bf16[768,256]{1,0:T(8,128)(2,1)S(1)}, bf16[768,256]{1,0:T(8,128)(2,1)S(1)}, u32[]{:S(2)}, u32[]{:S(2)}) collective-permute-start(bf16[768,256]{1,0:T(8,128)(2,1)S(1)} %back_send.1), channel_id=1, source_target_pairs={{0,32},{32,0},{64,96},{96,64},{128,160},{160,128},{192,224},{224,1... | collective-permute-start | bytes 1179656 | tf_op jit(solution)/shard_map/ppermute | solution.py:38
  75.2 6.4 %collective-permute-start.15 = (bf16[256,256]{1,0:T(8,128)(2,1)S(1)}, bf16[256,256]{1,0:T(8,128)(2,1)S(1)}, u32[]{:S(2)}, u32[]{:S(2)}) collective-permute-start(bf16[256,256]{1,0:T(8,128)(2,1)S(1)} %add_convert_fusion.2), channel_id=1, source_target_pairs={{0,128},{32,160},{64,192},{96,224},{128,0},{160,32},{192,64},{224,... | collective-permute-start | bytes 393224 | tf_op jit(solution)/shard_map/ppermute | solution.py:38
  77.5 6.1 %collective-permute-start.17 = (bf16[256,256]{1,0:T(8,128)(2,1)S(1)}, bf16[256,256]{1,0:T(8,128)(2,1)S(1)}, u32[]{:S(2)}, u32[]{:S(2)}) collective-permute-start(bf16[256,256]{1,0:T(8,128)(2,1)S(1)} %get-tuple-element.61), channel_id=1, source_target_pairs={{0,192},{32,224},{64,0},{96,32},{128,64},{160,96},{192,128},{224,1... | collective-permute-start | bytes 393224 | tf_op jit(solution)/shard_map/ppermute | solution.py:38
  78.5 5.6 %collective-permute-start.16 = (bf16[256,256]{1,0:T(8,128)(2,1)S(1)}, bf16[256,256]{1,0:T(8,128)(2,1)S(1)}, u32[]{:S(2)}, u32[]{:S(2)}) collective-permute-start(bf16[256,256]{1,0:T(8,128)(2,1)S(1)} %get-tuple-element.62), channel_id=1, source_target_pairs={{0,64},{32,96},{64,128},{96,160},{128,192},{160,224},{192,0},{224,... | collective-permute-start | bytes 393224 | tf_op jit(solution)/shard_map/ppermute | solution.py:38
  84.4 7.2 %collective-permute-start.23 = (bf16[272,256]{1,0:T(8,128)(2,1)S(1)}, bf16[272,256]{1,0:T(8,128)(2,1)S(1)}, u32[]{:S(2)}, u32[]{:S(2)}) collective-permute-start(bf16[272,256]{1,0:T(8,128)(2,1)S(1)} %own_gradient.1.refs_0_), channel_id=1, source_target_pairs={{0,128},{32,160},{64,192},{96,224},{128,0},{160,32},{192,64},{224,... | collective-permute-start | bytes 417800 | tf_op jit(solution)/shard_map/ppermute | solution.py:38
  87.5 7.4 %collective-permute-start.21 = (bf16[272,256]{1,0:T(8,128)(2,1)S(1)}, bf16[272,256]{1,0:T(8,128)(2,1)S(1)}, u32[]{:S(2)}, u32[]{:S(2)}) collective-permute-start(bf16[272,256]{1,0:T(8,128)(2,1)S(1)} %own_gradient.1.refs_0_), channel_id=1, source_target_pairs={{0,64},{32,96},{64,128},{96,160},{128,192},{160,224},{192,0},{224,... | collective-permute-start | bytes 417800 | tf_op jit(solution)/shard_map/ppermute | solution.py:38
  87.6 8.4 %collective-permute-start.19 = (bf16[272,256]{1,0:T(8,128)(2,1)S(1)}, bf16[272,256]{1,0:T(8,128)(2,1)S(1)}, u32[]{:S(2)}, u32[]{:S(2)}) collective-permute-start(bf16[272,256]{1,0:T(8,128)(2,1)S(1)} %own_gradient.1.refs_0_), channel_id=1, source_target_pairs={{0,192},{32,224},{64,0},{96,32},{128,64},{160,96},{192,128},{224,1... | collective-permute-start | bytes 417800 | tf_op jit(solution)/shard_map/ppermute | solution.py:38
  90.2 5.7 %collective-permute-start.18 = (bf16[272,256]{1,0:T(8,128)(2,1)S(1)}, bf16[272,256]{1,0:T(8,128)(2,1)S(1)}, u32[]{:S(2)}, u32[]{:S(2)}) collective-permute-start(bf16[272,256]{1,0:T(8,128)(2,1)S(1)} %own_gradient.1.refs_0_), channel_id=1, source_target_pairs={{0,32},{32,0},{64,96},{96,64},{128,160},{160,128},{192,224},{224,1... | collective-permute-start | bytes 417800 | tf_op jit(solution)/shard_map/ppermute | solution.py:38
  91.6 4.4 %collective-permute-start.24 = (bf16[272,256]{1,0:T(8,128)(2,1)S(1)}, bf16[272,256]{1,0:T(8,128)(2,1)S(1)}, u32[]{:S(2)}, u32[]{:S(2)}) collective-permute-start(bf16[272,256]{1,0:T(8,128)(2,1)S(1)} %collective-permute-done.23.refs_6_), channel_id=1, source_target_pairs={{0,32},{32,0},{64,96},{96,64},{128,160},{160,128},{192,224},{224,1... | collective-permute-start | bytes 417800 | tf_op jit(solution)/shard_map/ppermute | solution.py:38
  94.9 2.0 %collective-permute-start.22 = (bf16[272,256]{1,0:T(8,128)(2,1)S(1)}, bf16[272,256]{1,0:T(8,128)(2,1)S(1)}, u32[]{:S(2)}, u32[]{:S(2)}) collective-permute-start(bf16[272,256]{1,0:T(8,128)(2,1)S(1)} %collective-permute-done.21.refs_4_), channel_id=1, source_target_pairs={{0,32},{32,0},{64,96},{96,64},{128,160},{160,128},{192,224},{224,1... | collective-permute-start | bytes 417800 | tf_op jit(solution)/shard_map/ppermute | solution.py:38
  95.9 1.4 %collective-permute-start.20 = (bf16[272,256]{1,0:T(8,128)(2,1)S(1)}, bf16[272,256]{1,0:T(8,128)(2,1)S(1)}, u32[]{:S(2)}, u32[]{:S(2)}) collective-permute-start(bf16[272,256]{1,0:T(8,128)(2,1)S(1)} %collective-permute-done.19.refs_2_), channel_id=1, source_target_pairs={{0,32},{32,0},{64,96},{96,64},{128,160},{160,128},{192,224},{224,1... | collective-permute-start | bytes 417800 | tf_op jit(solution)/shard_map/ppermute | solution.py:38

commit v6 on v5

--- a/solution.py
+++ b/solution.py
@@ -22,9 +22,10 @@
 LN2 = 0.6931471805599453
 FAR = 2
 HOPS = (FAR, 1, 3)
+FORWARD = (3, FAR, 1)
 BACKWARD = HOPS[::-1]
 REST = (1, 3, 0)
-FIRST_REBUILD = 4
+FIRST_REBUILD = 6
 VMEM_BYTES = 16 * 1024 * 1024
 
 CORE_SWAP = [(i, i ^ 1) for i in range(8)]
@@ -68,7 +69,7 @@
     return lax.rem(x + 4, 4) * 2 + core
 
 
-def gathered_owners(hops=HOPS):
+def gathered_owners(hops=FORWARD):
     x, core = place()
     return [owner(x - d, side) for d in (0, *hops) for side in (core, 1 - core)]
 
@@ -401,7 +402,7 @@
     coded = [on_width(coded, x_shift(FAR))] + [on_width(encode(*rest, squares, d), x_shift(d)) for d in HOPS[1:]]
     features, own_weights = own_features(*rest, coded, squares, latent_bias[None, :])
 
-    feature_chunks = gather_chunks(features, HOPS)
+    feature_chunks = gather_chunks(features, FORWARD)
     partial = rebuild_first(feature_chunks[:FIRST_REBUILD], dec_t, own_weights)
     parts = rebuild_last(feature_chunks[FIRST_REBUILD:], dec_t, partial).reshape(32, 8, WIDE)
     parts, offset = lax.optimization_barrier((parts, offset_rows(act_t, output_bias[None, :])))
@@ -414,7 +415,7 @@
     keep_far, keep = back_keep(errors, dec_t)
     summed = keep_far + on_width(send, CORE_SWAP).astype(F32)
     send = rest_parts(errors, dec_t, True, BF16, "back_send")
-    summed, send, keep = lax.optimization_barrier((summed.astype(BF16), send, keep))
+    summed, keep = lax.optimization_barrier((summed.astype(BF16), keep))
     summed = [on_width(summed, x_shift(FAR))]
     rest = (keep, on_width(send, CORE_SWAP))
     for d in HOPS[1:]:

time: 99.4 us -> 100 us (level)
  no operation moved by 1% of the time
where the time goes in v6:
time: 100 us
  blocking collectives  38.5 us (38%)
  starting transfers between devices  35 us (35%)
  waiting for transfers between devices  13.4 us (13%)
  Pallas kernels  11.4 us (11%)
    ppermute x25, starting transfers between devices, on_width(): return lax.ppermute(value, 'width', pairs)  35 us
    all_to_all x1, blocking collectives, shards(): parts = lax.all_to_all(parts, 'latent', 0, 0)  22.8 us
    all_to_all x1, blocking collectives, shards(): errors = lax.all_to_all(errors, 'latent', 0, 0).reshape(TOK, WIDE)  15.8 us
    ppermute x25, waiting for transfers between devices, on_width(): return lax.ppermute(value, 'width', pairs)  13.4 us
    pallas_call x18, Pallas kernels, call(): pl.pallas_call(body, in_specs=in_specs, out_specs=out_specs or [IN_VMEM]...  11.4 us
  transfers between devices with their start and end apart: 25, of which 10 were waited for; matrix products, arithmetic and copies ran while one was open for 1% of the time, Pallas kernels for 5%

profile of v6, /device:TPU:1, one launch (start us, length us, event | category | flops | bytes accessed | tf_op | source)
XLA Modules:
  0.0 100.0 jit_solution(2561745489727690088)
XLA Ops:
  0.6 2.1 %preact_far.1 = (f32[256,256]{1,0:T(8,128)S(1)}, f32[256,256]{1,0:T(8,128)S(1)}, bf16[256,576]{1,0:T(8,128)(2,1)S(1)}, bf16[576,2048]{1,0:T(8,128)(2,1)S(1)}) custom-call(bf16[576,256]{1,0:T(8,128)(2,1)} %bitcast.22, bf16[576,2048]{1,0:T(8,128)(2,1)} %enc_ref.1), custom_call_target="tpu_custom_call" | custom-call | flops 2400000000 | bytes 1114112 | tf_op jit(solution)/shard_map/preact_far/pallas_call | solution.py:51
  2.7 3.3 %collective-permute-start = (f32[256,256]{1,0:T(8,128)S(1)}, f32[256,256]{1,0:T(8,128)S(1)}, u32[]{:S(2)}, u32[]{:S(2)}) collective-permute-start(f32[256,256]{1,0:T(8,128)S(1)} %get-tuple-element.34), channel_id=1, source_target_pairs={{0,32},{32,0},{64,96},{96,64},{128,160},{160,128},{192,224},{224,1... | collective-permute-start | bytes 786440 | tf_op jit(solution)/shard_map/ppermute | solution.py:39
  6.0 0.1 square_sums.1.square_ref.refs_3_
  6.2 0.4 collective-permute-start.1
  6.6 0.5 preact_keep.1.mine_ref
  7.1 0.5 preact_send.1
  7.6 0.0 copy-start.2
  7.6 0.0 collective-permute-done.other_ref
  7.6 0.2 encode_sums.3
  7.8 0.3 collective-permute-start.2
  8.1 1.0 %collective-permute-start.3 = (bf16[272,256]{1,0:T(8,128)(2,1)S(1)}, bf16[272,256]{1,0:T(8,128)(2,1)S(1)}, u32[]{:S(2)}, u32[]{:S(2)}) collective-permute-start(bf16[272,256]{1,0:T(8,128)(2,1)S(1)} %encode_sums.3), channel_id=1, source_target_pairs={{0,128},{32,160},{64,192},{96,224},{128,0},{160,32},{192,64},{224,... | collective-permute-start | bytes 417800 | tf_op jit(solution)/shard_map/ppermute | solution.py:39
  9.1 1.1 %collective-permute-done.2.other_ref = f32[768,256]{1,0:T(8,128)S(1)} collective-permute-done((f32[768,256]{1,0:T(8,128)S(1)}, f32[768,256]{1,0:T(8,128)S(1)}, u32[]{:S(2)}, u32[]{:S(2)}) %collective-permute-start.2) | collective-permute-done | bytes 786464 | tf_op jit(solution)/shard_map/ppermute | solution.py:39
  10.2 0.2 encode_sums.4
  10.4 0.0 copy-start.1
  10.4 0.1 collective-permute-start.4
  10.5 0.2 encode_sums.5
  10.8 2.7 %collective-permute-start.5 = (bf16[272,256]{1,0:T(8,128)(2,1)S(1)}, bf16[272,256]{1,0:T(8,128)(2,1)S(1)}, u32[]{:S(2)}, u32[]{:S(2)}) collective-permute-start(bf16[272,256]{1,0:T(8,128)(2,1)S(1)} %encode_sums.5), channel_id=1, source_target_pairs={{0,192},{32,224},{64,0},{96,32},{128,64},{160,96},{192,128},{224,1... | collective-permute-start | bytes 417800 | tf_op jit(solution)/shard_map/ppermute | solution.py:39
  13.5 1.1 %collective-permute-done.3.refs_0_ = bf16[272,256]{1,0:T(8,128)(2,1)S(1)} collective-permute-done((bf16[272,256]{1,0:T(8,128)(2,1)S(1)}, bf16[272,256]{1,0:T(8,128)(2,1)S(1)}, u32[]{:S(2)}, u32[]{:S(2)}) %collective-permute-start.3) | collective-permute-done | bytes 139296 | tf_op jit(solution)/shard_map/ppermute | solution.py:39
  14.6 3.4 %collective-permute-done.4.refs_1_ = bf16[272,256]{1,0:T(8,128)(2,1)S(1)} collective-permute-done((bf16[272,256]{1,0:T(8,128)(2,1)S(1)}, bf16[272,256]{1,0:T(8,128)(2,1)S(1)}, u32[]{:S(2)}, u32[]{:S(2)}) %collective-permute-start.4) | collective-permute-done | bytes 139296 | tf_op jit(solution)/shard_map/ppermute | solution.py:39
  18.1 0.6 own_features.1
  18.7 1.3 %collective-permute-start.11 = (bf16[272,256]{1,0:T(8,128)(2,1)S(1)}, bf16[272,256]{1,0:T(8,128)(2,1)S(1)}, u32[]{:S(2)}, u32[]{:S(2)}) collective-permute-start(bf16[272,256]{1,0:T(8,128)(2,1)S(1)} %get-tuple-element.53.refs_0_.feat_ref), channel_id=1, source_target_pairs={{0,128},{32,160},{64,192},{96,224},{128,0},{160,32},{192,64},{224,... | collective-permute-start | bytes 417800 | tf_op jit(solution)/shard_map/ppermute | solution.py:39
  19.9 0.3 collective-permute-start.9
  20.2 1.2 %collective-permute-start.6 = (bf16[272,256]{1,0:T(8,128)(2,1)S(1)}, bf16[272,256]{1,0:T(8,128)(2,1)S(1)}, u32[]{:S(2)}, u32[]{:S(2)}) collective-permute-start(bf16[272,256]{1,0:T(8,128)(2,1)S(1)} %get-tuple-element.53.refs_0_.feat_ref), channel_id=1, source_target_pairs={{0,64},{32,96},{64,128},{96,160},{128,192},{160,224},{192,0},{224,... | collective-permute-start | bytes 417800 | tf_op jit(solution)/shard_map/ppermute | solution.py:39
  21.4 1.3 %collective-permute-start.8 = (bf16[272,256]{1,0:T(8,128)(2,1)S(1)}, bf16[272,256]{1,0:T(8,128)(2,1)S(1)}, u32[]{:S(2)}, u32[]{:S(2)}) collective-permute-start(bf16[272,256]{1,0:T(8,128)(2,1)S(1)} %get-tuple-element.53.refs_0_.feat_ref), channel_id=1, source_target_pairs={{0,32},{32,0},{64,96},{96,64},{128,160},{160,128},{192,224},{224,1... | collective-permute-start | bytes 417800 | tf_op jit(solution)/shard_map/ppermute | solution.py:39
  22.7 2.1 %collective-permute-done.11.refs_4_ = bf16[272,256]{1,0:T(8,128)(2,1)S(1)} collective-permute-done((bf16[272,256]{1,0:T(8,128)(2,1)S(1)}, bf16[272,256]{1,0:T(8,128)(2,1)S(1)}, u32[]{:S(2)}, u32[]{:S(2)}) %collective-permute-start.11) | collective-permute-done | bytes 139296 | tf_op jit(solution)/shard_map/ppermute | solution.py:39
  24.8 2.6 %collective-permute-start.12 = (bf16[272,256]{1,0:T(8,128)(2,1)S(1)}, bf16[272,256]{1,0:T(8,128)(2,1)S(1)}, u32[]{:S(2)}, u32[]{:S(2)}) collective-permute-start(bf16[272,256]{1,0:T(8,128)(2,1)S(1)} %collective-permute-done.11.refs_4_), channel_id=1, source_target_pairs={{0,32},{32,0},{64,96},{96,64},{128,160},{160,128},{192,224},{224,1... | collective-permute-start | bytes 417800 | tf_op jit(solution)/shard_map/ppermute | solution.py:39
  27.5 0.0 collective-permute-done.9.refs_2_
  27.5 0.9 collective-permute-start.10
  28.3 1.0 collective-permute-start.7
  29.3 0.2 offset_rows.1.offset_ref
  29.5 0.0 collective-permute-done.8.refs_1_
  29.5 0.0 collective-permute-done.12.refs_5_
  29.5 0.0 collective-permute-done.10.refs_3_
  29.6 0.8 rebuild_first.1.refs_3_
  30.4 0.4 rebuild_last.1
  30.8 22.8 %all_to_all.10.parts_ref = bf16[32,8,640]{2,1,0:T(8,128)(2,1)S(1)} all-to-all(bf16[32,8,640]{2,1,0:T(8,128)(2,1)S(1)} %bitcast.21), channel_id=1, replica_groups=mesh['width'=8,'latent'=32] {'latent'}, dimensions={0} | all-to-all | bytes 655360 | tf_op jit(solution)/shard_map/all_to_all | solution.py:409
  53.5 0.3 error_rows.1
  53.8 15.8 %all_to_all.11 = bf16[32,8,640]{2,1,0:T(8,128)(2,1)S(1)} all-to-all(bf16[32,8,640]{2,1,0:T(8,128)(2,1)S(1)} %error_rows.1), channel_id=1, replica_groups=mesh['width'=8,'latent'=32] {'latent'}, dimensions={0} | all-to-all | bytes 655360 | tf_op jit(solution)/shard_map/all_to_all | solution.py:411
  69.6 0.3 back_far.1
  69.9 0.5 back_send.1
  70.4 3.8 %collective-permute-start.14 = (bf16[768,256]{1,0:T(8,128)(2,1)S(1)}, bf16[768,256]{1,0:T(8,128)(2,1)S(1)}, u32[]{:S(2)}, u32[]{:S(2)}) collective-permute-start(bf16[768,256]{1,0:T(8,128)(2,1)S(1)} %back_send.1), channel_id=1, source_target_pairs={{0,32},{32,0},{64,96},{96,64},{128,160},{160,128},{192,224},{224,1... | collective-permute-start | bytes 1179656 | tf_op jit(solution)/shard_map/ppermute | solution.py:39
  74.1 0.1 collective-permute-start.13
  74.2 0.6 back_keep.1
  74.8 0.8 collective-permute-done.13
  75.7 2.3 %collective-permute-start.15 = (bf16[256,256]{1,0:T(8,128)(2,1)S(1)}, bf16[256,256]{1,0:T(8,128)(2,1)S(1)}, u32[]{:S(2)}, u32[]{:S(2)}) collective-permute-start(bf16[256,256]{1,0:T(8,128)(2,1)S(1)} %add_convert_fusion.2), channel_id=1, source_target_pairs={{0,128},{32,160},{64,192},{96,224},{128,0},{160,32},{192,64},{224,... | collective-permute-start | bytes 393224 | tf_op jit(solution)/shard_map/ppermute | solution.py:39
  78.0 0.1 add_convert_fusion
  78.1 1.4 %collective-permute-start.17 = (bf16[256,256]{1,0:T(8,128)(2,1)S(1)}, bf16[256,256]{1,0:T(8,128)(2,1)S(1)}, u32[]{:S(2)}, u32[]{:S(2)}) collective-permute-start(bf16[256,256]{1,0:T(8,128)(2,1)S(1)} %get-tuple-element.59), channel_id=1, source_target_pairs={{0,192},{32,224},{64,0},{96,32},{128,64},{160,96},{192,128},{224,1... | collective-permute-start | bytes 393224 | tf_op jit(solution)/shard_map/ppermute | solution.py:39
  79.5 0.2 collective-permute-start.16
  79.6 1.9 %decoder_gradient.1 = (bf16[576,2048]{1,0:T(8,128)(2,1)}, f32[1,576]{1,0:T(1,128)S(1)}) custom-call(bf16[256,640]{1,0:T(8,128)(2,1)S(1)} %bitcast.19, bf16[272,256]{1,0:T(8,128)(2,1)S(1)} %get-tuple-element.53.refs_0_.feat_ref, bf16[272,256]{1,0:T(8,128)(2,1)S(1)} %collective-permute-done.8.refs_1_, bf16[272,256]{1,0:T(8,128)(2,1)S(1)} %collective-permute-done.9.refs_2_, ...), custom_call_target="tpu_custom_call" | custom-call | flops 603979776 | bytes 5767168 | tf_op jit(solution)/shard_map/decoder_gradient/pallas_call | solution.py:51
  81.6 0.6 reduce
  82.2 2.3 %collective-permute-done.17.three_ref = bf16[256,256]{1,0:T(8,128)(2,1)S(1)} collective-permute-done((bf16[256,256]{1,0:T(8,128)(2,1)S(1)}, bf16[256,256]{1,0:T(8,128)(2,1)S(1)}, u32[]{:S(2)}, u32[]{:S(2)}) %collective-permute-start.17) | collective-permute-done | bytes 131104 | tf_op jit(solution)/shard_map/ppermute | solution.py:39
  84.5 0.5 collective-permute-done.16.two_ref
  85.0 0.3 own_gradient.1.refs_0_
  85.2 2.8 %collective-permute-start.23 = (bf16[272,256]{1,0:T(8,128)(2,1)S(1)}, bf16[272,256]{1,0:T(8,128)(2,1)S(1)}, u32[]{:S(2)}, u32[]{:S(2)}) collective-permute-start(bf16[272,256]{1,0:T(8,128)(2,1)S(1)} %own_gradient.1.refs_0_), channel_id=1, source_target_pairs={{0,128},{32,160},{64,192},{96,224},{128,0},{160,32},{192,64},{224,... | collective-permute-start | bytes 417800 | tf_op jit(solution)/shard_map/ppermute | solution.py:39
  88.1 0.3 collective-permute-start.21
  88.4 2.4 %collective-permute-start.19 = (bf16[272,256]{1,0:T(8,128)(2,1)S(1)}, bf16[272,256]{1,0:T(8,128)(2,1)S(1)}, u32[]{:S(2)}, u32[]{:S(2)}) collective-permute-start(bf16[272,256]{1,0:T(8,128)(2,1)S(1)} %own_gradient.1.refs_0_), channel_id=1, source_target_pairs={{0,192},{32,224},{64,0},{96,32},{128,64},{160,96},{192,128},{224,1... | collective-permute-start | bytes 417800 | tf_op jit(solution)/shard_map/ppermute | solution.py:39
  90.8 1.4 %collective-permute-start.18 = (bf16[272,256]{1,0:T(8,128)(2,1)S(1)}, bf16[272,256]{1,0:T(8,128)(2,1)S(1)}, u32[]{:S(2)}, u32[]{:S(2)}) collective-permute-start(bf16[272,256]{1,0:T(8,128)(2,1)S(1)} %own_gradient.1.refs_0_), channel_id=1, source_target_pairs={{0,32},{32,0},{64,96},{96,64},{128,160},{160,128},{192,224},{224,1... | collective-permute-start | bytes 417800 | tf_op jit(solution)/shard_map/ppermute | solution.py:39
  92.1 2.9 %collective-permute-start.24 = (bf16[272,256]{1,0:T(8,128)(2,1)S(1)}, bf16[272,256]{1,0:T(8,128)(2,1)S(1)}, u32[]{:S(2)}, u32[]{:S(2)}) collective-permute-start(bf16[272,256]{1,0:T(8,128)(2,1)S(1)} %collective-permute-done.23.refs_6_), channel_id=1, source_target_pairs={{0,32},{32,0},{64,96},{96,64},{128,160},{160,128},{192,224},{224,1... | collective-permute-start | bytes 417800 | tf_op jit(solution)/shard_map/ppermute | solution.py:39
  95.0 0.6 collective-permute-done.21.refs_4_
  95.6 1.1 %collective-permute-start.22 = (bf16[272,256]{1,0:T(8,128)(2,1)S(1)}, bf16[272,256]{1,0:T(8,128)(2,1)S(1)}, u32[]{:S(2)}, u32[]{:S(2)}) collective-permute-start(bf16[272,256]{1,0:T(8,128)(2,1)S(1)} %collective-permute-done.21.refs_4_), channel_id=1, source_target_pairs={{0,32},{32,0},{64,96},{96,64},{128,160},{160,128},{192,224},{224,1... | collective-permute-start | bytes 417800 | tf_op jit(solution)/shard_map/ppermute | solution.py:39
  96.7 0.0 collective-permute-start.20
  96.7 1.0 collective-permute-done.22.refs_5_
  97.7 0.4 collective-permute-done.20.refs_3_
  98.1 1.8 %encoder_gradient.1 = (bf16[576,2048]{1,0:T(8,128)(2,1)}, f32[1,2048]{1,0:T(1,128)}, f32[1,128]{1,0:T(1,128)}) custom-call(bf16[576,256]{1,0:T(8,128)(2,1)S(1)} %bitcast.24, bf16[272,256]{1,0:T(8,128)(2,1)S(1)} %own_gradient.1.refs_0_, bf16[272,256]{1,0:T(8,128)(2,1)S(1)} %collective-permute-done.18.refs_1_, ...), custom_call_target="tpu_custom_call" | custom-call | flops 603979776 | bytes 3407872 | tf_op jit(solution)/shard_map/encoder_gradient/pallas_call | solution.py:51
  (18 shorter events, 0.1 us)
Async XLA Ops:
  0.6 5.4 %copy-start = (bf16[2048,576]{0,1:T(8,128)(2,1)S(1)}, bf16[2048,576]{0,1:T(8,128)(2,1)}, u32[]{:S(2)}) copy-start(bf16[2048,576]{0,1:T(8,128)(2,1)} %param.8) | copy-start | bytes 7077892
  2.7 4.9 %collective-permute-start = (f32[256,256]{1,0:T(8,128)S(1)}, f32[256,256]{1,0:T(8,128)S(1)}, u32[]{:S(2)}, u32[]{:S(2)}) collective-permute-start(f32[256,256]{1,0:T(8,128)S(1)} %get-tuple-element.34), channel_id=1, source_target_pairs={{0,32},{32,0},{64,96},{96,64},{128,160},{160,128},{192,224},{224,1... | collective-permute-start | bytes 786440 | tf_op jit(solution)/shard_map/ppermute | solution.py:39
  6.2 1.4 %collective-permute-start.1 = (f32[8,2048]{1,0:T(8,128)S(1)}, f32[8,2048]{1,0:T(8,128)S(1)}, u32[]{:S(2)}, u32[]{:S(2)}) collective-permute-start(f32[8,2048]{1,0:T(8,128)S(1)} %square_sums.1.square_ref.refs_3_), channel_id=1, source_target_pairs={{0,32},{32,0},{64,96},{96,64},{128,160},{160,128},{192,224},{224,1... | collective-permute-start | bytes 196616 | tf_op jit(solution)/shard_map/ppermute | solution.py:39
  7.6 10.5 %copy-start.2 = (f32[2048]{0:T(1024)S(1)}, f32[2048]{0:T(1024)}, u32[]{:S(2)}) copy-start(f32[2048]{0:T(1024)} %param.7) | copy-start | bytes 24580
  7.8 2.4 %collective-permute-start.2 = (f32[768,256]{1,0:T(8,128)S(1)}, f32[768,256]{1,0:T(8,128)S(1)}, u32[]{:S(2)}, u32[]{:S(2)}) collective-permute-start(f32[768,256]{1,0:T(8,128)S(1)} %preact_send.1), channel_id=1, source_target_pairs={{0,32},{32,0},{64,96},{96,64},{128,160},{160,128},{192,224},{224,1... | collective-permute-start | bytes 2359304 | tf_op jit(solution)/shard_map/ppermute | solution.py:39
  8.1 6.5 %collective-permute-start.3 = (bf16[272,256]{1,0:T(8,128)(2,1)S(1)}, bf16[272,256]{1,0:T(8,128)(2,1)S(1)}, u32[]{:S(2)}, u32[]{:S(2)}) collective-permute-start(bf16[272,256]{1,0:T(8,128)(2,1)S(1)} %encode_sums.3), channel_id=1, source_target_pairs={{0,128},{32,160},{64,192},{96,224},{128,0},{160,32},{192,64},{224,... | collective-permute-start | bytes 417800 | tf_op jit(solution)/shard_map/ppermute | solution.py:39
  10.4 18.9 %copy-start.3 = (f32[576]{0:T(1024)S(1)}, f32[576]{0:T(1024)}, u32[]{:S(2)}) copy-start(f32[576]{0:T(1024)} %param.9) | copy-start | bytes 6916
  10.4 18.9 %copy-start.1 = (bf16[256,576]{0,1:T(8,128)(2,1)S(1)}, bf16[256,576]{0,1:T(8,128)(2,1)}, u32[]{:S(2)}) copy-start(bf16[256,576]{0,1:T(8,128)(2,1)} %param.5) | copy-start | bytes 884740
  10.4 7.6 %collective-permute-start.4 = (bf16[272,256]{1,0:T(8,128)(2,1)S(1)}, bf16[272,256]{1,0:T(8,128)(2,1)S(1)}, u32[]{:S(2)}, u32[]{:S(2)}) collective-permute-start(bf16[272,256]{1,0:T(8,128)(2,1)S(1)} %encode_sums.4), channel_id=1, source_target_pairs={{0,64},{32,96},{64,128},{96,160},{128,192},{160,224},{192,0},{224,... | collective-permute-start | bytes 417800 | tf_op jit(solution)/shard_map/ppermute | solution.py:39
  10.8 7.3 %collective-permute-start.5 = (bf16[272,256]{1,0:T(8,128)(2,1)S(1)}, bf16[272,256]{1,0:T(8,128)(2,1)S(1)}, u32[]{:S(2)}, u32[]{:S(2)}) collective-permute-start(bf16[272,256]{1,0:T(8,128)(2,1)S(1)} %encode_sums.5), channel_id=1, source_target_pairs={{0,192},{32,224},{64,0},{96,32},{128,64},{160,96},{192,128},{224,1... | collective-permute-start | bytes 417800 | tf_op jit(solution)/shard_map/ppermute | solution.py:39
  18.7 6.2 %collective-permute-start.11 = (bf16[272,256]{1,0:T(8,128)(2,1)S(1)}, bf16[272,256]{1,0:T(8,128)(2,1)S(1)}, u32[]{:S(2)}, u32[]{:S(2)}) collective-permute-start(bf16[272,256]{1,0:T(8,128)(2,1)S(1)} %get-tuple-element.53.refs_0_.feat_ref), channel_id=1, source_target_pairs={{0,128},{32,160},{64,192},{96,224},{128,0},{160,32},{192,64},{224,... | collective-permute-start | bytes 417800 | tf_op jit(solution)/shard_map/ppermute | solution.py:39
  19.9 7.5 %collective-permute-start.9 = (bf16[272,256]{1,0:T(8,128)(2,1)S(1)}, bf16[272,256]{1,0:T(8,128)(2,1)S(1)}, u32[]{:S(2)}, u32[]{:S(2)}) collective-permute-start(bf16[272,256]{1,0:T(8,128)(2,1)S(1)} %get-tuple-element.53.refs_0_.feat_ref), channel_id=1, source_target_pairs={{0,192},{32,224},{64,0},{96,32},{128,64},{160,96},{192,128},{224,1... | collective-permute-start | bytes 417800 | tf_op jit(solution)/shard_map/ppermute | solution.py:39
  20.2 8.1 %collective-permute-start.6 = (bf16[272,256]{1,0:T(8,128)(2,1)S(1)}, bf16[272,256]{1,0:T(8,128)(2,1)S(1)}, u32[]{:S(2)}, u32[]{:S(2)}) collective-permute-start(bf16[272,256]{1,0:T(8,128)(2,1)S(1)} %get-tuple-element.53.refs_0_.feat_ref), channel_id=1, source_target_pairs={{0,64},{32,96},{64,128},{96,160},{128,192},{160,224},{192,0},{224,... | collective-permute-start | bytes 417800 | tf_op jit(solution)/shard_map/ppermute | solution.py:39
  21.4 8.1 %collective-permute-start.8 = (bf16[272,256]{1,0:T(8,128)(2,1)S(1)}, bf16[272,256]{1,0:T(8,128)(2,1)S(1)}, u32[]{:S(2)}, u32[]{:S(2)}) collective-permute-start(bf16[272,256]{1,0:T(8,128)(2,1)S(1)} %get-tuple-element.53.refs_0_.feat_ref), channel_id=1, source_target_pairs={{0,32},{32,0},{64,96},{96,64},{128,160},{160,128},{192,224},{224,1... | collective-permute-start | bytes 417800 | tf_op jit(solution)/shard_map/ppermute | solution.py:39
  24.8 4.7 %collective-permute-start.12 = (bf16[272,256]{1,0:T(8,128)(2,1)S(1)}, bf16[272,256]{1,0:T(8,128)(2,1)S(1)}, u32[]{:S(2)}, u32[]{:S(2)}) collective-permute-start(bf16[272,256]{1,0:T(8,128)(2,1)S(1)} %collective-permute-done.11.refs_4_), channel_id=1, source_target_pairs={{0,32},{32,0},{64,96},{96,64},{128,160},{160,128},{192,224},{224,1... | collective-permute-start | bytes 417800 | tf_op jit(solution)/shard_map/ppermute | solution.py:39
  27.5 2.1 %collective-permute-start.10 = (bf16[272,256]{1,0:T(8,128)(2,1)S(1)}, bf16[272,256]{1,0:T(8,128)(2,1)S(1)}, u32[]{:S(2)}, u32[]{:S(2)}) collective-permute-start(bf16[272,256]{1,0:T(8,128)(2,1)S(1)} %collective-permute-done.9.refs_2_), channel_id=1, source_target_pairs={{0,32},{32,0},{64,96},{96,64},{128,160},{160,128},{192,224},{224,1... | collective-permute-start | bytes 417800 | tf_op jit(solution)/shard_map/ppermute | solution.py:39
  28.3 2.0 %collective-permute-start.7 = (bf16[272,256]{1,0:T(8,128)(2,1)S(1)}, bf16[272,256]{1,0:T(8,128)(2,1)S(1)}, u32[]{:S(2)}, u32[]{:S(2)}) collective-permute-start(bf16[272,256]{1,0:T(8,128)(2,1)S(1)} %collective-permute-done.6.refs_0_.refs_6_), channel_id=1, source_target_pairs={{0,32},{32,0},{64,96},{96,64},{128,160},{160,128},{192,224},{224,1... | collective-permute-start | bytes 417800 | tf_op jit(solution)/shard_map/ppermute | solution.py:39
  70.4 7.6 %collective-permute-start.14 = (bf16[768,256]{1,0:T(8,128)(2,1)S(1)}, bf16[768,256]{1,0:T(8,128)(2,1)S(1)}, u32[]{:S(2)}, u32[]{:S(2)}) collective-permute-start(bf16[768,256]{1,0:T(8,128)(2,1)S(1)} %back_send.1), channel_id=1, source_target_pairs={{0,32},{32,0},{64,96},{96,64},{128,160},{160,128},{192,224},{224,1... | collective-permute-start | bytes 1179656 | tf_op jit(solution)/shard_map/ppermute | solution.py:39
  74.1 1.5 %collective-permute-start.13 = (bf16[256,256]{1,0:T(8,128)(2,1)S(1)}, bf16[256,256]{1,0:T(8,128)(2,1)S(1)}, u32[]{:S(2)}, u32[]{:S(2)}) collective-permute-start(bf16[256,256]{1,0:T(8,128)(2,1)S(1)} %back_far.1), channel_id=1, source_target_pairs={{0,32},{32,0},{64,96},{96,64},{128,160},{160,128},{192,224},{224,1... | collective-permute-start | bytes 393224 | tf_op jit(solution)/shard_map/ppermute | solution.py:39
  75.7 6.5 %collective-permute-start.15 = (bf16[256,256]{1,0:T(8,128)(2,1)S(1)}, bf16[256,256]{1,0:T(8,128)(2,1)S(1)}, u32[]{:S(2)}, u32[]{:S(2)}) collective-permute-start(bf16[256,256]{1,0:T(8,128)(2,1)S(1)} %add_convert_fusion.2), channel_id=1, source_target_pairs={{0,128},{32,160},{64,192},{96,224},{128,0},{160,32},{192,64},{224,... | collective-permute-start | bytes 393224 | tf_op jit(solution)/shard_map/ppermute | solution.py:39
  78.1 6.4 %collective-permute-start.17 = (bf16[256,256]{1,0:T(8,128)(2,1)S(1)}, bf16[256,256]{1,0:T(8,128)(2,1)S(1)}, u32[]{:S(2)}, u32[]{:S(2)}) collective-permute-start(bf16[256,256]{1,0:T(8,128)(2,1)S(1)} %get-tuple-element.59), channel_id=1, source_target_pairs={{0,192},{32,224},{64,0},{96,32},{128,64},{160,96},{192,128},{224,1... | collective-permute-start | bytes 393224 | tf_op jit(solution)/shard_map/ppermute | solution.py:39
  79.5 5.5 %collective-permute-start.16 = (bf16[256,256]{1,0:T(8,128)(2,1)S(1)}, bf16[256,256]{1,0:T(8,128)(2,1)S(1)}, u32[]{:S(2)}, u32[]{:S(2)}) collective-permute-start(bf16[256,256]{1,0:T(8,128)(2,1)S(1)} %get-tuple-element.60), channel_id=1, source_target_pairs={{0,64},{32,96},{64,128},{96,160},{128,192},{160,224},{192,0},{224,... | collective-permute-start | bytes 393224 | tf_op jit(solution)/shard_map/ppermute | solution.py:39
  85.2 6.9 %collective-permute-start.23 = (bf16[272,256]{1,0:T(8,128)(2,1)S(1)}, bf16[272,256]{1,0:T(8,128)(2,1)S(1)}, u32[]{:S(2)}, u32[]{:S(2)}) collective-permute-start(bf16[272,256]{1,0:T(8,128)(2,1)S(1)} %own_gradient.1.refs_0_), channel_id=1, source_target_pairs={{0,128},{32,160},{64,192},{96,224},{128,0},{160,32},{192,64},{224,... | collective-permute-start | bytes 417800 | tf_op jit(solution)/shard_map/ppermute | solution.py:39
  88.1 7.6 %collective-permute-start.21 = (bf16[272,256]{1,0:T(8,128)(2,1)S(1)}, bf16[272,256]{1,0:T(8,128)(2,1)S(1)}, u32[]{:S(2)}, u32[]{:S(2)}) collective-permute-start(bf16[272,256]{1,0:T(8,128)(2,1)S(1)} %own_gradient.1.refs_0_), channel_id=1, source_target_pairs={{0,64},{32,96},{64,128},{96,160},{128,192},{160,224},{192,0},{224,... | collective-permute-start | bytes 417800 | tf_op jit(solution)/shard_map/ppermute | solution.py:39
  88.4 8.3 %collective-permute-start.19 = (bf16[272,256]{1,0:T(8,128)(2,1)S(1)}, bf16[272,256]{1,0:T(8,128)(2,1)S(1)}, u32[]{:S(2)}, u32[]{:S(2)}) collective-permute-start(bf16[272,256]{1,0:T(8,128)(2,1)S(1)} %own_gradient.1.refs_0_), channel_id=1, source_target_pairs={{0,192},{32,224},{64,0},{96,32},{128,64},{160,96},{192,128},{224,1... | collective-permute-start | bytes 417800 | tf_op jit(solution)/shard_map/ppermute | solution.py:39
  90.8 5.9 %collective-permute-start.18 = (bf16[272,256]{1,0:T(8,128)(2,1)S(1)}, bf16[272,256]{1,0:T(8,128)(2,1)S(1)}, u32[]{:S(2)}, u32[]{:S(2)}) collective-permute-start(bf16[272,256]{1,0:T(8,128)(2,1)S(1)} %own_gradient.1.refs_0_), channel_id=1, source_target_pairs={{0,32},{32,0},{64,96},{96,64},{128,160},{160,128},{192,224},{224,1... | collective-permute-start | bytes 417800 | tf_op jit(solution)/shard_map/ppermute | solution.py:39
  92.1 4.6 %collective-permute-start.24 = (bf16[272,256]{1,0:T(8,128)(2,1)S(1)}, bf16[272,256]{1,0:T(8,128)(2,1)S(1)}, u32[]{:S(2)}, u32[]{:S(2)}) collective-permute-start(bf16[272,256]{1,0:T(8,128)(2,1)S(1)} %collective-permute-done.23.refs_6_), channel_id=1, source_target_pairs={{0,32},{32,0},{64,96},{96,64},{128,160},{160,128},{192,224},{224,1... | collective-permute-start | bytes 417800 | tf_op jit(solution)/shard_map/ppermute | solution.py:39
  95.6 2.1 %collective-permute-start.22 = (bf16[272,256]{1,0:T(8,128)(2,1)S(1)}, bf16[272,256]{1,0:T(8,128)(2,1)S(1)}, u32[]{:S(2)}, u32[]{:S(2)}) collective-permute-start(bf16[272,256]{1,0:T(8,128)(2,1)S(1)} %collective-permute-done.21.refs_4_), channel_id=1, source_target_pairs={{0,32},{32,0},{64,96},{96,64},{128,160},{160,128},{192,224},{224,1... | collective-permute-start | bytes 417800 | tf_op jit(solution)/shard_map/ppermute | solution.py:39
  96.7 1.4 %collective-permute-start.20 = (bf16[272,256]{1,0:T(8,128)(2,1)S(1)}, bf16[272,256]{1,0:T(8,128)(2,1)S(1)}, u32[]{:S(2)}, u32[]{:S(2)}) collective-permute-start(bf16[272,256]{1,0:T(8,128)(2,1)S(1)} %collective-permute-done.19.refs_2_), channel_id=1, source_target_pairs={{0,32},{32,0},{64,96},{96,64},{128,160},{160,128},{192,224},{224,1... | collective-permute-start | bytes 417800 | tf_op jit(solution)/shard_map/ppermute | solution.py:39
